TPU v7x, 32 devices: a whole 2x2x4 slice. The times are simulated.
32 devices in a mesh: chan: 2 (over x), tm: 16 (over z, y, core).
Axes of the slice: x: 2, y: 2, z: 4, core: 2. Of those that a mesh axis runs over, the one named last changes fastest.
Arguments:
- frames_in: bfloat16 [65536, 128], P(('tm', 'chan')), may hold values from -6 to 6
- item_lengths: int32 [16], replicated, may hold values from 1 to 8192, 65536 in all
- out_cotangent: bfloat16 [65536, 128], P(('tm', 'chan')), may hold values from -6 to 6
- skip_cotangent: bfloat16 [65536, 128], P(('tm', 'chan')), may hold values from -6 to 6
- expand: float32 [128, 512], P(None, 'chan'), may hold values from -0.5 to 0.5
- expand_moment: float32 [128, 512], P(None, 'chan'), may hold values from -0.0078125 to 0.0078125
- expand_square: float32 [128, 512], P(None, 'chan'), may hold values from 6.2042744e-08 to 9.926839e-07
- depthwise: float32 [3, 512], P(None, 'chan'), may hold values from -3.5 to 3.5
- depth_moment: float32 [3, 512], P(None, 'chan'), may hold values from -0.0078125 to 0.0078125
- depth_square: float32 [3, 512], P(None, 'chan'), may hold values from 6.2042744e-08 to 9.926839e-07
- project: float32 [2, 512, 128], P(None, 'chan'), may hold values from -0.17872982 to 0.17872982
- project_moment: float32 [2, 512, 128], P(None, 'chan'), may hold values from -0.0078125 to 0.0078125
- project_square: float32 [2, 512, 128], P(None, 'chan'), may hold values from 6.2042744e-08 to 9.926839e-07
- channel_vectors: float32 [6, 512], P(None, 'chan'), may hold values from 0.5 to 1.5
- vector_moment: float32 [6, 512], P(None, 'chan'), may hold values from -0.0078125 to 0.0078125
- vector_square: float32 [6, 512], P(None, 'chan'), may hold values from 6.2042744e-08 to 9.926839e-07
- output_biases: float32 [2, 128], replicated, may hold values from -3 to 3
- bias_moment: float32 [2, 128], replicated, may hold values from -0.0078125 to 0.0078125
- bias_square: float32 [2, 128], replicated, may hold values from 6.2042744e-08 to 9.926839e-07
- prelu_slopes: float32 [2], replicated, may hold values from 0.1 to 0.4
- slope_moment: float32 [2], replicated, may hold values from -0.15625 to 0.15625
- slope_square: float32 [2], replicated, may hold values from 2.4817098e-05 to 0.00039707357
Outputs:
- block_out: bfloat16 [65536, 128], P(('tm', 'chan'))
- skip_out: bfloat16 [65536, 128], P(('tm', 'chan'))
- input_grad: float32 [65536, 128], P(('tm', 'chan'))
- grad_norm: float32 [], replicated
- expand_new: float32 [128, 512], P(None, 'chan')
- expand_moment_new: float32 [128, 512], P(None, 'chan')
- expand_square_new: float32 [128, 512], P(None, 'chan')
- depthwise_new: float32 [3, 512], P(None, 'chan')
- depth_moment_new: float32 [3, 512], P(None, 'chan')
- depth_square_new: float32 [3, 512], P(None, 'chan')
- project_new: float32 [2, 512, 128], P(None, 'chan')
- project_moment_new: float32 [2, 512, 128], P(None, 'chan')
- project_square_new: float32 [2, 512, 128], P(None, 'chan')
- vectors_new: float32 [6, 512], P(None, 'chan')
- vector_moment_new: float32 [6, 512], P(None, 'chan')
- vector_square_new: float32 [6, 512], P(None, 'chan')
- biases_new: float32 [2, 128], replicated
- bias_moment_new: float32 [2, 128], replicated
- bias_square_new: float32 [2, 128], replicated
- slopes_new: float32 [2], replicated
- slope_moment_new: float32 [2], replicated
- slope_square_new: float32 [2], replicated
Inputs may be any that keep to these rules, and one draw needn't show every extreme that they name: `item_lengths`: frame counts of the 16 items laid end to end; they sum to 65536, and the largest is exactly 8192.
All inputs are finite; a program needn't handle non-finite values.
Results may differ from a plain program's by a relative error of at most 0.005.
The roundings to bfloat16 on the way count: a program that leaves them out, or rounds other values in their place, can miss the bound.
Values may be sent and summed in bfloat16 or wider, within the bound.
A program may use at most 64 MiB of HBM per device.

v0:
```python
import jax
import jax.numpy as jnp
from jax import lax
from jax.sharding import PartitionSpec as P

H = 512
DILATION_STEP = 16


norm_eps = 1e-06
clip_level = 5.0
rate = 0.05
small_rate = 0.5
beta_first = 0.9
beta_second = 0.999
adam_eps = 1e-08
decay = 0.01
step_count = 10.0


def padded(block, sides, width):
    for axis, dim in sides:
        count = lax.axis_size(axis)
        forward = [(i, i + 1) for i in range(count - 1)]
        backward = [(target, source) for source, target in forward]
        low = lax.ppermute(
            lax.slice_in_dim(block, block.shape[dim] - width, None, axis=dim), axis, forward
        )
        high = lax.ppermute(lax.slice_in_dim(block, 0, width, axis=dim), axis, backward)
        block = jnp.concatenate([low, block, high], axis=dim)
    return block


def contract(left_side, right_side, left_dim, right_dim):
    return lax.dot_general(
        left_side,
        right_side,
        (((left_dim,), (right_dim,)), ((), ())),
        preferred_element_type=jnp.float32,
    )


def element_sums(value_entries, indicator_matrix):
    return jnp.sum(indicator_matrix * value_entries[:, None], axis=0)


def to_rows(value_entries, indicator_matrix):
    return jnp.sum(indicator_matrix * value_entries[None, :], axis=1)


def prelu(value_entries, slope_value):
    return jnp.where(value_entries > 0, value_entries, slope_value * value_entries)


def tap_valid_mask(widened_positions, inside_window, start_position, length, offset):
    here_ids = widened_positions[start_position : start_position + length]
    there_ids = widened_positions[start_position + offset : start_position + offset + length]
    return (
        inside_window[start_position : start_position + length]
        & inside_window[start_position + offset : start_position + offset + length]
        & (here_ids == there_ids)
    )


def frame_setup(item_lengths, leading_frame, frame_series, whole_frames):
    starts = jnp.cumsum(item_lengths) - item_lengths
    frame_positions = (
        leading_frame
        - 2 * DILATION_STEP
        + jnp.arange(frame_series + 4 * DILATION_STEP, dtype=jnp.int32)
    )
    widened_positions = (
        jnp.sum((frame_positions[:, None] >= starts[None, :]).astype(jnp.int32), axis=1) - 1
    )
    inside_window = (frame_positions >= 0) & (frame_positions < whole_frames)
    local_positions = widened_positions[2 * DILATION_STEP : 2 * DILATION_STEP + frame_series]
    item_count = item_lengths.shape[0]
    indicator_matrix = (
        local_positions[:, None] == jnp.arange(item_count, dtype=jnp.int32)[None, :]
    ).astype(jnp.float32)
    element_count = item_lengths.astype(jnp.float32) * H
    here_valid = [
        tap_valid_mask(
            widened_positions,
            inside_window,
            2 * DILATION_STEP,
            frame_series,
            (tap_position_index - 1) * DILATION_STEP,
        )
        for tap_position_index in range(3)
    ]
    wide_valid = [
        tap_valid_mask(
            widened_positions,
            inside_window,
            DILATION_STEP,
            frame_series + 2 * DILATION_STEP,
            (tap_position_index - 1) * DILATION_STEP,
        )
        for tap_position_index in range(3)
    ]
    return (indicator_matrix, element_count, here_valid, wide_valid, frame_series)


def global_norm_forward(active, gain_vector_row, shift_vector_row, indicator_matrix, element_count):
    first_sum = lax.psum(element_sums(jnp.sum(active, axis=1), indicator_matrix), ("chan", "tm"))
    item_mean = first_sum / element_count
    mean_removed = active - to_rows(item_mean, indicator_matrix)[:, None]
    item_spread = (
        lax.psum(
            element_sums(jnp.sum(mean_removed * mean_removed, axis=1), indicator_matrix),
            ("chan", "tm"),
        )
        / element_count
    )
    per_row_scale = to_rows(lax.rsqrt(item_spread + norm_eps), indicator_matrix)
    standardized_input = mean_removed * per_row_scale[:, None]
    return (
        gain_vector_row * standardized_input + shift_vector_row,
        standardized_input,
        per_row_scale,
    )


def global_norm_backward(
    incoming_gradient,
    standardized_input,
    per_row_scale,
    gain_vector_row,
    indicator_matrix,
    element_count,
):
    gain_gradient = jnp.sum(incoming_gradient * standardized_input, axis=0)
    shift_grad = jnp.sum(incoming_gradient, axis=0)
    scaled_values = gain_vector_row * incoming_gradient
    first_sum, second_sum = lax.psum(
        (
            element_sums(jnp.sum(scaled_values, axis=1), indicator_matrix),
            element_sums(jnp.sum(scaled_values * standardized_input, axis=1), indicator_matrix),
        ),
        ("chan", "tm"),
    )
    opening_rows = to_rows(first_sum / element_count, indicator_matrix)
    following_rows = to_rows(second_sum / element_count, indicator_matrix)
    activated_gradient = (
        scaled_values - opening_rows[:, None] - standardized_input * following_rows[:, None]
    ) * per_row_scale[:, None]
    return (activated_gradient, gain_gradient, shift_grad)


def forward_core(inputs, expand_low, depth_taps, parameter_vectors, slopes, local_setup, extend):
    indicator_matrix, element_count, here_valid, wide_valid, frame_series = local_setup
    hidden_state = (
        jnp.dot(inputs, expand_low, preferred_element_type=jnp.float32) + parameter_vectors[0]
    )
    normalized_values, standardized_first, first_scale = global_norm_forward(
        prelu(hidden_state, slopes[0]),
        parameter_vectors[1],
        parameter_vectors[2],
        indicator_matrix,
        element_count,
    )
    normed_low = normalized_values.astype(jnp.bfloat16)
    zero_padded = extend(normed_low)
    incoming_taps = [
        jnp.where(
            here_valid[tap_position_index][:, None],
            zero_padded[
                tap_position_index * DILATION_STEP : tap_position_index * DILATION_STEP
                + frame_series
            ].astype(jnp.float32),
            0.0,
        )
        for tap_position_index in range(3)
    ]
    depthwise_output = (
        parameter_vectors[3]
        + incoming_taps[0] * depth_taps[0]
        + incoming_taps[1] * depth_taps[1]
        + incoming_taps[2] * depth_taps[2]
    )
    normalized_second, standardized_second, second_scale = global_norm_forward(
        prelu(depthwise_output, slopes[1]),
        parameter_vectors[4],
        parameter_vectors[5],
        indicator_matrix,
        element_count,
    )
    mixed_reduced = normalized_second.astype(jnp.bfloat16)
    return (
        hidden_state,
        standardized_first,
        first_scale,
        incoming_taps,
        depthwise_output,
        standardized_second,
        second_scale,
        mixed_reduced,
    )


def backward_core(
    mixed_gradient, saved_residuals, depth_taps, parameter_vectors, slopes, local_setup, extend
):
    indicator_matrix, element_count, here_valid, wide_valid, frame_series = local_setup
    (
        hidden_state,
        standardized_first,
        first_scale,
        incoming_taps,
        depthwise_output,
        standardized_second,
        second_scale,
        mixed_reduced,
    ) = saved_residuals
    active_two, gain_two, shift_two = global_norm_backward(
        mixed_gradient,
        standardized_second,
        second_scale,
        parameter_vectors[4],
        indicator_matrix,
        element_count,
    )
    depth_grad = jnp.where(depthwise_output > 0, active_two, slopes[1] * active_two)
    slope_two = jnp.sum(jnp.where(depthwise_output > 0, 0.0, active_two * depthwise_output))
    depth_low = depth_grad.astype(jnp.bfloat16)
    depth_float = depth_low.astype(jnp.float32)
    taps_grad = jnp.stack(
        [
            jnp.sum(depth_float * incoming_taps[tap_position_index], axis=0)
            for tap_position_index in range(3)
        ]
    )
    depth_bias_grad = jnp.sum(depth_float, axis=0)
    beside_all = extend(depth_low).astype(jnp.float32)
    normalized_gradient = jnp.zeros(depth_float.shape, jnp.float32)
    for tap_position_index in range(3):
        start_position = (2 - tap_position_index) * DILATION_STEP
        window = jnp.where(
            wide_valid[tap_position_index][start_position : start_position + frame_series][:, None],
            beside_all[start_position : start_position + frame_series],
            0.0,
        )
        normalized_gradient = normalized_gradient + depth_taps[tap_position_index] * window
    active_one, gain_one, shift_one = global_norm_backward(
        normalized_gradient,
        standardized_first,
        first_scale,
        parameter_vectors[1],
        indicator_matrix,
        element_count,
    )
    hidden_grad = jnp.where(hidden_state > 0, active_one, slopes[0] * active_one)
    slope_one = jnp.sum(jnp.where(hidden_state > 0, 0.0, active_one * hidden_state))
    hidden_low = hidden_grad.astype(jnp.bfloat16)
    vectors_grad = jnp.stack(
        [
            jnp.sum(hidden_low.astype(jnp.float32), axis=0),
            gain_one,
            shift_one,
            depth_bias_grad,
            gain_two,
            shift_two,
        ]
    )
    slopes_grad = jnp.stack([slope_one, slope_two])
    return (hidden_low, taps_grad, vectors_grad, slopes_grad)


def halo_forward(value_entries):
    return padded(value_entries, (("tm", 0),), DILATION_STEP)


def halo_backward(value_entries):
    return padded(value_entries, (("tm", 0),), DILATION_STEP)


def by_channels(
    frames_in,
    item_lengths,
    out_cotangent,
    skip_cotangent,
    expand,
    depthwise,
    project,
    channel_vectors,
    output_biases,
    prelu_slopes,
):
    whole_in = lax.all_gather(frames_in, "chan", axis=0, tiled=True)
    frame_series = whole_in.shape[0]
    local_setup = frame_setup(
        item_lengths,
        lax.axis_index("tm") * frame_series,
        frame_series,
        lax.axis_size("tm") * frame_series,
    )
    expand_low = expand.astype(jnp.bfloat16)
    project_low = project.astype(jnp.bfloat16)
    saved_residuals = forward_core(
        whole_in, expand_low, depthwise, channel_vectors, prelu_slopes, local_setup, halo_forward
    )
    mixed_reduced = saved_residuals[7]
    residual_part, skip_part = (
        lax.psum_scatter(
            jnp.dot(mixed_reduced, project_low[0], preferred_element_type=jnp.float32),
            "chan",
            scatter_dimension=0,
            tiled=True,
        ),
        lax.psum_scatter(
            jnp.dot(mixed_reduced, project_low[1], preferred_element_type=jnp.float32),
            "chan",
            scatter_dimension=0,
            tiled=True,
        ),
    )
    block_out = (frames_in.astype(jnp.float32) + residual_part + output_biases[0]).astype(
        jnp.bfloat16
    )
    skip_out = (skip_part + output_biases[1]).astype(jnp.bfloat16)
    whole_out, whole_skip = (
        lax.all_gather(out_cotangent, "chan", axis=0, tiled=True),
        lax.all_gather(skip_cotangent, "chan", axis=0, tiled=True),
    )
    mixed_gradient = contract(whole_out, project_low[0], 1, 1) + contract(
        whole_skip, project_low[1], 1, 1
    )
    project_grad = jnp.stack(
        [contract(mixed_reduced, whole_out, 0, 0), contract(mixed_reduced, whole_skip, 0, 0)]
    )
    biases_grad = jnp.stack(
        [
            jnp.sum(whole_out.astype(jnp.float32), axis=0),
            jnp.sum(whole_skip.astype(jnp.float32), axis=0),
        ]
    )
    hidden_low, taps_grad, vectors_grad, slopes_grad = backward_core(
        mixed_gradient,
        saved_residuals,
        depthwise,
        channel_vectors,
        prelu_slopes,
        local_setup,
        halo_backward,
    )
    expand_grad = contract(whole_in, hidden_low, 0, 0)
    input_part = contract(hidden_low, expand_low, 1, 1)
    input_grad = out_cotangent.astype(jnp.float32) + lax.psum_scatter(
        input_part.astype(jnp.bfloat16), "chan", scatter_dimension=0, tiled=True
    ).astype(jnp.float32)
    summed = lax.psum(
        (expand_grad, taps_grad, project_grad, vectors_grad, biases_grad, slopes_grad), "tm"
    )
    local_squares = jnp.float32(0.0)
    for piece in summed[:4]:
        local_squares = local_squares + jnp.sum(piece * piece)
    total_squares, slopes_total = lax.psum((local_squares, summed[5]), "chan")
    grad_norm = jnp.sqrt(
        total_squares + jnp.sum(summed[4] * summed[4]) + jnp.sum(slopes_total * slopes_total)
    )
    grads = (summed[0], summed[1], summed[2], summed[3], summed[4], slopes_total)
    return (block_out, skip_out, input_grad, grad_norm, grads)


def adam(weight, moment, square, incoming_gradient, clip_scale, step_rate):
    clipped = incoming_gradient * clip_scale
    moment_next = beta_first * moment + (1.0 - beta_first) * clipped
    square_next = beta_second * square + (1.0 - beta_second) * clipped * clipped
    update = (
        moment_next
        / (1.0 - beta_first**step_count)
        / (jnp.sqrt(square_next / (1.0 - beta_second**step_count)) + adam_eps)
    )
    return (weight - step_rate * (update + decay * weight), moment_next, square_next)


def per_device(
    frames_in,
    item_lengths,
    out_cotangent,
    skip_cotangent,
    expand,
    expand_moment,
    expand_square,
    depthwise,
    depth_moment,
    depth_square,
    project,
    project_moment,
    project_square,
    channel_vectors,
    vector_moment,
    vector_square,
    output_biases,
    bias_moment,
    bias_square,
    prelu_slopes,
    slope_moment,
    slope_square,
):
    block_out, skip_out, input_grad, grad_norm, grads = by_channels(
        frames_in,
        item_lengths,
        out_cotangent,
        skip_cotangent,
        expand,
        depthwise,
        project,
        channel_vectors,
        output_biases,
        prelu_slopes,
    )
    clip_scale = jnp.minimum(1.0, clip_level / grad_norm)
    expand_set = adam(expand, expand_moment, expand_square, grads[0], clip_scale, rate)
    depth_set = adam(depthwise, depth_moment, depth_square, grads[1], clip_scale, small_rate)
    project_set = adam(project, project_moment, project_square, grads[2], clip_scale, rate)
    vector_set = adam(
        channel_vectors, vector_moment, vector_square, grads[3], clip_scale, small_rate
    )
    bias_set = adam(output_biases, bias_moment, bias_square, grads[4], clip_scale, small_rate)
    slope_set = adam(prelu_slopes, slope_moment, slope_square, grads[5], clip_scale, small_rate)
    return (
        block_out,
        skip_out,
        input_grad,
        grad_norm,
        expand_set[0],
        expand_set[1],
        expand_set[2],
        depth_set[0],
        depth_set[1],
        depth_set[2],
        project_set[0],
        project_set[1],
        project_set[2],
        vector_set[0],
        vector_set[1],
        vector_set[2],
        bias_set[0],
        bias_set[1],
        bias_set[2],
        slope_set[0],
        slope_set[1],
        slope_set[2],
    )


def solution(mesh):
    in_specs = (
        P(("tm", "chan"), None),
        P(),
        P(("tm", "chan"), None),
        P(("tm", "chan"), None),
        P(None, "chan"),
        P(None, "chan"),
        P(None, "chan"),
        P(None, "chan"),
        P(None, "chan"),
        P(None, "chan"),
        P(None, "chan", None),
        P(None, "chan", None),
        P(None, "chan", None),
        P(None, "chan"),
        P(None, "chan"),
        P(None, "chan"),
        P(),
        P(),
        P(),
        P(),
        P(),
        P(),
    )
    out_specs = (
        P(("tm", "chan"), None),
        P(("tm", "chan"), None),
        P(("tm", "chan"), None),
        P(),
        P(None, "chan"),
        P(None, "chan"),
        P(None, "chan"),
        P(None, "chan"),
        P(None, "chan"),
        P(None, "chan"),
        P(None, "chan", None),
        P(None, "chan", None),
        P(None, "chan", None),
        P(None, "chan"),
        P(None, "chan"),
        P(None, "chan"),
        P(),
        P(),
        P(),
        P(),
        P(),
        P(),
    )
    return jax.shard_map(
        per_device, mesh=mesh, in_specs=in_specs, out_specs=out_specs, check_vma=False
    )
```

profile of v0, /device:TPU:0, one launch (start us, length us, event | category | flops | bytes accessed | tf_op | source)
XLA Modules:
  0.0 559.2 jit_solution(2219006056744830506)
XLA Ops:
  7.2 0.7 all-gather.4.cloned.1.call-update
  8.0 0.7 all-gather.6.cloned.1.call-update
  9.5 0.7 copy.60
  11.3 1.5 fusion.45
  12.8 1.3 fusion.48
  14.2 19.4 %all-gather.4.cloned.1.call-done = bf16[4096,128]{1,0:T(8,128)(2,1)} async-done(((bf16[2048,128]{1,0:T(8,128)(2,1)}), bf16[4096,128]{1,0:T(8,128)(2,1)}) %all-gather.4.cloned.1.call-update) | async-done | bytes 1048592 | tf_op jit(solution)/shard_map/all_gather | solution.py:290
  33.7 4.7 fusion.10
  38.5 0.7 fusion.21
  39.2 39.8 %psum.112 = f32[16]{0:T(128)S(1)} all-reduce(f32[16]{0:T(128)S(1)} %select_reduce_fusion.17), channel_id=1, replica_groups=mesh['chan'=2,'tm'=16] {'chan','tm'}, use_global_device_ids=true, to_apply=%region_4.5 | all-reduce | flops 16 | bytes 128 | tf_op jit(solution)/shard_map/psum | solution.py:106
  79.1 3.6 multiply_reduce_fusion.5
  83.1 41.0 %psum.113 = f32[16]{0:T(128)S(1)} all-reduce(f32[16]{0:T(128)S(1)} %select_reduce_fusion.15), channel_id=1, replica_groups=mesh['chan'=2,'tm'=16] {'chan','tm'}, use_global_device_ids=true, to_apply=%region_8.9 | all-reduce | flops 16 | bytes 128 | tf_op jit(solution)/shard_map/psum | solution.py:110
  124.2 4.9 add_convert_fusion.1
  129.2 1.4 collective-permute-start
  130.6 1.3 collective-permute-start.1
  132.0 4.2 collective-permute-done.1
  136.2 8.8 %fusion.11 = (f32[4096]{0:T(1024)S(1)}, f32[4096,256]{1,0:T(8,128)}) fusion(f32[]{:T(128)} %bitcast.10, f32[256]{0:T(256)S(1)} %bitcast.66, bf16[16,256]{1,0:T(8,128)(2,1)S(1)} %collective-permute-done.1, bf16[4096,256]{1,0:T(8,128)(2,1)S(1)} %add_convert_fusion.1, pred[4096]{0:T(1024)(128)(4,1)S(1)} %get-tuple-element.161, f32[256]{0:T(256)S(1)} %bitcast.64, ...), kind=kLoop, calls=%fused_computation.59 | loop fusion | flops 23064576 | bytes 6340612 | tf_op jit(solution)/shard_map/reduce_sum | solution.py:106
  145.2 40.5 %psum.114 = f32[16]{0:T(128)S(1)} all-reduce(f32[16]{0:T(128)S(1)} %select_reduce_fusion.13), channel_id=1, replica_groups=mesh['chan'=2,'tm'=16] {'chan','tm'}, use_global_device_ids=true, to_apply=%region_12.13 | all-reduce | flops 16 | bytes 128 | tf_op jit(solution)/shard_map/psum | solution.py:106
  185.9 3.6 multiply_reduce_fusion.4
  189.7 3.9 fusion.14
  193.6 40.5 %psum.115 = f32[16]{0:T(128)S(1)} all-reduce(f32[16]{0:T(128)S(1)} %select_reduce_fusion.11), channel_id=1, replica_groups=mesh['chan'=2,'tm'=16] {'chan','tm'}, use_global_device_ids=true, to_apply=%region_16.17 | all-reduce | flops 16 | bytes 128 | tf_op jit(solution)/shard_map/psum | solution.py:110
  234.3 6.8 %multiply_reduce_fusion.7 = (f32[4096]{0:T(1024)S(1)}, f32[4096]{0:T(1024)S(1)}, f32[4096,256]{1,0:T(8,128)}) fusion(f32[256]{0:T(256)S(1)} %bitcast.60, f32[4096]{0:T(1024)S(1)} %select_reduce_fusion.10, f32[4096]{0:T(1024)S(1)} %select_reduce_fusion.12, f32[4096,256]{1,0:T(8,128)} %get-tuple-element.145, f32[]{:T(128)} %bitcast.10, ...), kind=kOutput, calls=%fused_computation.44 | convolution fusion | flops 278913024 | bytes 13763588 | tf_op jit(solution)/shard_map/dot_general | solution.py:35
  241.3 39.6 %all-reduce.1 = (f32[16]{0:T(128)S(1)}, f32[16]{0:T(128)S(1)}) all-reduce(f32[16]{0:T(128)S(1)} %get-tuple-element.108, f32[16]{0:T(128)S(1)} %get-tuple-element.109), channel_id=1, replica_groups=mesh['chan'=2,'tm'=16] {'chan','tm'}, use_global_device_ids=true, to_apply=%region_22.23 | all-reduce | flops 32 | bytes 256 | tf_op jit(solution)/shard_map/psum | solution.py:136
  281.1 14.4 %select_reduce_fusion = (f32[]{:T(128)}, f32[256]{0:T(256)}, f32[256]{0:T(256)}, f32[256]{0:T(256)}, f32[256]{0:T(256)}, /*index=5*/f32[256]{0:T(256)}, f32[256]...) fusion(f32[4096,256]{1,0:T(8,128)} %get-tuple-element.145, f32[4096]{0:T(1024)S(1)} %get-tuple-element.107, ...), kind=kLoop, calls=%fused_computation.24 | loop fusion | flops 44038656 | bytes 14782472 | tf_op jit(solution)/shard_map/reduce_sum | solution.py:225
  295.5 1.3 collective-permute-start.2
  296.8 1.3 collective-permute-start.3
  298.1 0.8 convolution_bitcast_fusion
  298.9 0.8 convolution_bitcast_fusion.1
  299.7 0.7 pad_maximum_fusion.2
  300.5 1.9 collective-permute-done.3
  302.8 8.0 %multiply_reduce_fusion.6 = (f32[4096]{0:T(1024)S(1)}, f32[4096]{0:T(1024)S(1)}, f32[4096,256]{1,0:T(8,128)}) fusion(f32[256]{0:T(256)S(1)} %bitcast.59, f32[4096]{0:T(1024)S(1)} %copy-done.13, f32[4096]{0:T(1024)S(1)} %copy-done.11, f32[4096,256]{1,0:T(8,128)S(1)} %copy-done, f32[]{:T(128)} %bitcast.5, f32[4128,256]{1,0:T(8,128)S(1)} %maximum_convert_fusion, ...), kind=kLoop, calls=%fused_computation.43 | loop fusion | flops 17817600 | bytes 21053444 | tf_op jit(solution)/shard_map/reduce_sum | solution.py:138
  310.7 0.7 select_reduce_fusion.5
  311.4 42.9 %all-reduce = (f32[16]{0:T(128)}, f32[16]{0:T(128)}) all-reduce(f32[16]{0:T(128)} %get-tuple-element.104, f32[16]{0:T(128)} %get-tuple-element.105), channel_id=1, replica_groups=mesh['chan'=2,'tm'=16] {'chan','tm'}, use_global_device_ids=true, to_apply=%region_30.31 | all-reduce | flops 32 | bytes 256 | tf_op jit(solution)/shard_map/psum | solution.py:136
  354.3 0.7 fusion.27
  355.2 9.6 %select_reduce_fusion.1 = (f32[]{:T(128)}, f32[256]{0:T(256)}, f32[256]{0:T(256)}, f32[256]{0:T(256)}, bf16[4096,256]{1,0:T(8,128)(2,1)S(1)}) fusion(f32[4096,256]{1,0:T(8,128)} %get-tuple-element.188, f32[4096]{0:T(1024)S(1)} %get-tuple-element.103, f32[4096]{0:T(1024)} %copy-done.12, f32[4096]{0:T(1024)} %copy-done.10, f32[]{:T(128)} %bitcast.5, ...), kind=kLoop, calls=%fused_computation.25 | loop fusion | flops 22019328 | bytes 10555400 | tf_op jit(solution)/shard_map/reduce_sum | solution.py:254
  364.9 1.3 copy-done.1
  366.2 1.4 convolution_bitcast_fusion.2
  367.7 3.3 convolution_convert_fusion
  371.0 2.0 fusion.16
  373.1 2.1 fusion.15
  375.2 1.1 copy.64
  376.3 1.7 copy.61
  378.0 1.7 copy.62
  379.7 1.3 slice_bitcast_fusion.6
  382.8 0.8 stack.73
  383.6 1.4 pad_maximum_fusion.5
  384.9 60.0 %all-reduce.2 = (f32[3,256]{1,0:T(4,128)S(1)}, f32[6,256]{1,0:T(8,128)S(1)}, f32[2,128]{1,0:T(2,128)S(1)}, f32[2]{0:T(128)S(1)}) all-reduce(f32[3,256]{1,0:T(4,128)S(1)} %pad_maximum_fusion.3, f32[6,256]{1,0:T(8,128)S(1)} %stack.73, f32[2,128]{1,0:T(2,128)S(1)} %pad_maximum_fusion.4, ...), channel_id=1, replica_groups=mesh['chan'=2,'tm'=16] {'tm'}, use_global_device_ids=true, to_apply=%region_42.43 | all-reduce | flops 2562 | bytes 20496 | tf_op jit(solution)/shard_map/psum | solution.py:352
  446.7 12.1 %all-reduce.7.cloned.1.call-done = (f32[128,256]{0,1:T(8,128)}, f32[2,256,128]{2,1,0:T(8,128)}) async-done(((f32[128,256]{0,1:T(8,128)}, f32[2,256,128]{2,1,0:T(8,128)}), (f32[128,256]{0,1:T(8,128)}, f32[2,256,128]{2,1,0:T(8,128)})) %all-reduce.7.cloned.1.call-update) | async-done | bytes 393232 | tf_op jit(solution)/shard_map/psum | solution.py:352
  458.8 1.5 multiply_reduce_fusion.9
  461.7 1.6 multiply_reduce_fusion.8
  464.6 5.4 all-reduce.4
  472.7 1.2 multiply_subtract_fusion.1
  473.9 0.8 copy.65
  474.6 0.8 copy.66
  475.4 0.8 copy.67
  476.1 1.2 multiply_subtract_fusion.5
  477.3 1.3 multiply_subtract_fusion.4
  478.6 1.3 multiply_subtract_fusion.3
  480.0 1.4 multiply_subtract_fusion.2
  481.3 2.1 multiply_subtract_fusion
  483.4 2.1 convert_add_fusion
  485.6 29.3 %reduce-scatter.6.cloned.1.call-done = f32[2048,128]{1,0:T(8,128)} async-done(((f32[4096,128]{1,0:T(8,128)}), f32[2048,128]{1,0:T(8,128)}) %reduce-scatter.6.cloned.1.call-update) | async-done | bytes 1048592 | tf_op jit(solution)/shard_map/reduce_scatter | solution.py:311
  514.9 2.1 add_convert_fusion.2
  517.0 32.1 %reduce-scatter.4.cloned.1.call-done = f32[2048,128]{1,0:T(8,128)} async-done(((f32[4096,128]{1,0:T(8,128)}), f32[2048,128]{1,0:T(8,128)}) %reduce-scatter.4.cloned.1.call-update) | async-done | bytes 1048592 | tf_op jit(solution)/shard_map/reduce_scatter | solution.py:305
  549.1 2.2 add_convert_fusion.3
  (138 shorter events, 8.8 us)
Async XLA Ops:
  7.2 26.5 %all-gather.4.cloned.1.call-start = ((), (), s32[]{:S(2)}) async-start(), calls=%async_computation.3 | async-start | bytes 1572864 | tf_op jit(solution)/shard_map/all_gather | solution.py:290
  7.9 71.0 %copy-start.34 = (s32[16]{0:T(128)S(1)}, s32[16]{0:T(128)}, u32[]{:S(2)}) copy-start(s32[16]{0:T(128)} %param.23) | copy-start | bytes 196
  7.9 181.8 %all-gather.6.cloned.1.call-start = ((), (), s32[]{:S(2)}) async-start(), calls=%async_computation.6 | async-start | bytes 1572864 | tf_op jit(solution)/shard_map/all_gather | solution.py:323
  8.7 225.6 %all-gather.8.cloned.1.call-start = ((), (), s32[]{:S(2)}) async-start(), calls=%async_computation.7 | async-start | bytes 1572864 | tf_op jit(solution)/shard_map/all_gather | solution.py:324
  9.4 449.4 %all-reduce.7.cloned.1.call-start = ((), (), s32[]{:S(2)}) async-start(), calls=%async_computation.9 | async-start | bytes 786432 | tf_op jit(solution)/shard_map/psum | solution.py:352
  12.8 111.4 %copy-start.24 = (f32[1,256]{1,0:T(1,128)}, f32[1,256]{1,0:T(1,128)S(1)}, u32[]{:S(2)}) copy-start(f32[1,256]{1,0:T(1,128)S(1)} %get-tuple-element.168) | copy-start | bytes 3076
  12.8 221.5 %copy-start.27 = (f32[1,256]{1,0:T(1,128)}, f32[1,256]{1,0:T(1,128)S(1)}, u32[]{:S(2)}) copy-start(f32[1,256]{1,0:T(1,128)S(1)} %get-tuple-element.165) | copy-start | bytes 3076
  79.1 50.0 %copy-start.10 = (f32[4096]{0:T(1024)}, f32[4096]{0:T(1024)S(1)}, u32[]{:S(2)}) copy-start(f32[4096]{0:T(1024)S(1)} %select_reduce_fusion.16) | copy-start | bytes 49156
  82.8 49.2 %copy-start.26 = (f32[3,256]{1,0:T(4,128)S(1)}, f32[3,256]{1,0:T(4,128)}, u32[]{:S(2)}) copy-start(f32[3,256]{1,0:T(4,128)} %param.29) | copy-start | bytes 9220
  83.0 62.0 %copy-start.16 = (pred[4096]{0:T(1024)(128)(4,1)}, pred[4096]{0:T(1024)(128)(4,1)S(1)}, u32[]{:S(2)}) copy-start(pred[4096]{0:T(1024)(128)(4,1)S(1)} %get-tuple-element.160) | copy-start | bytes 12292
  83.0 62.0 %copy-start.17 = (pred[4096]{0:T(1024)(128)(4,1)}, pred[4096]{0:T(1024)(128)(4,1)S(1)}, u32[]{:S(2)}) copy-start(pred[4096]{0:T(1024)(128)(4,1)S(1)} %get-tuple-element.161) | copy-start | bytes 12292
  83.0 62.0 %copy-start.18 = (pred[4096]{0:T(1024)(128)(4,1)}, pred[4096]{0:T(1024)(128)(4,1)S(1)}, u32[]{:S(2)}) copy-start(pred[4096]{0:T(1024)(128)(4,1)S(1)} %get-tuple-element.175) | copy-start | bytes 12292
  124.2 20.8 %copy-start.12 = (f32[4096]{0:T(1024)}, f32[4096]{0:T(1024)S(1)}, u32[]{:S(2)}) copy-start(f32[4096]{0:T(1024)S(1)} %select_reduce_fusion.14) | copy-start | bytes 49156
  129.1 7.0 %copy-start.2 = (bf16[4096,256]{1,0:T(8,128)(2,1)}, bf16[4096,256]{1,0:T(8,128)(2,1)S(1)}, u32[]{:S(2)}) copy-start(bf16[4096,256]{1,0:T(8,128)(2,1)S(1)} %add_convert_fusion.1) | copy-start | bytes 6291460
  129.2 16.0 %copy-start.9 = (f32[2,256,128]{2,1,0:T(8,128)S(1)}, f32[2,256,128]{2,1,0:T(8,128)}, u32[]{:S(2)}) copy-start(f32[2,256,128]{2,1,0:T(8,128)} %param.32) | copy-start | bytes 786436
  129.2 2.8 collective-permute-start
  130.6 5.6 collective-permute-start.1
  131.9 57.6 %copy-start.28 = (f32[1,256]{1,0:T(1,128)}, f32[1,256]{1,0:T(1,128)S(1)}, u32[]{:S(2)}) copy-start(f32[1,256]{1,0:T(1,128)S(1)} %get-tuple-element.176) | copy-start | bytes 3076
  131.9 57.6 %copy-start.30 = (f32[1,256]{1,0:T(1,128)}, f32[1,256]{1,0:T(1,128)S(1)}, u32[]{:S(2)}) copy-start(f32[1,256]{1,0:T(1,128)S(1)} %get-tuple-element.177) | copy-start | bytes 3076
  132.0 57.6 %copy-start.32 = (f32[1,256]{1,0:T(1,128)}, f32[1,256]{1,0:T(1,128)S(1)}, u32[]{:S(2)}) copy-start(f32[1,256]{1,0:T(1,128)S(1)} %get-tuple-element.178) | copy-start | bytes 3076
  132.0 13.0 %copy-start.19 = (bf16[16,256]{1,0:T(8,128)(2,1)}, bf16[16,256]{1,0:T(8,128)(2,1)S(1)}, u32[]{:S(2)}) copy-start(bf16[16,256]{1,0:T(8,128)(2,1)S(1)} %collective-permute-done) | copy-start | bytes 24580
  136.2 8.8 %copy-start.20 = (bf16[16,256]{1,0:T(8,128)(2,1)}, bf16[16,256]{1,0:T(8,128)(2,1)S(1)}, u32[]{:S(2)}) copy-start(bf16[16,256]{1,0:T(8,128)(2,1)S(1)} %collective-permute-done.1) | copy-start | bytes 24580
  185.9 48.5 %copy-start.14 = (f32[4096]{0:T(1024)}, f32[4096]{0:T(1024)S(1)}, u32[]{:S(2)}) copy-start(f32[4096]{0:T(1024)S(1)} %select_reduce_fusion.12) | copy-start | bytes 49156
  234.3 6.9 %copy-start.15 = (f32[4096]{0:T(1024)}, f32[4096]{0:T(1024)S(1)}, u32[]{:S(2)}) copy-start(f32[4096]{0:T(1024)S(1)} %select_reduce_fusion.10) | copy-start | bytes 49156
  281.1 17.0 %copy-start.4 = (bf16[4096,128]{1,0:T(8,128)(2,1)S(1)}, bf16[4096,128]{1,0:T(8,128)(2,1)}, u32[]{:S(2)}) copy-start(bf16[4096,128]{1,0:T(8,128)(2,1)} %all-gather.8.cloned.1.call-done) | copy-start | bytes 3145732
  281.1 17.8 %copy-start.3 = (bf16[4096,128]{1,0:T(8,128)(2,1)S(1)}, bf16[4096,128]{1,0:T(8,128)(2,1)}, u32[]{:S(2)}) copy-start(bf16[4096,128]{1,0:T(8,128)(2,1)} %all-gather.6.cloned.1.call-done) | copy-start | bytes 3145732
  295.5 5.0 collective-permute-start.2
  296.8 5.6 collective-permute-start.3
  299.6 3.1 copy-start
  299.6 3.1 copy-start.11
  299.6 3.1 copy-start.13
  299.7 3.0 copy-start.21
  299.7 3.0 copy-start.22
  299.7 3.0 copy-start.23
  299.7 3.0 copy-start.25
  299.7 3.0 copy-start.29
  299.7 3.0 copy-start.31
  299.7 3.0 copy-start.33
  355.2 11.0 %copy-start.8 = (bf16[4096,128]{1,0:T(8,128)(2,1)S(1)}, bf16[4096,128]{1,0:T(8,128)(2,1)}, u32[]{:S(2)}) copy-start(bf16[4096,128]{1,0:T(8,128)(2,1)} %all-gather.4.cloned.1.call-done) | copy-start | bytes 3145732
  364.9 1.4 copy-start.1
  367.6 115.8 %reduce-scatter.8.cloned.1.call-start = ((), (), s32[]{:S(2)}) async-start(), calls=%async_computation.8 | async-start | bytes 1572864 | tf_op jit(solution)/shard_map/reduce_scatter | solution.py:349
  371.0 143.9 %reduce-scatter.6.cloned.1.call-start = ((), (), s32[]{:S(2)}) async-start(), calls=%async_computation.5 | async-start | bytes 3145728 | tf_op jit(solution)/shard_map/reduce_scatter | solution.py:311
  373.1 176.0 %reduce-scatter.4.cloned.1.call-start = ((), (), s32[]{:S(2)}) async-start(), calls=%async_computation.4 | async-start | bytes 3145728 | tf_op jit(solution)/shard_map/reduce_scatter | solution.py:305
  375.2 6.3 %copy-start.5 = (bf16[4096,128]{1,0:T(8,128)(2,1)S(1)}, bf16[4096,128]{1,0:T(8,128)(2,1)}, u32[]{:S(2)}) copy-start(bf16[4096,128]{1,0:T(8,128)(2,1)} %all-gather.8.cloned.1.call-done) | copy-start | bytes 3145732
  375.2 6.9 %copy-start.37 = (f32[256]{0:T(256)S(1)}, f32[256]{0:T(256)}, u32[]{:S(2)}) copy-start(f32[256]{0:T(256)} %get-tuple-element.147) | copy-start | bytes 3076
  375.2 6.9 %copy-start.38 = (f32[256]{0:T(256)S(1)}, f32[256]{0:T(256)}, u32[]{:S(2)}) copy-start(f32[256]{0:T(256)} %get-tuple-element.148) | copy-start | bytes 3076
  375.2 7.6 %copy-start.35 = (f32[256]{0:T(256)S(1)}, f32[256]{0:T(256)}, u32[]{:S(2)}) copy-start(f32[256]{0:T(256)} %get-tuple-element.91) | copy-start | bytes 3076
  375.2 7.6 %copy-start.36 = (f32[256]{0:T(256)S(1)}, f32[256]{0:T(256)}, u32[]{:S(2)}) copy-start(f32[256]{0:T(256)} %get-tuple-element.97) | copy-start | bytes 3076
  375.2 108.2 %copy-start.7 = (bf16[2048,128]{1,0:T(8,128)(2,1)S(1)}, bf16[2048,128]{1,0:T(8,128)(2,1)}, u32[]{:S(2)}) copy-start(bf16[2048,128]{1,0:T(8,128)(2,1)} %param.24) | copy-start | bytes 1572868
  381.5 133.4 %copy-start.40 = (f32[128]{0:T(128)S(1)}, f32[128]{0:T(128)}, u32[]{:S(2)}) copy-start(f32[128]{0:T(128)} %get-tuple-element.179) | copy-start | bytes 1540
  381.5 167.6 %copy-start.6 = (bf16[2048,128]{1,0:T(8,128)(2,1)S(1)}, bf16[2048,128]{1,0:T(8,128)(2,1)}, u32[]{:S(2)}) copy-start(bf16[2048,128]{1,0:T(8,128)(2,1)} %param.22) | copy-start | bytes 1572868
  381.5 167.6 %copy-start.39 = (f32[128]{0:T(128)S(1)}, f32[128]{0:T(128)}, u32[]{:S(2)}) copy-start(f32[128]{0:T(128)} %get-tuple-element.180) | copy-start | bytes 1540
Sparse Core Ops, SparseCore 0:
  9.6 24.0 all-gather.3
  35.2 21.9 all-gather.5
  58.8 21.7 all-gather.7
  367.8 91.0 all-reduce.6
  461.6 19.3 reduce-scatter.7
  483.1 31.7 reduce-scatter.5
  517.2 31.8 reduce-scatter.3
where the time goes:
time: 561 us; the launch traced here: 559 us
  blocking collectives  310 us (55%)
  waiting for transfers between devices  101 us (18%)
  other arithmetic  82.3 us (15%)
  matrix products  25.6 us (5%)
  between operations  20.6 us (4%)
  local copies, waits for them, and re-layouts  14.1 us (3%)
    psum x2, blocking collectives, global_norm_backward(): lax.psum((element_sums(jnp.sum(scaled_values, axis=1), indicator_matrix),...  82.5 us
    psum x2, blocking collectives, global_norm_forward(): lax.psum(element_sums(jnp.sum(mean_removed * mean_removed, axis=1), indic...  81.5 us
    psum x2, blocking collectives, global_norm_forward(): lax.psum(element_sums(jnp.sum(active, axis=1), indicator_matrix), ('chan'...  80.3 us
    psum x1, blocking collectives, by_channels(): lax.psum((expand_grad, taps_grad, project_grad, vectors_grad, biases_grad...  60 us
    reduce_scatter x1, waiting for transfers between devices, by_channels(): lax.psum_scatter(jnp.dot(mixed_reduced, project_low[0], preferred_element...  32.1 us
    reduce_scatter x1, waiting for transfers between devices, by_channels(): lax.psum_scatter(jnp.dot(mixed_reduced, project_low[1], preferred_element...  29.3 us
    all_gather x1, waiting for transfers between devices, by_channels(): whole_in = lax.all_gather(frames_in, 'chan', axis=0, tiled=True)  19.4 us
    dot_general x6, matrix products, contract(): lax.dot_general(left_side, right_side, (((left_dim,), (right_dim,)), ((),...  16.9 us
  transfers between devices with their start and end apart: 11, of which 6 were waited for; matrix products, arithmetic and copies ran while one was open for 14% of the time, Pallas kernels for 0%

commit v1 on v0

v1 whole, which is shorter than its diff:
```python
import functools

import jax
import jax.numpy as jnp
from jax import lax
from jax.experimental import pallas as pl
from jax.experimental.pallas import tpu as pltpu
from jax.sharding import PartitionSpec as P

F32 = jnp.float32
BF16 = jnp.bfloat16
MESH = pl.DeviceIdType.MESH

DILATION = 16
HALO = 2 * DILATION
LONGEST_ITEM = 8192
LANES = 128
ROWS = 64
BLOCK = 512
PIECES = 16

norm_eps = 1e-06
clip_level = 5.0
rate = 0.05
small_rate = 0.5
beta_first = 0.9
beta_second = 0.999
adam_eps = 1e-08
decay = 0.01
step_count = 10.0

TAP_ROW = 6
BIAS_ROW = 9
SLOPE_TWO_ROW = 10
SLOPE_ONE_ROW = 11
SQUARES_ROW = 12

(GAIN_TWO, SHIFT_TWO, TAP_A, TAP_B, TAP_C, DEPTH_BIAS, GAIN_ONE, SHIFT_ONE, SLOPE_TWO, SLOPE_ONE, COLUMN_SUMS) = range(11)


def dot(a, b):
    return lax.dot_general(a, b, (((1,), (0,)), ((), ())), preferred_element_type=F32)


def dot_rows(a, b):
    return lax.dot_general(a, b, (((1,), (1,)), ((), ())), preferred_element_type=F32)


def dot_frames(a, b):
    return lax.dot_general(a, b, (((0,), (0,)), ((), ())), preferred_element_type=F32)


def rounded(v):
    return v.astype(BF16).astype(F32)


def spread_lanes(v):
    return jnp.broadcast_to(jnp.sum(v, axis=1, keepdims=True), (v.shape[0], LANES))


def fold_rows(v):
    return jnp.sum(v.reshape(v.shape[0] // 8, 8, v.shape[1]), axis=0)


def block_kernel(
    tm_size,
    item_count,
    item_pad,
    len_ref,
    slope_ref,
    frames_ref,
    out_cot_ref,
    skip_cot_ref,
    expand_ref,
    project_ref,
    taps_ref,
    vectors_ref,
    biases_ref,
    block_ref,
    skip_ref,
    input_grad_ref,
    expand_grad_ref,
    project_grad_ref,
    small_grad_ref,
    x,
    cots,
    w_expand,
    w_project,
    params,
    item_rows,
    item_cols,
    mask_low,
    mask_high,
    table,
    counts,
    act_one,
    xhat_one,
    normed,
    mixed_grad,
    act_two,
    mixed,
    hidden_grad,
    seg,
    column,
    block_out,
    skip_out,
    input_out,
    tile_one,
    tile_two,
    tile_three,
    stats_one,
    stats_two,
    stats_three,
    project_part,
    expand_part,
    project_in,
    expand_in,
    small_part,
    small_in,
    late_part,
    late_in,
    project_sum,
    expand_sum,
    small_sum,
    late_sum,
    square_part,
    square_in,
    local_sem,
    out_sem,
    send_sem,
    recv_sem,
):
    frames = block_out.shape[0]
    wide = x.shape[0]
    half = expand_ref.shape[1]
    hidden = 2 * half
    blocks = hidden // LANES
    devices = 2 * tm_size
    stride = tm_size // PIECES
    spans = -(-LONGEST_ITEM // frames)
    chan = lax.axis_index("chan")
    tm = lax.axis_index("tm")
    me = tm * 2 + chan
    other = 1 - chan

    def device(index):
        return {"chan": lax.rem(index, 2), "tm": lax.div(index, 2)}

    def remote(src, dst, phase, target):
        return pltpu.make_async_remote_copy(
            src_ref=src,
            dst_ref=dst,
            send_sem=send_sem.at[phase],
            recv_sem=recv_sem.at[phase],
            device_id=target,
            device_id_type=MESH,
        )

    def wait_bytes(ref, sem):
        pltpu.make_async_copy(ref, ref, sem).wait()

    own = pl.ds(HALO, frames)
    loads = [
        pltpu.make_async_copy(frames_ref, x.at[own, :], local_sem.at[0]),
        pltpu.make_async_copy(out_cot_ref, cots.at[own, pl.ds(0, LANES)], local_sem.at[1]),
        pltpu.make_async_copy(skip_cot_ref, cots.at[own, pl.ds(LANES, LANES)], local_sem.at[2]),
    ]
    for load in loads:
        load.start()

    barrier = pltpu.get_barrier_semaphore()

    def greet(k, carry):
        pl.semaphore_signal(
            barrier, inc=1, device_id=device(lax.rem(me + k, devices)), device_id_type=MESH
        )
        return carry

    lax.fori_loop(1, devices, greet, 0)

    my_half = pl.ds(pl.multiple_of(chan * half, half), half)
    w_expand[:, my_half] = expand_ref[...].astype(BF16)
    w_project[my_half, 0:LANES] = project_ref[0].astype(BF16)
    w_project[my_half, LANES : 2 * LANES] = project_ref[1].astype(BF16)
    params[0:6, my_half] = vectors_ref[...]
    params[6:9, my_half] = taps_ref[...]
    params[9:16, my_half] = jnp.zeros((7, half), F32)

    width = table.shape[0]
    lane = lax.broadcasted_iota(jnp.int32, (8, width), 1)
    lane_item = lax.rem(lane, item_pad)
    row_item = lax.broadcasted_iota(jnp.int32, (item_pad, LANES), 0)

    def bounds(j, carry):
        lane_start, lane_end, row_start, row_end = carry
        length = len_ref[j]
        return (
            lane_start + jnp.where(lane_item > j, length, 0),
            lane_end + jnp.where(lane_item >= j, length, 0),
            row_start + jnp.where(row_item > j, length, 0),
            row_end + jnp.where(row_item >= j, length, 0),
        )

    lane_zero, row_zero = jnp.zeros_like(lane), jnp.zeros_like(row_item)
    lane_start, lane_end, row_start, row_end = lax.fori_loop(
        0, item_count, bounds, (lane_zero, lane_zero, row_zero, row_zero)
    )
    lane_end = jnp.where(lane < 3 * item_pad, lane_end, lane_start)
    first = me * frames
    lane_start_row, lane_end_row = lane_start[0:1], lane_end[0:1]
    elements = jnp.maximum((row_end - row_start).astype(F32) * hidden, 1.0)

    def count_of(index):
        low = jnp.maximum(row_start, index * frames)
        high = jnp.minimum(row_end, (index + 1) * frames)
        return jnp.maximum(high - low, 0).astype(F32) * hidden

    my_count = count_of(me)
    my_safe = jnp.maximum(my_count, 1.0)
    offsets = [o for o in range(-spans, spans + 1) if o != 0]
    for slot, offset in enumerate(offsets):
        counts[slot] = count_of(lax.rem(me - offset + devices, devices))
    column[...] = jnp.zeros_like(column)

    def put_table(place, v):
        high = v.astype(BF16)
        rest = v - high.astype(F32)
        middle = rest.astype(BF16)
        low = (rest - middle.astype(F32)).astype(BF16)
        where = slice(place * LANES, (place + 1) * LANES)
        table[0:item_pad, where] = high
        table[item_pad : 2 * item_pad, where] = middle
        table[2 * item_pad : 3 * item_pad, where] = low

    def rows_of(r, n, count):
        return dot(item_rows[pl.ds(r, n), :], table[:, 0 : count * LANES])

    def part(values, k, n, b):
        return values[k : k + n, b * LANES : (b + 1) * LANES]

    def put_seg(r, n, place, v):
        high = v.astype(BF16)
        seg[pl.ds(r, n), pl.ds(2 * place * LANES, LANES)] = high
        seg[pl.ds(r, n), pl.ds((2 * place + 1) * LANES, LANES)] = (v - high.astype(F32)).astype(BF16)

    def item_sums(count):
        sums = dot(item_cols[...], seg[:, 0 : 2 * count * LANES])
        return [
            spread_lanes(
                sums[:, 2 * k * LANES : (2 * k + 1) * LANES]
                + sums[:, (2 * k + 1) * LANES : (2 * k + 2) * LANES]
            )
            for k in range(count)
        ]

    def loop(start, size, count, body, rep=1):
        def step(i, carry):
            i = i if rep == 1 else lax.rem(i, count)
            body(pl.multiple_of(start + i * size, 16))
            return carry

        lax.fori_loop(0, count * rep, step, 0)

    def at(r, k, shift=0):
        return pl.multiple_of(r + (k - shift), 16)

    table[...] = jnp.zeros_like(table)
    put_table(0, row_start.astype(F32))
    put_table(1, row_end.astype(F32))

    wide_block = wide // 4
    wide_rows = wide_block // 11

    @functools.partial(loop, 0, wide_block, 4)
    def _(r):
        for k in range(0, wide_block, wide_rows):
            position = first - HALO + r + k + lax.broadcasted_iota(jnp.int32, (wide_rows, width), 0)
            inside = (position >= lane_start_row) & (position < lane_end_row)
            item_rows[pl.ds(at(r, k), wide_rows), :] = inside.astype(F32).astype(BF16)
        ends = rows_of(r, wide_block, 2)
        for k in range(0, wide_block, wide_rows):
            here = first - HALO + r + k + lax.broadcasted_iota(jnp.int32, (wide_rows, LANES), 0)
            here = here.astype(F32)
            after = here - part(ends, k, wide_rows, 0)
            before = part(ends, k, wide_rows, 1) - here
            mask_low[pl.ds(at(r, k), wide_rows), :] = (after >= DILATION).astype(F32)
            mask_high[pl.ds(at(r, k), wide_rows), :] = (before > DILATION).astype(F32)

    for i in range(frames // LANES):
        position = first + i * LANES + lax.broadcasted_iota(jnp.int32, (item_pad, LANES), 1)
        inside = (position >= row_start) & (position < row_end)
        item_cols[:, i * LANES : (i + 1) * LANES] = inside.astype(F32).astype(BF16)

    loads[0].wait()
    pl.semaphore_wait(barrier, devices - 1)

    partner = device(tm * 2 + other)
    left, right = device(lax.rem(me + devices - 1, devices)), device(lax.rem(me + 1, devices))
    sends = [
        remote(w_expand.at[:, my_half], w_expand.at[:, my_half], 0, partner),
        remote(params.at[:, my_half], params.at[:, my_half], 1, partner),
        remote(x.at[pl.ds(HALO, HALO), :], x.at[pl.ds(HALO + frames, HALO), :], 2, left),
        remote(x.at[pl.ds(frames, HALO), :], x.at[pl.ds(0, HALO), :], 3, right),
        remote(w_project.at[my_half, :], w_project.at[my_half, :], 4, partner),
    ]
    for send in sends:
        send.start()
    loads[1].wait()
    loads[2].wait()
    edges = [
        remote(
            cots.at[pl.ds(HALO, DILATION), :], cots.at[pl.ds(HALO + frames, DILATION), :], 5, left
        ),
        remote(
            cots.at[pl.ds(HALO + frames - DILATION, DILATION), :],
            cots.at[pl.ds(HALO - DILATION, DILATION), :],
            6,
            right,
        ),
    ]
    for send in edges:
        send.start()

    slope_one, slope_two = slope_ref[0], slope_ref[1]

    def lanes_of(which, b):
        return pl.ds(pl.multiple_of(which * half + b * LANES, LANES), LANES)

    def half_of(which):
        return pl.ds(pl.multiple_of(which * half, half), half)

    def activate(product, k, n, which, b):
        v = part(product, k, n, b) + params[0:1, lanes_of(which, b)]
        return jnp.maximum(v, slope_one * v)

    own_loop = functools.partial(functools.partial, loop, HALO, BLOCK, frames // BLOCK)

    @own_loop()
    def _(r):
        product = dot(x[pl.ds(r, BLOCK), :], w_expand[:, half_of(chan)])
        for k in range(0, BLOCK, ROWS):
            total = jnp.zeros((ROWS, LANES), F32)
            for b in range(blocks // 2):
                a = activate(product, k, ROWS, chan, b)
                act_one[pl.ds(at(r, k), ROWS), lanes_of(chan, b)] = a
                total = total + a
            put_seg(at(r, k, HALO), ROWS, 0, total)

    (total,) = item_sums(1)
    shift = total / jnp.maximum(my_count * 0.5, 1.0)
    put_table(0, shift)
    for k in range(4):
        sends[k].wait_recv()

    @own_loop()
    def _(r):
        centres = rows_of(r, BLOCK, 1)
        product = dot(x[pl.ds(r, BLOCK), :], w_expand[:, half_of(other)])
        for k in range(0, BLOCK, ROWS):
            rows = pl.ds(at(r, k), ROWS)
            centre = part(centres, k, ROWS, 0)
            total = jnp.zeros((ROWS, LANES), F32)
            squares = jnp.zeros((ROWS, LANES), F32)
            for b in range(blocks // 2):
                d = act_one[rows, lanes_of(chan, b)] - centre
                total = total + d
                squares = squares + d * d
                a = activate(product, k, ROWS, other, b)
                act_one[rows, lanes_of(other, b)] = a
                d = a - centre
                total = total + d
                squares = squares + d * d
            put_seg(at(r, k, HALO), ROWS, 0, total)
            put_seg(at(r, k, HALO), ROWS, 1, squares)

    tile_lane = lax.broadcasted_iota(jnp.int32, (item_pad, LANES), 1)

    def pack_tile(values):
        tile = jnp.zeros((item_pad, LANES), F32)
        for k, v in enumerate(values):
            tile = jnp.where(tile_lane == k, v, tile)
        return tile

    def lane_of(tile, k):
        return spread_lanes(jnp.where(tile_lane == k, tile, 0.0))

    def local_moments(shift, total, squares):
        mean = shift + total / my_safe
        spread = jnp.maximum(squares - total * total / my_safe, 0.0)
        return mean, spread

    def exchange(tile, stats, phase):
        for slot, offset in enumerate(offsets):
            target = device(lax.rem(me + offset + devices, devices))
            remote(tile, stats.at[slot], phase, target).start()

    def arrived(stats, phase):
        wait_bytes(stats, recv_sem.at[phase])

    def combined(tile, stats):
        tiles = [tile[...]] + [stats[slot] for slot in range(len(offsets))]
        sizes = [my_count] + [counts[slot] for slot in range(len(offsets))]
        plain = tiles[0]
        for t in tiles[1:]:
            plain = plain + t
        mean = lane_of(plain, 0) / elements
        between = jnp.zeros((item_pad, LANES), F32)
        for t, size in zip(tiles, sizes):
            gap = t - mean
            between = between + size * gap * gap
        spread = (lane_of(plain, 1) + lane_of(between, 2)) / elements
        return tiles, plain, mean, lax.rsqrt(spread + norm_eps)

    total, squares = item_sums(2)
    mean, spread = local_moments(shift, total, squares)
    tile_one[...] = pack_tile([mean * my_count, spread, mean])
    exchange(tile_one, stats_one, 7)

    for r in (0, HALO + frames):
        for which in (chan, other):
            product = dot(x[pl.ds(r, HALO), :], w_expand[:, half_of(which)])
            for b in range(blocks // 2):
                act_one[pl.ds(r, HALO), lanes_of(which, b)] = activate(product, 0, HALO, which, b)

    sends[4].wait_recv()
    for send in edges:
        send.wait_recv()

    def lanes(b):
        return pl.ds(b * LANES, LANES)

    def mixed_rows(r, n, size, add):
        product = dot_rows(cots[pl.ds(r, n), :], w_project[...])
        for k in range(0, n, size):
            total = jnp.zeros((size, LANES), F32)
            for b in range(blocks):
                y = part(product, k, size, b)
                mixed_grad[pl.ds(at(r, k), size), lanes(b)] = y
                if add:
                    total = total + params[4:5, lanes(b)] * y
                    column[SHIFT_TWO, :, lanes(b)] += fold_rows(y)
            if add:
                put_seg(at(r, k, HALO), size, 2, total)

    @own_loop()
    def _(r):
        mixed_rows(r, BLOCK, ROWS, True)

    for r in (HALO - DILATION, HALO + frames):
        mixed_rows(r, DILATION, DILATION, False)
    bias_sum = dot(jnp.ones((16, frames), BF16), cots[own, :])[0:1]

    arrived(stats_one, 7)
    _, _, mean_one, scale_one = combined(tile_one, stats_one)
    put_table(0, mean_one)
    put_table(1, scale_one)

    @functools.partial(loop, 0, wide_block, 4)
    def _(r):
        values = rows_of(r, wide_block, 2)
        for k in range(0, wide_block, wide_rows):
            rows = pl.ds(at(r, k), wide_rows)
            mean, scale = part(values, k, wide_rows, 0), part(values, k, wide_rows, 1)
            for b in range(blocks):
                xhat = (act_one[rows, lanes(b)] - mean) * scale
                xhat_one[rows, lanes(b)] = xhat
                normed[rows, lanes(b)] = rounded(
                    params[1:2, lanes(b)] * xhat + params[2:3, lanes(b)]
                )

    def depth_rows(r, n, b):
        low, high = mask_low[pl.ds(r, n), :], mask_high[pl.ds(r, n), :]
        v = (
            params[3:4, lanes(b)]
            + params[6:7, lanes(b)] * (low * normed[pl.ds(r - DILATION, n), lanes(b)])
            + params[7:8, lanes(b)] * normed[pl.ds(r, n), lanes(b)]
            + params[8:9, lanes(b)] * (high * normed[pl.ds(r + DILATION, n), lanes(b)])
        )
        return jnp.maximum(v, slope_two * v)

    @own_loop()
    def _(r):
        for k in range(0, BLOCK, ROWS):
            a = depth_rows(at(r, k), ROWS, 0)
            act_two[pl.ds(at(r, k), ROWS), lanes(0)] = a
            put_seg(at(r, k, HALO), ROWS, 0, a)

    (total,) = item_sums(1)
    shift = total / jnp.maximum(my_count * (1.0 / blocks), 1.0)
    put_table(0, shift)

    @own_loop()
    def _(r):
        centres = rows_of(r, BLOCK, 1)
        for k in range(0, BLOCK, ROWS):
            rows = pl.ds(at(r, k), ROWS)
            centre = part(centres, k, ROWS, 0)
            total = jnp.zeros((ROWS, LANES), F32)
            squares = jnp.zeros((ROWS, LANES), F32)
            crossed = jnp.zeros((ROWS, LANES), F32)
            for b in range(blocks):
                if b == 0:
                    a = act_two[rows, lanes(b)]
                else:
                    a = depth_rows(at(r, k), ROWS, b)
                    act_two[rows, lanes(b)] = a
                d = a - centre
                total = total + d
                squares = squares + d * d
                crossed = crossed + params[4:5, lanes(b)] * mixed_grad[rows, lanes(b)] * d
            put_seg(at(r, k, HALO), ROWS, 0, total)
            put_seg(at(r, k, HALO), ROWS, 1, squares)
            put_seg(at(r, k, HALO), ROWS, 3, crossed)

    total, squares, q_sum, crossed = item_sums(4)
    mean, spread = local_moments(shift, total, squares)
    crossed = crossed - (mean - shift) * q_sum
    tile_two[...] = pack_tile([mean * my_count, spread, mean, q_sum, crossed])
    exchange(tile_two, stats_two, 8)

    for r in (HALO - DILATION, HALO + frames):
        for b in range(blocks):
            act_two[pl.ds(r, DILATION), lanes(b)] = depth_rows(r, DILATION, b)

    arrived(stats_two, 8)
    tiles, plain, mean_two, scale_two = combined(tile_two, stats_two)
    cross_sum = lane_of(plain, 4)
    for t in tiles:
        cross_sum = cross_sum + (lane_of(t, 2) - mean_two) * lane_of(t, 3)
    put_table(0, mean_two)
    put_table(1, scale_two)
    put_table(2, scale_two * lane_of(plain, 3) / elements)
    put_table(3, scale_two * scale_two * cross_sum / elements)

    def second_back(r, n, size, add):
        values = rows_of(r, n, 4)
        for k in range(0, n, size):
            rows = pl.ds(at(r, k), size)
            mean, scale, q_mean, cross_mean = [part(values, k, size, j) for j in range(4)]
            for b in range(blocks):
                a = act_two[rows, lanes(b)]
                y = mixed_grad[rows, lanes(b)]
                xhat = (a - mean) * scale
                g = (params[4:5, lanes(b)] * y) * scale - q_mean - xhat * cross_mean
                act_two[rows, lanes(b)] = rounded(g * jnp.where(a > 0, 1.0, slope_two))
                if add:
                    mixed[pl.ds(at(r, k, HALO), size), lanes(b)] = (
                        params[4:5, lanes(b)] * xhat + params[5:6, lanes(b)]
                    ).astype(BF16)
                    column[GAIN_TWO, :, lanes(b)] += fold_rows(y * xhat)
                    column[SLOPE_TWO, :, lanes(b)] += fold_rows(g * jnp.minimum(a, 0.0))

    @own_loop()
    def _(r):
        second_back(r, BLOCK, ROWS, True)

    for r in (HALO - DILATION, HALO + frames):
        second_back(r, DILATION, DILATION, False)

    @functools.partial(loop, HALO, 2 * ROWS, frames // (2 * ROWS))
    def _(r):
        for k in range(0, 2 * ROWS, ROWS):
            rows = pl.ds(at(r, k), ROWS)
            low, high = mask_low[rows, :], mask_high[rows, :]
            total = jnp.zeros((ROWS, LANES), F32)
            crossed = jnp.zeros((ROWS, LANES), F32)
            for b in range(blocks):
                later = high * act_two[pl.ds(at(r, k + DILATION), ROWS), lanes(b)]
                here = act_two[rows, lanes(b)]
                earlier = low * act_two[pl.ds(at(r, k - DILATION), ROWS), lanes(b)]
                n = normed[rows, lanes(b)]
                column[TAP_A, :, lanes(b)] += fold_rows(later * n)
                column[TAP_B, :, lanes(b)] += fold_rows(here * n)
                column[TAP_C, :, lanes(b)] += fold_rows(earlier * n)
                column[DEPTH_BIAS, :, lanes(b)] += fold_rows(here)
                y = (
                    params[6:7, lanes(b)] * later
                    + params[7:8, lanes(b)] * here
                    + params[8:9, lanes(b)] * earlier
                )
                column[SHIFT_ONE, :, lanes(b)] += fold_rows(y)
                xhat = xhat_one[rows, lanes(b)]
                column[GAIN_ONE, :, lanes(b)] += fold_rows(y * xhat)
                q = params[1:2, lanes(b)] * y
                mixed_grad[rows, lanes(b)] = q
                total = total + q
                crossed = crossed + q * xhat
            put_seg(at(r, k, HALO), ROWS, 0, total)
            put_seg(at(r, k, HALO), ROWS, 1, crossed)

    total, crossed = item_sums(2)
    tile_three[...] = pack_tile([total, crossed])
    exchange(tile_three, stats_three, 9)

    @own_loop()
    def _(r):
        product = dot(mixed[pl.ds(at(r, 0, HALO), BLOCK), :], w_project[...])
        for k in range(0, BLOCK, ROWS):
            rows = pl.ds(at(r, k, HALO), ROWS)
            inputs = x[pl.ds(at(r, k), ROWS), :].astype(F32)
            block_out[rows, :] = (
                inputs + part(product, k, ROWS, 0) + biases_ref[0:1, :]
            ).astype(BF16)
            skip_out[rows, :] = (part(product, k, ROWS, 1) + biases_ref[1:2, :]).astype(BF16)

    stores = [
        pltpu.make_async_copy(block_out, block_ref, out_sem.at[0]),
        pltpu.make_async_copy(skip_out, skip_ref, out_sem.at[1]),
    ]
    for store in stores:
        store.start()

    step = 512
    total = jnp.zeros((2 * LANES, hidden), F32)
    for k in range(frames // step):
        total = total + dot_frames(
            cots[pl.ds(HALO + k * step, step), :], mixed[pl.ds(k * step, step), :]
        )
    project_part[...] = total

    def column_sum(which):
        return jnp.sum(column[which], axis=0, keepdims=True)

    early_rows = {
        1: column_sum(GAIN_ONE),
        2: column_sum(SHIFT_ONE),
        3: column_sum(DEPTH_BIAS),
        4: column_sum(GAIN_TWO),
        5: column_sum(SHIFT_TWO),
        TAP_ROW: column_sum(TAP_A),
        TAP_ROW + 1: column_sum(TAP_B),
        TAP_ROW + 2: column_sum(TAP_C),
    }
    slope_two_row = column_sum(SLOPE_TWO)
    slope_two_row = (slope_two_row[:, 0:half] + slope_two_row[:, half:hidden]) / slope_two
    for c in range(2):
        small_part[c] = jnp.zeros((16, half), F32)
        for row, v in early_rows.items():
            small_part[c, row : row + 1, :] = v[:, c * half : (c + 1) * half]
        small_part[c, BIAS_ROW : BIAS_ROW + 1, :] = bias_sum
        small_part[c, SLOPE_TWO_ROW : SLOPE_TWO_ROW + 1, :] = slope_two_row

    reducers = 2 * PIECES
    piece = lax.div(tm, stride)
    place = piece * 2 + chan

    def when_reducer(body):
        if stride == 1:
            body()
        else:
            pl.when(lax.rem(tm, stride) == 0)(body)

    def reducer_device(q):
        return lax.rem(q, 2), lax.div(q, 2) * stride

    def to_reducers(send):
        def one(k, carry):
            q = lax.rem(place + k, reducers)
            c, t = reducer_device(q)
            if stride == 1:
                send(q, {"chan": c, "tm": t})
            else:

                @pl.when(t * 2 + c != me)
                def _():
                    send(q, {"chan": c, "tm": t})

            return carry

        lax.fori_loop(1 if stride == 1 else 0, reducers, one, 0)

    def project_piece(q):
        rows = pl.ds(pl.multiple_of(lax.div(q, 2) * 16, 16), 16)
        return rows, pl.ds(pl.multiple_of(lax.rem(q, 2) * half, half), half)

    def expand_piece(q):
        j, c = lax.div(q, 2), lax.rem(q, 2)
        rows = pl.ds(pl.multiple_of(lax.div(j, 2) * 16, 16), 16)
        at = c * half + lax.rem(j, 2) * LANES
        return rows, pl.ds(pl.multiple_of(at, LANES), LANES)

    def send_project(q, target):
        rows, cols = project_piece(q)
        remote(project_part.at[rows, cols], project_in.at[me], 10, target).start()

    to_reducers(send_project)
    for c in range(2):

        @pl.when((tm != 0) | (chan != c))
        def _(c=c):
            remote(small_part.at[c], small_in.at[me], 11, {"chan": c, "tm": 0}).start()

    arrived(stats_three, 9)
    plain = tile_three[...]
    for slot in range(len(offsets)):
        plain = plain + stats_three[slot]
    put_table(0, lane_of(plain, 0) / elements)
    put_table(1, lane_of(plain, 1) / elements)
    put_table(2, scale_one)

    @own_loop()
    def _(r):
        values = rows_of(r, BLOCK, 3)
        for k in range(0, BLOCK, ROWS):
            rows, local = pl.ds(at(r, k), ROWS), pl.ds(at(r, k, HALO), ROWS)
            q_mean, cross_mean, scale = [part(values, k, ROWS, j) for j in range(3)]
            for b in range(blocks):
                a = act_one[rows, lanes(b)]
                g = (mixed_grad[rows, lanes(b)] - q_mean - xhat_one[rows, lanes(b)] * cross_mean) * scale
                column[SLOPE_ONE, :, lanes(b)] += fold_rows(g * jnp.minimum(a, 0.0))
                hidden_grad[local, lanes(b)] = (g * jnp.where(a > 0, 1.0, slope_one)).astype(BF16)

    total = jnp.zeros((LANES, hidden), F32)
    for k in range(frames // step):
        total = total + dot_frames(
            x[pl.ds(HALO + k * step, step), :], hidden_grad[pl.ds(k * step, step), :]
        )
    expand_part[...] = total
    bias_one = dot(jnp.ones((16, frames), BF16), hidden_grad[...])[0:1]
    slope_row = column_sum(SLOPE_ONE)
    slope_row = (slope_row[:, 0:half] + slope_row[:, half:hidden]) / slope_one
    for c in range(2):
        late_part[c] = jnp.zeros((8, half), F32)
        late_part[c, 0:1, :] = bias_one[:, c * half : (c + 1) * half]
        late_part[c, 1:2, :] = slope_row

    def send_expand(q, target):
        rows, cols = expand_piece(q)
        remote(expand_part.at[rows, cols], expand_in.at[me], 12, target).start()

    to_reducers(send_expand)
    for c in range(2):

        @pl.when((tm != 0) | (chan != c))
        def _(c=c):
            remote(late_part.at[c], late_in.at[me], 13, {"chan": c, "tm": 0}).start()

    def to_group(send):
        def one(k, carry):
            send({"chan": chan, "tm": lax.rem(tm + k, tm_size)})
            return carry

        lax.fori_loop(1, tm_size, one, 0)

    my_sum_rows = pl.ds(pl.multiple_of(piece * 16, 16), 16)

    def sum_project():
        rows, cols = project_piece(place)
        wait_bytes(project_in.at[pl.ds(0, devices - 1)], recv_sem.at[10])
        project_in[me] = project_part[rows, cols]

        def add(k, total):
            return total + project_in[k]

        total = lax.fori_loop(0, devices, add, jnp.zeros((16, half), F32))
        project_sum[my_sum_rows, :] = total
        squares = jnp.sum(total * total, axis=0, keepdims=True)
        square_part[...] = squares[:, 0:LANES] + squares[:, LANES:half]

        def send(target):
            remote(project_sum.at[my_sum_rows, :], project_sum.at[my_sum_rows, :], 14, target).start()

        to_group(send)

    when_reducer(sum_project)

    @pl.when(tm == 0)
    def _():
        wait_bytes(small_in.at[pl.ds(0, devices - 1)], recv_sem.at[11])
        small_in[me] = small_part[chan]

        def add(k, total):
            return total + small_in[k]

        total = lax.fori_loop(0, devices, add, jnp.zeros((16, half), F32))
        small_sum[...] = total
        squares = jnp.sum((total * total)[0:BIAS_ROW], axis=0, keepdims=True)
        square_part[...] += squares[:, 0:LANES] + squares[:, LANES:half]

        def send(target):
            remote(small_sum, small_sum, 15, target).start()

        to_group(send)

    @own_loop()
    def _(r):
        product = dot_rows(hidden_grad[pl.ds(at(r, 0, HALO), BLOCK), :], w_expand[...])
        for k in range(0, BLOCK, ROWS):
            above = cots[pl.ds(at(r, k), ROWS), 0:LANES].astype(F32)
            input_out[pl.ds(at(r, k, HALO), ROWS), :] = above + part(product, k, ROWS, 0)

    stores.append(pltpu.make_async_copy(input_out, input_grad_ref, out_sem.at[2]))
    stores[2].start()

    def sum_piece(q):
        j = lax.div(q, 2)
        rows = pl.ds(pl.multiple_of(lax.div(j, 2) * 16, 16), 16)
        return rows, pl.ds(pl.multiple_of(lax.rem(j, 2) * LANES, LANES), LANES)

    @pl.when(tm == 0)
    def _():
        wait_bytes(late_in.at[pl.ds(0, devices - 1)], recv_sem.at[13])
        late_in[me] = late_part[chan]

        def add(k, total):
            return total + late_in[k]

        total = lax.fori_loop(0, devices, add, jnp.zeros((8, half), F32))
        late_sum[...] = total
        squares = (total * total)[0:1]
        square_part[...] += squares[:, 0:LANES] + squares[:, LANES:half]

        def send(target):
            remote(late_sum, late_sum, 16, target).start()

        to_group(send)

    def sum_expand():
        wait_bytes(expand_in.at[pl.ds(0, devices - 1)], recv_sem.at[12])
        rows, cols = expand_piece(place)
        expand_in[me] = expand_part[rows, cols]

        def add(k, total):
            return total + expand_in[k]

        total = lax.fori_loop(0, devices, add, jnp.zeros((16, LANES), F32))
        rows, cols = sum_piece(place)
        expand_sum[rows, cols] = total
        square_part[...] += jnp.sum(total * total, axis=0, keepdims=True)
        square_in[place] = square_part[...]

        def send(target):
            remote(expand_sum.at[rows, cols], expand_sum.at[rows, cols], 17, target).start()

        to_group(send)

        def send_square(k, carry):
            target = device(lax.rem(me + k, devices))
            remote(square_part, square_in.at[place], 18, target).start()
            return carry

        lax.fori_loop(1, devices, send_square, 0)

    when_reducer(sum_expand)

    def wait_group(ref, phase, mine):
        rows = ref.shape[0] // PIECES

        def some(count):
            wait_bytes(ref.at[pl.ds(0, count * rows)], recv_sem.at[phase])

        if stride == 1:
            some(PIECES - 1)
        else:
            is_reducer = lax.rem(tm, stride) == 0
            pl.when(is_reducer)(lambda: some(PIECES - 1))
            pl.when(jnp.logical_not(is_reducer))(lambda: some(PIECES))

    wait_group(project_sum, 14, None)
    for k in range(2):
        project_grad_ref[k] = project_sum[k * LANES : (k + 1) * LANES, :].T

    @pl.when(tm != 0)
    def _():
        wait_bytes(small_sum, recv_sem.at[15])
        wait_bytes(late_sum, recv_sem.at[16])

    small_grad_ref[...] = small_sum[...]
    small_grad_ref[0:1, :] = late_sum[0:1, :]
    small_grad_ref[SLOPE_ONE_ROW : SLOPE_ONE_ROW + 1, :] = late_sum[1:2, :]
    wait_group(expand_sum, 17, None)
    expand_grad_ref[...] = expand_sum[...]

    def wait_squares(count):
        wait_bytes(square_in.at[pl.ds(0, count)], recv_sem.at[18])

    if stride == 1:
        wait_squares(reducers - 1)
    else:
        is_reducer = lax.rem(tm, stride) == 0
        pl.when(is_reducer)(lambda: wait_squares(reducers - 1))
        pl.when(jnp.logical_not(is_reducer))(lambda: wait_squares(reducers))
    total = square_in[0]
    for q in range(1, reducers):
        total = total + square_in[q]
    small_grad_ref[SQUARES_ROW : SQUARES_ROW + 1, 0:LANES] = total
    small_grad_ref[SQUARES_ROW : SQUARES_ROW + 1, LANES:half] = jnp.zeros((1, half - LANES), F32)

    for send in sends + edges:
        send.wait_send()
    for phase, stats in ((7, stats_one), (8, stats_two), (9, stats_three)):
        wait_bytes(stats, send_sem.at[phase])

    def sent_to_reducers(ref, phase):
        if stride == 1:
            wait_bytes(ref.at[pl.ds(0, reducers - 1)], send_sem.at[phase])
        else:
            is_reducer = lax.rem(tm, stride) == 0
            pl.when(is_reducer)(
                lambda: wait_bytes(ref.at[pl.ds(0, reducers - 1)], send_sem.at[phase])
            )
            pl.when(jnp.logical_not(is_reducer))(
                lambda: wait_bytes(ref.at[pl.ds(0, reducers)], send_sem.at[phase])
            )

    sent_to_reducers(project_in, 10)
    sent_to_reducers(expand_in, 12)
    for part, phase in ((small_in, 11), (late_in, 13)):
        pl.when(tm == 0)(lambda: wait_bytes(part.at[0], send_sem.at[phase]))
        pl.when(tm != 0)(lambda: wait_bytes(part.at[pl.ds(0, 2)], send_sem.at[phase]))

    def group_bytes(ref, phase):
        def one(k, carry):
            wait_bytes(ref, send_sem.at[phase])
            return carry

        lax.fori_loop(1, tm_size, one, 0)

    def sent_sums():
        group_bytes(project_sum.at[pl.ds(0, 16), :], 14)
        rows, cols = sum_piece(place)
        group_bytes(expand_sum.at[rows, cols], 17)

        def one(k, carry):
            wait_bytes(square_part, send_sem.at[18])
            return carry

        lax.fori_loop(1, devices, one, 0)

    when_reducer(sent_sums)

    @pl.when(tm == 0)
    def _():
        group_bytes(small_sum, 15)
        group_bytes(late_sum, 16)

    for store in stores:
        store.wait()


def adam(weight, moment, square, gradient, scale, step_rate):
    clipped = gradient * scale
    moment_next = beta_first * moment + (1.0 - beta_first) * clipped
    square_next = beta_second * square + (1.0 - beta_second) * clipped * clipped
    update = (
        moment_next
        / (1.0 - beta_first**step_count)
        / (jnp.sqrt(square_next / (1.0 - beta_second**step_count)) + adam_eps)
    )
    return weight - step_rate * (update + decay * weight), moment_next, square_next


def adam_kernel(
    block_in,
    skip_in,
    input_in,
    expand_grad,
    project_grad,
    small_grad,
    *refs,
):
    state, outs = refs[:18], refs[18:40]
    sem = refs[40]
    copies = [
        pltpu.make_async_copy(src, dst, sem.at[k])
        for k, (src, dst) in enumerate(
            zip((block_in, skip_in, input_in), (outs[0], outs[1], outs[2]))
        )
    ]
    for copy in copies:
        copy.start()
    biases = small_grad[BIAS_ROW : BIAS_ROW + 1, :]
    slopes = [
        jnp.sum(small_grad[row : row + 1, :], axis=1, keepdims=True)
        for row in (SLOPE_ONE_ROW, SLOPE_TWO_ROW)
    ]
    total = jnp.sum(small_grad[SQUARES_ROW : SQUARES_ROW + 1, :] + biases * biases, axis=1, keepdims=True)
    total = total + slopes[0] * slopes[0] + slopes[1] * slopes[1]
    grad_norm = jnp.sqrt(total)
    scale = jnp.minimum(1.0, clip_level / grad_norm)
    outs[3][0, 0] = grad_norm[0, 0]

    def update(k, gradient, step_rate, at=...):
        results = adam(
            state[3 * k][at], state[3 * k + 1][at], state[3 * k + 2][at], gradient, scale, step_rate
        )
        for j in range(3):
            outs[4 + 3 * k + j][at] = results[j]

    update(0, expand_grad[...], rate)
    update(1, small_grad[TAP_ROW : TAP_ROW + 3, :], small_rate)
    for k in range(2):
        update(2, project_grad[k], rate, k)
    update(3, small_grad[0:6, :], small_rate)
    lanes = biases.shape[1] // 2
    for k in range(2):
        update(4, biases[:, k * lanes : (k + 1) * lanes], small_rate, slice(k, k + 1))
    for k in range(2):
        results = adam(
            state[15][k], state[16][k], state[17][k], slopes[k], scale, small_rate
        )
        for j in range(3):
            outs[19 + j][k] = results[j][0, 0]
    for copy in copies:
        copy.wait()


def per_device(
    tm_size,
    frames_in,
    item_lengths,
    out_cotangent,
    skip_cotangent,
    expand,
    expand_moment,
    expand_square,
    depthwise,
    depth_moment,
    depth_square,
    project,
    project_moment,
    project_square,
    channel_vectors,
    vector_moment,
    vector_square,
    output_biases,
    bias_moment,
    bias_square,
    prelu_slopes,
    slope_moment,
    slope_square,
):
    frames, inputs = frames_in.shape
    half = expand.shape[1]
    hidden = 2 * half
    items = item_lengths.shape[0]
    item_pad = -(-items // 16) * 16
    width = -(-3 * item_pad // LANES) * LANES
    wide = frames + 2 * HALO
    devices = 2 * tm_size
    reducers = 2 * PIECES
    peers = 2 * (-(-LONGEST_ITEM // frames))
    vmem, smem, anywhere = (
        pl.BlockSpec(memory_space=pltpu.VMEM),
        pl.BlockSpec(memory_space=pltpu.SMEM),
        pl.BlockSpec(memory_space=pl.ANY),
    )
    shape = jax.ShapeDtypeStruct
    scratch = [
        ((wide, inputs), BF16),
        ((wide, 2 * inputs), BF16),
        ((inputs, hidden), BF16),
        ((hidden, 2 * inputs), BF16),
        ((16, hidden), F32),
        ((wide, width), BF16),
        ((item_pad, frames), BF16),
        ((wide, LANES), F32),
        ((wide, LANES), F32),
        ((width, 4 * LANES), BF16),
        ((peers, item_pad, LANES), F32),
        ((wide, hidden), F32),
        ((wide, hidden), F32),
        ((wide, hidden), F32),
        ((wide, hidden), F32),
        ((wide, hidden), F32),
        ((frames, hidden), BF16),
        ((frames, hidden), BF16),
        ((frames, 8 * LANES), BF16),
        ((COLUMN_SUMS, 8, hidden), F32),
        ((frames, inputs), BF16),
        ((frames, inputs), BF16),
        ((frames, inputs), F32),
        ((item_pad, LANES), F32),
        ((item_pad, LANES), F32),
        ((item_pad, LANES), F32),
        ((peers, item_pad, LANES), F32),
        ((peers, item_pad, LANES), F32),
        ((peers, item_pad, LANES), F32),
        ((2 * inputs, hidden), F32),
        ((inputs, hidden), F32),
        ((devices, 16, half), F32),
        ((devices, 16, LANES), F32),
        ((2, 16, half), F32),
        ((devices, 16, half), F32),
        ((2, 8, half), F32),
        ((devices, 8, half), F32),
        ((2 * inputs, half), F32),
        ((inputs, half), F32),
        ((16, half), F32),
        ((8, half), F32),
        ((1, LANES), F32),
        ((reducers, 1, LANES), F32),
    ]
    block_raw, skip_raw, input_raw, expand_grad, project_grad, small_grad = pl.pallas_call(
        functools.partial(block_kernel, tm_size, items, item_pad),
        out_shape=[
            shape((frames, inputs), BF16),
            shape((frames, inputs), BF16),
            shape((frames, inputs), F32),
            shape((inputs, half), F32),
            shape((2, half, inputs), F32),
            shape((16, half), F32),
        ],
        in_specs=[smem, smem] + [anywhere] * 3 + [vmem] * 5,
        out_specs=[anywhere] * 3 + [vmem] * 3,
        scratch_shapes=[pltpu.VMEM(s, t) for s, t in scratch]
        + [
            pltpu.SemaphoreType.DMA((3,)),
            pltpu.SemaphoreType.DMA((3,)),
            pltpu.SemaphoreType.DMA((19,)),
            pltpu.SemaphoreType.DMA((19,)),
        ],
        compiler_params=pltpu.CompilerParams(
            collective_id=0, has_side_effects=True, vmem_limit_bytes=60 * 2**20
        ),
        name="temporal_block",
    )(
        item_lengths,
        prelu_slopes,
        frames_in,
        out_cotangent,
        skip_cotangent,
        expand,
        project,
        depthwise,
        channel_vectors,
        output_biases,
    )
    state = [
        expand,
        expand_moment,
        expand_square,
        depthwise,
        depth_moment,
        depth_square,
        project,
        project_moment,
        project_square,
        channel_vectors,
        vector_moment,
        vector_square,
        output_biases,
        bias_moment,
        bias_square,
        prelu_slopes,
        slope_moment,
        slope_square,
    ]
    results = pl.pallas_call(
        adam_kernel,
        out_shape=[
            shape((frames, inputs), BF16),
            shape((frames, inputs), BF16),
            shape((frames, inputs), F32),
            shape((1, 1), F32),
        ]
        + [shape(v.shape, F32) for v in state],
        in_specs=[anywhere] * 3 + [vmem] * 18 + [smem] * 3,
        out_specs=[anywhere] * 3 + [smem] + [vmem] * 15 + [smem] * 3,
        scratch_shapes=[pltpu.SemaphoreType.DMA((3,))],
        compiler_params=pltpu.CompilerParams(vmem_limit_bytes=32 * 2**20),
        name="adam_step",
    )(block_raw, skip_raw, input_raw, expand_grad, project_grad, small_grad, *state)
    results = list(results)
    results[3] = results[3].reshape(())
    return tuple(results)


def solution(mesh):
    frames = P(("tm", "chan"), None)
    columns = P(None, "chan")
    rows = P(None, "chan", None)
    in_specs = (
        (frames, P(), frames, frames)
        + (columns,) * 3
        + (columns,) * 3
        + (rows,) * 3
        + (columns,) * 3
        + (P(),) * 6
    )
    out_specs = (
        (frames, frames, frames, P())
        + (columns,) * 3
        + (columns,) * 3
        + (rows,) * 3
        + (columns,) * 3
        + (P(),) * 6
    )
    return jax.shard_map(
        functools.partial(per_device, mesh.shape["tm"]),
        mesh=mesh,
        in_specs=in_specs,
        out_specs=out_specs,
        check_vma=False,
    )
```

time: 561 us -> 83.2 us (0.15)
  blocking collectives: 310 us -> 0 us
  waiting for transfers between devices: 101 us -> 0 us
  other arithmetic: 82.3 us -> 0 us
  Pallas kernels: 0 us -> 75.3 us
  matrix products: 25.6 us -> 0 us
  between operations: 20.6 us -> 0.94 us
  local copies, waits for them, and re-layouts: 14.1 us -> 6.47 us
    psum x8 -> x0, blocking collectives: 310 us -> none  [the longest x2 82.5 us: global_norm_backward(): lax.psum((element_sums(jnp.sum(scaled_values, axis=1), indicator_matrix),...]
    pallas_call x0 -> x2, Pallas kernels: none -> 75.3 us  [the longest x1 71.9 us: per_device(): pl.pallas_call(functools.partial(block_kernel, tm_size, items, item_pad),...]
    reduce_scatter x3 -> x0, waiting for transfers between devices: 61.5 us -> none  [the longest x1 32.1 us: by_channels(): lax.psum_scatter(jnp.dot(mixed_reduced, project_low[0], preferred_element...]
    reduce_sum x27 -> x0, other arithmetic: 57.2 us -> none  [the longest x1 14.4 us: backward_core(): jnp.sum(jnp.where(depthwise_output > 0, 0.0, active_two * depthwise_output))]
    dot_general x9 -> x0, matrix products: 25.6 us -> none  [the longest x6 16.9 us: contract(): lax.dot_general(left_side, right_side, (((left_dim,), (right_dim,)), ((),...]
    all_gather x3 -> x0, waiting for transfers between devices: 19.5 us -> none  [the longest x1 19.4 us: by_channels(): whole_in = lax.all_gather(frames_in, 'chan', axis=0, tiled=True)]
    psum x1 -> x0, waiting for transfers between devices: 12.1 us -> none  [by_channels(): lax.psum((expand_grad, taps_grad, project_grad, vectors_grad, biases_grad...]
    convert_element_type x5 -> x0, other arithmetic: 9.46 us -> none  [the longest x1 4.89 us: forward_core(): normed_low = normalized_values.astype(jnp.bfloat16)]
  transfers between devices with their start and end apart: 11 -> 0, of which waited for: 6 -> 0; matrix products, arithmetic and copies ran while one was open for 14% -> 0% of each run, Pallas kernels for 0% -> 0%
where the time goes in v1:
time: 83.2 us; the launch traced here: 82.7 us
  Pallas kernels  75.3 us (91%)
  local copies, waits for them, and re-layouts  6.47 us (8%)
  between operations  0.94 us (1%)
    pallas_call x1, Pallas kernels, per_device(): pl.pallas_call(functools.partial(block_kernel, tm_size, items, item_pad),...  71.9 us
    unnamed x48, local copies, waits for them, and re-layouts  6.47 us
    pallas_call x1, Pallas kernels, per_device(): pl.pallas_call(adam_kernel, out_shape=[shape((frames, inputs), BF16), sha...  3.4 us

profile of v1, /device:TPU:0, one launch (start us, length us, event | category | flops | bytes accessed | tf_op | source)
XLA Modules:
  0.0 82.7 jit_solution(11453303459467153879)
XLA Ops:
  0.7 0.0 copy-start
  0.7 0.0 copy-start.2
  0.7 0.0 copy-start.6
  0.7 0.0 copy-start.5
  0.7 0.0 copy-start.9
  0.7 0.0 copy-start.8
  0.7 0.0 copy-start.13
  0.7 0.0 copy-start.14
  0.7 0.0 copy-start.15
  0.8 0.0 copy-start.16
  0.8 0.0 copy-start.17
  0.8 0.0 copy-start.20
  0.8 0.0 copy-start.21
  0.8 0.0 copy-start.22
  0.8 0.0 copy-start.23
  0.8 71.9 %temporal_block.1 = (bf16[2048,128]{1,0:T(8,128)(2,1)}, bf16[2048,128]{1,0:T(8,128)(2,1)}, f32[2048,128]{1,0:T(8,128)}, f32[128,256]{1,0:T(8,128)}, f32[2,256,128]{2,1,0:T(8,128)}, /*index=5*/f32[16,256]{1,0:T(8,128)}) custom-call(s32[16]{0:T(128)} %len_ref.1, f32[2]{0:T(128)} %refs_15_.1, bf16[2048,128]{1,0:T(8,128)(2,1)} %frames_ref.1, ...), custom_call_target="tpu_custom_call" | custom-call | tf_op jit(solution)/shard_map/temporal_block/pallas_call | solution.py:1094
  72.7 0.0 copy-start.11
  72.8 0.0 copy-start.18
  72.8 0.0 copy-start.19
  72.8 0.0 copy-done
  72.8 0.0 copy-done.2
  72.8 0.0 copy-done.6
  72.8 0.0 copy-done.5
  72.8 0.0 copy-done.9
  72.8 0.0 copy-done.8
  72.8 0.0 copy-done.13
  72.9 0.0 copy-done.14
  72.9 0.0 copy-done.15
  72.9 0.0 copy-done.16
  72.9 0.0 copy-done.17
  72.9 0.0 copy-done.20
  72.9 0.0 copy-done.21
  72.9 0.0 copy-done.22
  72.9 0.0 copy-done.23
  72.9 0.5 copy-done.11
  73.4 0.0 copy-done.18
  73.4 0.0 copy-done.19
  73.5 0.0 copy-start.1
  73.5 1.2 %copy-done.1 = f32[2048,128]{1,0:T(8,128)S(1)} copy-done((f32[2048,128]{1,0:T(8,128)S(1)}, f32[2048,128]{1,0:T(8,128)}, u32[]{:S(2)}) %copy-start.1) | copy-done | bytes 1048600
  74.7 0.0 copy-start.3
  74.7 1.0 %copy-done.3 = bf16[2048,128]{1,0:T(8,128)(2,1)S(1)} copy-done((bf16[2048,128]{1,0:T(8,128)(2,1)S(1)}, bf16[2048,128]{1,0:T(8,128)(2,1)}, u32[]{:S(2)}) %copy-start.3) | copy-done | bytes 524312
  75.7 0.0 copy-start.4
  75.7 1.0 %copy-done.4 = bf16[2048,128]{1,0:T(8,128)(2,1)S(1)} copy-done((bf16[2048,128]{1,0:T(8,128)(2,1)S(1)}, bf16[2048,128]{1,0:T(8,128)(2,1)}, u32[]{:S(2)}) %copy-start.4) | copy-done | bytes 524312
  76.8 0.0 copy-start.7
  76.8 0.9 %copy-done.7 = f32[2,256,128]{2,1,0:T(8,128)S(1)} copy-done((f32[2,256,128]{2,1,0:T(8,128)S(1)}, f32[2,256,128]{2,1,0:T(8,128)}, u32[]{:S(2)}) %copy-start.7) | copy-done | bytes 262168
  77.7 0.0 copy-start.10
  77.7 0.9 %copy-done.10 = f32[128,256]{1,0:T(8,128)S(1)} copy-done((f32[128,256]{1,0:T(8,128)S(1)}, f32[128,256]{1,0:T(8,128)}, u32[]{:S(2)}) %copy-start.10) | copy-done | bytes 131096
  78.6 0.0 copy-start.12
  78.6 0.7 copy-done.12
  79.3 3.4 %adam_step.1 = (bf16[2048,128]{1,0:T(8,128)(2,1)}, bf16[2048,128]{1,0:T(8,128)(2,1)}, f32[2048,128]{1,0:T(8,128)}, f32[1,1]{1,0:T(1,128)}, f32[128,256]{1,0:T(8,...) custom-call(bf16[2048,128]{1,0:T(8,128)(2,1)S(1)} %copy-done.3, ...), custom_call_target="tpu_custom_call" | custom-call | tf_op jit(solution)/shard_map/adam_step/pallas_call | solution.py:1149
Async XLA Ops:
  0.7 72.1 %copy-start = (f32[2,256,128]{2,1,0:T(8,128)S(1)}, f32[2,256,128]{2,1,0:T(8,128)}, u32[]{:S(2)}) copy-start(f32[2,256,128]{2,1,0:T(8,128)} %refs_6_.1) | copy-start | bytes 786436
  0.7 72.1 %copy-start.2 = (f32[128,256]{1,0:T(8,128)S(1)}, f32[128,256]{1,0:T(8,128)}, u32[]{:S(2)}) copy-start(f32[128,256]{1,0:T(8,128)} %refs_0_.1) | copy-start | bytes 393220
  0.7 72.1 %copy-start.6 = (f32[2,256,128]{2,1,0:T(8,128)S(1)}, f32[2,256,128]{2,1,0:T(8,128)}, u32[]{:S(2)}) copy-start(f32[2,256,128]{2,1,0:T(8,128)} %refs_8_.1) | copy-start | bytes 786436
  0.7 72.1 %copy-start.5 = (f32[2,256,128]{2,1,0:T(8,128)S(1)}, f32[2,256,128]{2,1,0:T(8,128)}, u32[]{:S(2)}) copy-start(f32[2,256,128]{2,1,0:T(8,128)} %refs_7_.1) | copy-start | bytes 786436
  0.7 72.1 %copy-start.9 = (f32[128,256]{1,0:T(8,128)S(1)}, f32[128,256]{1,0:T(8,128)}, u32[]{:S(2)}) copy-start(f32[128,256]{1,0:T(8,128)} %refs_2_.1) | copy-start | bytes 393220
  0.7 72.1 %copy-start.8 = (f32[128,256]{1,0:T(8,128)S(1)}, f32[128,256]{1,0:T(8,128)}, u32[]{:S(2)}) copy-start(f32[128,256]{1,0:T(8,128)} %refs_1_.1) | copy-start | bytes 393220
  0.7 72.1 %copy-start.13 = (f32[3,256]{1,0:T(4,128)S(1)}, f32[3,256]{1,0:T(4,128)}, u32[]{:S(2)}) copy-start(f32[3,256]{1,0:T(4,128)} %refs_3_.1) | copy-start | bytes 9220
  0.7 72.1 %copy-start.14 = (f32[6,256]{1,0:T(8,128)S(1)}, f32[6,256]{1,0:T(8,128)}, u32[]{:S(2)}) copy-start(f32[6,256]{1,0:T(8,128)} %refs_10_.1) | copy-start | bytes 18436
  0.7 72.1 %copy-start.15 = (f32[6,256]{1,0:T(8,128)S(1)}, f32[6,256]{1,0:T(8,128)}, u32[]{:S(2)}) copy-start(f32[6,256]{1,0:T(8,128)} %refs_11_.1) | copy-start | bytes 18436
  0.8 72.1 %copy-start.16 = (f32[3,256]{1,0:T(4,128)S(1)}, f32[3,256]{1,0:T(4,128)}, u32[]{:S(2)}) copy-start(f32[3,256]{1,0:T(4,128)} %refs_4_.1) | copy-start | bytes 9220
  0.8 72.1 %copy-start.17 = (f32[3,256]{1,0:T(4,128)S(1)}, f32[3,256]{1,0:T(4,128)}, u32[]{:S(2)}) copy-start(f32[3,256]{1,0:T(4,128)} %refs_5_.1) | copy-start | bytes 9220
  0.8 72.1 %copy-start.20 = (f32[2,128]{1,0:T(2,128)S(1)}, f32[2,128]{1,0:T(2,128)}, u32[]{:S(2)}) copy-start(f32[2,128]{1,0:T(2,128)} %refs_13_.1) | copy-start | bytes 3076
  0.8 72.1 %copy-start.21 = (f32[2,128]{1,0:T(2,128)S(1)}, f32[2,128]{1,0:T(2,128)}, u32[]{:S(2)}) copy-start(f32[2,128]{1,0:T(2,128)} %refs_14_.1) | copy-start | bytes 3076
  0.8 72.1 %copy-start.22 = (f32[2]{0:T(128)S(1)}, f32[2]{0:T(128)}, u32[]{:S(2)}) copy-start(f32[2]{0:T(128)} %refs_16_.1) | copy-start | bytes 28
  0.8 72.1 %copy-start.23 = (f32[2]{0:T(128)S(1)}, f32[2]{0:T(128)}, u32[]{:S(2)}) copy-start(f32[2]{0:T(128)} %refs_17_.1) | copy-start | bytes 28
  72.7 0.7 copy-start.11
  72.8 0.7 copy-start.18
  72.8 0.7 copy-start.19
  73.5 1.2 %copy-start.1 = (f32[2048,128]{1,0:T(8,128)S(1)}, f32[2048,128]{1,0:T(8,128)}, u32[]{:S(2)}) copy-start(f32[2048,128]{1,0:T(8,128)} %get-tuple-element.52.input_in) | copy-start | bytes 3145732
  74.7 1.0 %copy-start.3 = (bf16[2048,128]{1,0:T(8,128)(2,1)S(1)}, bf16[2048,128]{1,0:T(8,128)(2,1)}, u32[]{:S(2)}) copy-start(bf16[2048,128]{1,0:T(8,128)(2,1)} %get-tuple-element.50.block_in) | copy-start | bytes 1572868
  75.7 1.0 %copy-start.4 = (bf16[2048,128]{1,0:T(8,128)(2,1)S(1)}, bf16[2048,128]{1,0:T(8,128)(2,1)}, u32[]{:S(2)}) copy-start(bf16[2048,128]{1,0:T(8,128)(2,1)} %get-tuple-element.51.skip_in) | copy-start | bytes 1572868
  76.8 0.9 %copy-start.7 = (f32[2,256,128]{2,1,0:T(8,128)S(1)}, f32[2,256,128]{2,1,0:T(8,128)}, u32[]{:S(2)}) copy-start(f32[2,256,128]{2,1,0:T(8,128)} %get-tuple-element.54.project_grad) | copy-start | bytes 786436
  77.7 0.9 %copy-start.10 = (f32[128,256]{1,0:T(8,128)S(1)}, f32[128,256]{1,0:T(8,128)}, u32[]{:S(2)}) copy-start(f32[128,256]{1,0:T(8,128)} %get-tuple-element.53.expand_grad) | copy-start | bytes 393220
  78.6 0.7 copy-start.12

commit v2 on v1

--- a/solution.py
+++ b/solution.py
@@ -58,6 +58,13 @@
     return jnp.broadcast_to(jnp.sum(v, axis=1, keepdims=True), (v.shape[0], LANES))
 
 
+def spots_of(item_pad):
+    names = ("sum", "spread", "mean", "crossed")
+    if 4 * item_pad <= LANES:
+        return 2, {**{n: (0, k * item_pad) for k, n in enumerate(names)}, "q": (1, 2 * item_pad)}
+    return 5, {n: (k, 0) for k, n in enumerate(names + ("q",))}
+
+
 def fold_rows(v):
     return jnp.sum(v.reshape(v.shape[0] // 8, 8, v.shape[1]), axis=0)
 
@@ -66,22 +73,29 @@
     tm_size,
     item_count,
     item_pad,
+    len_hbm,
+    slope_hbm,
+    frames_hbm,
+    out_cot_hbm,
+    skip_cot_hbm,
+    expand_hbm,
+    project_hbm,
+    taps_hbm,
+    vectors_hbm,
+    biases_hbm,
+    block_out,
+    skip_out,
+    input_out,
+    expand_grad_ref,
+    project_grad_ref,
+    small_grad_ref,
     len_ref,
     slope_ref,
-    frames_ref,
-    out_cot_ref,
-    skip_cot_ref,
     expand_ref,
     project_ref,
     taps_ref,
     vectors_ref,
     biases_ref,
-    block_ref,
-    skip_ref,
-    input_grad_ref,
-    expand_grad_ref,
-    project_grad_ref,
-    small_grad_ref,
     x,
     cots,
     w_expand,
@@ -102,9 +116,6 @@
     hidden_grad,
     seg,
     column,
-    block_out,
-    skip_out,
-    input_out,
     tile_one,
     tile_two,
     tile_three,
@@ -113,6 +124,8 @@
     stats_three,
     project_part,
     expand_part,
+    project_pair,
+    expand_pair,
     project_in,
     expand_in,
     small_part,
@@ -120,15 +133,15 @@
     late_part,
     late_in,
     project_sum,
-    expand_sum,
     small_sum,
-    late_sum,
     square_part,
-    square_in,
+    last_part,
+    last_in,
     local_sem,
-    out_sem,
     send_sem,
     recv_sem,
+    near_send,
+    near_recv,
 ):
     frames = block_out.shape[0]
     wide = x.shape[0]
@@ -159,14 +172,50 @@
     def wait_bytes(ref, sem):
         pltpu.make_async_copy(ref, ref, sem).wait()
 
+    pending = {}
+
+    def settle(*keys):
+        for key in keys:
+            pending.pop(key)()
+
+    def started(copy, name, sends=None, receives=None):
+        def maybe(condition, body):
+            if condition is None:
+                body()
+            else:
+                pl.when(condition)(body)
+
+        maybe(sends, copy.start)
+        pending[name, "sent"] = lambda: maybe(sends, copy.wait_send)
+        pending[name, "here"] = lambda: maybe(receives, copy.wait_recv)
+
     own = pl.ds(HALO, frames)
-    loads = [
-        pltpu.make_async_copy(frames_ref, x.at[own, :], local_sem.at[0]),
-        pltpu.make_async_copy(out_cot_ref, cots.at[own, pl.ds(0, LANES)], local_sem.at[1]),
-        pltpu.make_async_copy(skip_cot_ref, cots.at[own, pl.ds(LANES, LANES)], local_sem.at[2]),
-    ]
-    for load in loads:
+    loads = {
+        "expand": (expand_hbm, expand_ref),
+        "frames": (frames_hbm, x.at[own, :]),
+        "vectors": (vectors_hbm, vectors_ref),
+        "taps": (taps_hbm, taps_ref),
+        "lengths": (len_hbm, len_ref),
+        "slopes": (slope_hbm, slope_ref),
+        "project": (project_hbm, project_ref),
+        "out": (out_cot_hbm, cots.at[own, pl.ds(0, LANES)]),
+        "skip": (skip_cot_hbm, cots.at[own, pl.ds(LANES, LANES)]),
+        "biases": (biases_hbm, biases_ref),
+    }
+    for k, (name, (src, dst)) in enumerate(loads.items()):
+        load = pltpu.make_async_copy(src, dst, local_sem.at[k])
         load.start()
+        pending["load", name] = load.wait
+
+    def loaded(*names):
+        settle(*[("load", name) for name in names])
+
+    for r in (0, HALO + frames):
+        x[r : r + HALO, :] = jnp.zeros((HALO, x.shape[1]), BF16)
+    for r in (HALO - DILATION, HALO + frames):
+        cots[r : r + DILATION, :] = jnp.zeros((DILATION, cots.shape[1]), BF16)
+    for stats in (stats_one, stats_two, stats_three):
+        stats[...] = jnp.zeros_like(stats)
 
     barrier = pltpu.get_barrier_semaphore()
 
@@ -179,12 +228,44 @@
     lax.fori_loop(1, devices, greet, 0)
 
     my_half = pl.ds(pl.multiple_of(chan * half, half), half)
+    loaded("expand", "vectors", "taps")
     w_expand[:, my_half] = expand_ref[...].astype(BF16)
-    w_project[my_half, 0:LANES] = project_ref[0].astype(BF16)
-    w_project[my_half, LANES : 2 * LANES] = project_ref[1].astype(BF16)
     params[0:6, my_half] = vectors_ref[...]
     params[6:9, my_half] = taps_ref[...]
     params[9:16, my_half] = jnp.zeros((7, half), F32)
+    loaded("frames")
+    pl.semaphore_wait(barrier, devices - 1)
+
+    partner = device(tm * 2 + other)
+    left, right = device(me - 1), device(me + 1)
+    has_left, has_right = me > 0, me < devices - 1
+
+    def to_left(ref, count, name):
+        copy = remote(
+            ref.at[pl.ds(HALO, count), :], ref.at[pl.ds(HALO + frames, count), :], name, left
+        )
+        started(copy, name, has_left, has_right)
+
+    def to_right(ref, count, name):
+        copy = remote(
+            ref.at[pl.ds(HALO + frames - count, count), :],
+            ref.at[pl.ds(HALO - count, count), :],
+            name,
+            right,
+        )
+        started(copy, name, has_right, has_left)
+
+    started(remote(w_expand.at[:, my_half], w_expand.at[:, my_half], 0, partner), 0)
+    started(remote(params.at[:, my_half], params.at[:, my_half], 1, partner), 1)
+    to_left(x, HALO, 2)
+    to_right(x, HALO, 3)
+    loaded("project", "out", "skip")
+    w_project[my_half, 0:LANES] = project_ref[0].astype(BF16)
+    w_project[my_half, LANES : 2 * LANES] = project_ref[1].astype(BF16)
+    started(remote(w_project.at[my_half, :], w_project.at[my_half, :], 4, partner), 4)
+    to_left(cots, DILATION, 5)
+    to_right(cots, DILATION, 6)
+    loaded("lengths", "slopes", "biases")
 
     width = table.shape[0]
     lane = lax.broadcasted_iota(jnp.int32, (8, width), 1)
@@ -217,9 +298,21 @@
 
     my_count = count_of(me)
     my_safe = jnp.maximum(my_count, 1.0)
-    offsets = [o for o in range(-spans, spans + 1) if o != 0]
+    offsets = [sign * o for o in range(spans, 0, -1) for sign in (1, -1)]
+    spots = spots_of(item_pad)[1]
+    tile_lane = lax.broadcasted_iota(jnp.int32, (item_pad, LANES), 1)
+
+    def packed(v, name):
+        chosen = tile_lane == spots[name][1] + row_item
+        return jnp.sum(jnp.where(chosen, v, 0.0), axis=0, keepdims=True)
+
+    def unpacked(row, name):
+        chosen = tile_lane == spots[name][1] + row_item
+        return spread_lanes(jnp.where(chosen, jnp.broadcast_to(row, chosen.shape), 0.0))
+
+    counts[len(offsets)] = packed(my_count, "mean")
     for slot, offset in enumerate(offsets):
-        counts[slot] = count_of(lax.rem(me - offset + devices, devices))
+        counts[slot] = packed(count_of(me - offset), "mean")
     column[...] = jnp.zeros_like(column)
 
     def put_table(place, v):
@@ -238,20 +331,23 @@
     def part(values, k, n, b):
         return values[k : k + n, b * LANES : (b + 1) * LANES]
 
-    def put_seg(r, n, place, v):
+    def put_seg(r, n, place, v, exact=True):
         high = v.astype(BF16)
-        seg[pl.ds(r, n), pl.ds(2 * place * LANES, LANES)] = high
-        seg[pl.ds(r, n), pl.ds((2 * place + 1) * LANES, LANES)] = (v - high.astype(F32)).astype(BF16)
-
-    def item_sums(count):
-        sums = dot(item_cols[...], seg[:, 0 : 2 * count * LANES])
-        return [
-            spread_lanes(
-                sums[:, 2 * k * LANES : (2 * k + 1) * LANES]
-                + sums[:, (2 * k + 1) * LANES : (2 * k + 2) * LANES]
-            )
-            for k in range(count)
-        ]
+        seg[pl.ds(r, n), pl.ds(place * LANES, LANES)] = high
+        if exact:
+            low = (v - high.astype(F32)).astype(BF16)
+            seg[pl.ds(r, n), pl.ds((place + 1) * LANES, LANES)] = low
+
+    def item_sums(first, widths):
+        sums = dot(item_cols[...], seg[:, first * LANES : (first + sum(widths)) * LANES])
+        results, k = [], 0
+        for n in widths:
+            v = sums[:, k * LANES : (k + 1) * LANES]
+            if n == 2:
+                v = v + sums[:, (k + 1) * LANES : (k + 2) * LANES]
+            results.append(spread_lanes(v))
+            k += n
+        return results
 
     def loop(start, size, count, body, rep=1):
         def step(i, carry):
@@ -291,36 +387,6 @@
         inside = (position >= row_start) & (position < row_end)
         item_cols[:, i * LANES : (i + 1) * LANES] = inside.astype(F32).astype(BF16)
 
-    loads[0].wait()
-    pl.semaphore_wait(barrier, devices - 1)
-
-    partner = device(tm * 2 + other)
-    left, right = device(lax.rem(me + devices - 1, devices)), device(lax.rem(me + 1, devices))
-    sends = [
-        remote(w_expand.at[:, my_half], w_expand.at[:, my_half], 0, partner),
-        remote(params.at[:, my_half], params.at[:, my_half], 1, partner),
-        remote(x.at[pl.ds(HALO, HALO), :], x.at[pl.ds(HALO + frames, HALO), :], 2, left),
-        remote(x.at[pl.ds(frames, HALO), :], x.at[pl.ds(0, HALO), :], 3, right),
-        remote(w_project.at[my_half, :], w_project.at[my_half, :], 4, partner),
-    ]
-    for send in sends:
-        send.start()
-    loads[1].wait()
-    loads[2].wait()
-    edges = [
-        remote(
-            cots.at[pl.ds(HALO, DILATION), :], cots.at[pl.ds(HALO + frames, DILATION), :], 5, left
-        ),
-        remote(
-            cots.at[pl.ds(HALO + frames - DILATION, DILATION), :],
-            cots.at[pl.ds(HALO - DILATION, DILATION), :],
-            6,
-            right,
-        ),
-    ]
-    for send in edges:
-        send.start()
-
     slope_one, slope_two = slope_ref[0], slope_ref[1]
 
     def lanes_of(which, b):
@@ -346,11 +412,10 @@
                 total = total + a
             put_seg(at(r, k, HALO), ROWS, 0, total)
 
-    (total,) = item_sums(1)
+    (total,) = item_sums(0, (2,))
     shift = total / jnp.maximum(my_count * 0.5, 1.0)
     put_table(0, shift)
-    for k in range(4):
-        sends[k].wait_recv()
+    settle(*[(k, "here") for k in range(4)])
 
     @own_loop()
     def _(r):
@@ -371,18 +436,15 @@
                 total = total + d
                 squares = squares + d * d
             put_seg(at(r, k, HALO), ROWS, 0, total)
-            put_seg(at(r, k, HALO), ROWS, 1, squares)
-
-    tile_lane = lax.broadcasted_iota(jnp.int32, (item_pad, LANES), 1)
-
-    def pack_tile(values):
-        tile = jnp.zeros((item_pad, LANES), F32)
-        for k, v in enumerate(values):
-            tile = jnp.where(tile_lane == k, v, tile)
-        return tile
-
-    def lane_of(tile, k):
-        return spread_lanes(jnp.where(tile_lane == k, tile, 0.0))
+            put_seg(at(r, k, HALO), ROWS, 2, squares)
+
+    def pack_tile(tile, values):
+        for r in range(tile.shape[0]):
+            row = jnp.zeros((1, LANES), F32)
+            for name, v in values.items():
+                if spots[name][0] == r:
+                    row = row + packed(v, name)
+            tile[r : r + 1, :] = row
 
     def local_moments(shift, total, squares):
         mean = shift + total / my_safe
@@ -390,31 +452,48 @@
         return mean, spread
 
     def exchange(tile, stats, phase):
-        for slot, offset in enumerate(offsets):
-            target = device(lax.rem(me + offset + devices, devices))
-            remote(tile, stats.at[slot], phase, target).start()
-
-    def arrived(stats, phase):
-        wait_bytes(stats, recv_sem.at[phase])
+        def near(slot, offset):
+            return pltpu.make_async_remote_copy(
+                src_ref=tile,
+                dst_ref=stats.at[slot],
+                send_sem=near_send.at[phase, slot],
+                recv_sem=near_recv.at[phase, slot],
+                device_id=device(me + offset),
+                device_id_type=MESH,
+            )
+
+        def all_near(source, act):
+            for slot, offset in enumerate(offsets):
+                index = me - offset if source else me + offset
+                pl.when((index >= 0) & (index < devices))(lambda: act(near(slot, offset)))
+
+        all_near(False, lambda copy: copy.start())
+        pending["near", phase, "sent"] = lambda: all_near(False, lambda copy: copy.wait_send())
+        pending["near", phase, "here"] = lambda: all_near(True, lambda copy: copy.wait_recv())
+
+    def rows_with(name, tile, stats):
+        r = spots[name][0]
+        return [stats[slot, r : r + 1, :] for slot in range(len(offsets))] + [tile[r : r + 1, :]]
+
+    def sum_of(name, tile, stats):
+        total = None
+        for row in rows_with(name, tile, stats):
+            total = row if total is None else total + row
+        return unpacked(total, name)
 
     def combined(tile, stats):
-        tiles = [tile[...]] + [stats[slot] for slot in range(len(offsets))]
-        sizes = [my_count] + [counts[slot] for slot in range(len(offsets))]
-        plain = tiles[0]
-        for t in tiles[1:]:
-            plain = plain + t
-        mean = lane_of(plain, 0) / elements
-        between = jnp.zeros((item_pad, LANES), F32)
-        for t, size in zip(tiles, sizes):
-            gap = t - mean
-            between = between + size * gap * gap
-        spread = (lane_of(plain, 1) + lane_of(between, 2)) / elements
-        return tiles, plain, mean, lax.rsqrt(spread + norm_eps)
-
-    total, squares = item_sums(2)
+        mean = sum_of("sum", tile, stats) / elements
+        centre = packed(mean, "mean")
+        between = jnp.zeros((1, LANES), F32)
+        for k, row in enumerate(rows_with("mean", tile, stats)):
+            between = between + counts[k] * (row - centre) * (row - centre)
+        spread = (sum_of("spread", tile, stats) + unpacked(between, "mean")) / elements
+        return mean, centre, lax.rsqrt(spread + norm_eps)
+
+    total, squares = item_sums(0, (2, 2))
     mean, spread = local_moments(shift, total, squares)
-    tile_one[...] = pack_tile([mean * my_count, spread, mean])
-    exchange(tile_one, stats_one, 7)
+    pack_tile(tile_one, {"sum": mean * my_count, "spread": spread, "mean": mean})
+    exchange(tile_one, stats_one, 0)
 
     for r in (0, HALO + frames):
         for which in (chan, other):
@@ -422,9 +501,7 @@
             for b in range(blocks // 2):
                 act_one[pl.ds(r, HALO), lanes_of(which, b)] = activate(product, 0, HALO, which, b)
 
-    sends[4].wait_recv()
-    for send in edges:
-        send.wait_recv()
+    settle(*[(k, "here") for k in (4, 5, 6)])
 
     def lanes(b):
         return pl.ds(b * LANES, LANES)
@@ -440,7 +517,7 @@
                     total = total + params[4:5, lanes(b)] * y
                     column[SHIFT_TWO, :, lanes(b)] += fold_rows(y)
             if add:
-                put_seg(at(r, k, HALO), size, 2, total)
+                put_seg(at(r, k, HALO), size, 4, total)
 
     @own_loop()
     def _(r):
@@ -449,9 +526,10 @@
     for r in (HALO - DILATION, HALO + frames):
         mixed_rows(r, DILATION, DILATION, False)
     bias_sum = dot(jnp.ones((16, frames), BF16), cots[own, :])[0:1]
-
-    arrived(stats_one, 7)
-    _, _, mean_one, scale_one = combined(tile_one, stats_one)
+    (q_sum,) = item_sums(4, (2,))
+
+    settle(("near", 0, "here"))
+    mean_one, _, scale_one = combined(tile_one, stats_one)
     put_table(0, mean_one)
     put_table(1, scale_one)
 
@@ -485,7 +563,7 @@
             act_two[pl.ds(at(r, k), ROWS), lanes(0)] = a
             put_seg(at(r, k, HALO), ROWS, 0, a)
 
-    (total,) = item_sums(1)
+    (total,) = item_sums(0, (2,))
     shift = total / jnp.maximum(my_count * (1.0 / blocks), 1.0)
     put_table(0, shift)
 
@@ -509,27 +587,29 @@
                 squares = squares + d * d
                 crossed = crossed + params[4:5, lanes(b)] * mixed_grad[rows, lanes(b)] * d
             put_seg(at(r, k, HALO), ROWS, 0, total)
-            put_seg(at(r, k, HALO), ROWS, 1, squares)
-            put_seg(at(r, k, HALO), ROWS, 3, crossed)
-
-    total, squares, q_sum, crossed = item_sums(4)
+            put_seg(at(r, k, HALO), ROWS, 2, squares, exact=False)
+            put_seg(at(r, k, HALO), ROWS, 3, crossed, exact=False)
+
+    total, squares, crossed = item_sums(0, (2, 1, 1))
     mean, spread = local_moments(shift, total, squares)
     crossed = crossed - (mean - shift) * q_sum
-    tile_two[...] = pack_tile([mean * my_count, spread, mean, q_sum, crossed])
-    exchange(tile_two, stats_two, 8)
+    values = {"sum": mean * my_count, "spread": spread, "mean": mean, "crossed": crossed, "q": q_sum}
+    pack_tile(tile_two, values)
+    exchange(tile_two, stats_two, 1)
 
     for r in (HALO - DILATION, HALO + frames):
         for b in range(blocks):
             act_two[pl.ds(r, DILATION), lanes(b)] = depth_rows(r, DILATION, b)
 
-    arrived(stats_two, 8)
-    tiles, plain, mean_two, scale_two = combined(tile_two, stats_two)
-    cross_sum = lane_of(plain, 4)
-    for t in tiles:
-        cross_sum = cross_sum + (lane_of(t, 2) - mean_two) * lane_of(t, 3)
+    settle(("near", 1, "here"))
+    mean_two, centre, scale_two = combined(tile_two, stats_two)
+    between = jnp.zeros((1, LANES), F32)
+    for row, q_row in zip(rows_with("mean", tile_two, stats_two), rows_with("q", tile_two, stats_two)):
+        between = between + (row - centre) * q_row
+    cross_sum = sum_of("crossed", tile_two, stats_two) + unpacked(between, "mean")
     put_table(0, mean_two)
     put_table(1, scale_two)
-    put_table(2, scale_two * lane_of(plain, 3) / elements)
+    put_table(2, scale_two * sum_of("q", tile_two, stats_two) / elements)
     put_table(3, scale_two * scale_two * cross_sum / elements)
 
     def second_back(r, n, size, add):
@@ -586,29 +666,11 @@
                 total = total + q
                 crossed = crossed + q * xhat
             put_seg(at(r, k, HALO), ROWS, 0, total)
-            put_seg(at(r, k, HALO), ROWS, 1, crossed)
-
-    total, crossed = item_sums(2)
-    tile_three[...] = pack_tile([total, crossed])
-    exchange(tile_three, stats_three, 9)
-
-    @own_loop()
-    def _(r):
-        product = dot(mixed[pl.ds(at(r, 0, HALO), BLOCK), :], w_project[...])
-        for k in range(0, BLOCK, ROWS):
-            rows = pl.ds(at(r, k, HALO), ROWS)
-            inputs = x[pl.ds(at(r, k), ROWS), :].astype(F32)
-            block_out[rows, :] = (
-                inputs + part(product, k, ROWS, 0) + biases_ref[0:1, :]
-            ).astype(BF16)
-            skip_out[rows, :] = (part(product, k, ROWS, 1) + biases_ref[1:2, :]).astype(BF16)
-
-    stores = [
-        pltpu.make_async_copy(block_out, block_ref, out_sem.at[0]),
-        pltpu.make_async_copy(skip_out, skip_ref, out_sem.at[1]),
-    ]
-    for store in stores:
-        store.start()
+            put_seg(at(r, k, HALO), ROWS, 2, crossed)
+
+    total, crossed = item_sums(0, (2, 2))
+    pack_tile(tile_three, {"sum": total, "crossed": crossed})
+    exchange(tile_three, stats_three, 2)
 
     step = 512
     total = jnp.zeros((2 * LANES, hidden), F32)
@@ -617,6 +679,12 @@
             cots[pl.ds(HALO + k * step, step), :], mixed[pl.ds(k * step, step), :]
         )
     project_part[...] = total
+
+    core = lax.rem(tm, 2)
+    sibling = {"chan": chan, "tm": tm + 1 - 2 * core}
+    mine = pl.ds(pl.multiple_of(core * LANES, LANES), LANES)
+    yours = pl.ds(pl.multiple_of((1 - core) * LANES, LANES), LANES)
+    started(remote(project_part.at[yours, :], project_pair, 7, sibling), 7)
 
     def column_sum(which):
         return jnp.sum(column[which], axis=0, keepdims=True)
@@ -640,62 +708,99 @@
         small_part[c, BIAS_ROW : BIAS_ROW + 1, :] = bias_sum
         small_part[c, SLOPE_TWO_ROW : SLOPE_TWO_ROW + 1, :] = slope_two_row
 
+    chips = tm_size // 2
+    chip = lax.div(tm, 2)
+    mates = 2 * chips
+    mate = chip * 2 + chan
+    spot = lax.div(chip, stride)
     reducers = 2 * PIECES
-    piece = lax.div(tm, stride)
-    place = piece * 2 + chan
+    place = (spot * 2 + core) * 2 + chan
+    is_reducer = lax.rem(chip, stride) == 0
 
     def when_reducer(body):
         if stride == 1:
             body()
         else:
-            pl.when(lax.rem(tm, stride) == 0)(body)
-
-    def reducer_device(q):
-        return lax.rem(q, 2), lax.div(q, 2) * stride
-
-    def to_reducers(send):
+            pl.when(is_reducer)(body)
+
+    def by_role(body, count):
+        if stride == 1:
+            body(count - 1)
+        else:
+            pl.when(is_reducer)(lambda: body(count - 1))
+            pl.when(jnp.logical_not(is_reducer))(lambda: body(count))
+
+    def to_reducers(source, ref, phase):
         def one(k, carry):
-            q = lax.rem(place + k, reducers)
-            c, t = reducer_device(q)
+            q = lax.rem(spot * 2 + chan + k, PIECES)
+            c, at_spot = lax.rem(q, 2), lax.div(q, 2)
+            target = {"chan": c, "tm": at_spot * stride * 2 + core}
+
+            def send():
+                remote(source(c, at_spot), ref.at[mate], phase, target).start()
+
             if stride == 1:
-                send(q, {"chan": c, "tm": t})
+                send()
             else:
-
-                @pl.when(t * 2 + c != me)
-                def _():
-                    send(q, {"chan": c, "tm": t})
-
+                pl.when(at_spot * stride * 2 + c != mate)(send)
             return carry
 
-        lax.fori_loop(1 if stride == 1 else 0, reducers, one, 0)
-
-    def project_piece(q):
-        rows = pl.ds(pl.multiple_of(lax.div(q, 2) * 16, 16), 16)
-        return rows, pl.ds(pl.multiple_of(lax.rem(q, 2) * half, half), half)
-
-    def expand_piece(q):
-        j, c = lax.div(q, 2), lax.rem(q, 2)
-        rows = pl.ds(pl.multiple_of(lax.div(j, 2) * 16, 16), 16)
-        at = c * half + lax.rem(j, 2) * LANES
-        return rows, pl.ds(pl.multiple_of(at, LANES), LANES)
-
-    def send_project(q, target):
-        rows, cols = project_piece(q)
-        remote(project_part.at[rows, cols], project_in.at[me], 10, target).start()
-
-    to_reducers(send_project)
-    for c in range(2):
-
-        @pl.when((tm != 0) | (chan != c))
-        def _(c=c):
-            remote(small_part.at[c], small_in.at[me], 11, {"chan": c, "tm": 0}).start()
-
-    arrived(stats_three, 9)
-    plain = tile_three[...]
-    for slot in range(len(offsets)):
-        plain = plain + stats_three[slot]
-    put_table(0, lane_of(plain, 0) / elements)
-    put_table(1, lane_of(plain, 1) / elements)
+        lax.fori_loop(1 if stride == 1 else 0, PIECES, one, 0)
+        pending[phase, "sent"] = lambda: by_role(
+            lambda n: wait_bytes(ref.at[pl.ds(0, n)], send_sem.at[phase]), PIECES
+        )
+        pending[phase, "here"] = lambda: when_reducer(
+            lambda: wait_bytes(ref.at[pl.ds(0, mates - 1)], recv_sem.at[phase])
+        )
+
+    def piece_rows(at_spot):
+        return pl.ds(pl.multiple_of(at_spot * 16, 16), 16)
+
+    def project_piece(c, at_spot):
+        return project_pair.at[piece_rows(at_spot), pl.ds(pl.multiple_of(c * half, half), half)]
+
+    def expand_piece(c, at_spot):
+        return expand_pair.at[c, piece_rows(at_spot), :]
+
+    first_of_group = tm == 0
+
+    def to_first(parts, ref, phase):
+        for c in range(2):
+
+            @pl.when((tm != 0) | (chan != c))
+            def _(c=c):
+                remote(parts.at[c], ref.at[me], phase, {"chan": c, "tm": 0}).start()
+
+        def sent():
+            pl.when(first_of_group)(lambda: wait_bytes(ref.at[0], send_sem.at[phase]))
+            pl.when(jnp.logical_not(first_of_group))(
+                lambda: wait_bytes(ref.at[pl.ds(0, 2)], send_sem.at[phase])
+            )
+
+        pending[phase, "sent"] = sent
+        pending[phase, "here"] = lambda: pl.when(first_of_group)(
+            lambda: wait_bytes(ref.at[pl.ds(0, devices - 1)], recv_sem.at[phase])
+        )
+
+    to_first(small_part, small_in, 11)
+    settle((7, "here"))
+    project_pair[...] += project_part[mine, :]
+    to_reducers(project_piece, project_in, 10)
+
+    @own_loop()
+    def _(r):
+        product = dot(mixed[pl.ds(at(r, 0, HALO), BLOCK), :], w_project[...])
+        for k in range(0, BLOCK, ROWS):
+            rows = pl.ds(at(r, k, HALO), ROWS)
+            inputs = x[pl.ds(at(r, k), ROWS), :].astype(F32)
+            block_out[rows, :] = (
+                inputs + part(product, k, ROWS, 0) + biases_ref[0:1, :]
+            ).astype(BF16)
+            skip_out[rows, :] = (part(product, k, ROWS, 1) + biases_ref[1:2, :]).astype(BF16)
+
+    settle(("near", 2, "here"))
+    put_table(0, sum_of("sum", tile_three, stats_three) / elements)
+    put_table(1, sum_of("crossed", tile_three, stats_three) / elements)
     put_table(2, scale_one)
 
     @own_loop()
@@ -716,71 +821,83 @@
             x[pl.ds(HALO + k * step, step), :], hidden_grad[pl.ds(k * step, step), :]
         )
     expand_part[...] = total
+    for c in range(2):
+        source = pl.ds(pl.multiple_of(c * half + (1 - core) * LANES, LANES), LANES)
+        started(remote(expand_part.at[:, source], expand_pair.at[c], 8 + c, sibling), 8 + c)
     bias_one = dot(jnp.ones((16, frames), BF16), hidden_grad[...])[0:1]
     slope_row = column_sum(SLOPE_ONE)
     slope_row = (slope_row[:, 0:half] + slope_row[:, half:hidden]) / slope_one
     for c in range(2):
-        late_part[c] = jnp.zeros((8, half), F32)
         late_part[c, 0:1, :] = bias_one[:, c * half : (c + 1) * half]
         late_part[c, 1:2, :] = slope_row
-
-    def send_expand(q, target):
-        rows, cols = expand_piece(q)
-        remote(expand_part.at[rows, cols], expand_in.at[me], 12, target).start()
-
-    to_reducers(send_expand)
+    to_first(late_part, late_in, 13)
+    settle((8, "here"), (9, "here"))
     for c in range(2):
-
-        @pl.when((tm != 0) | (chan != c))
-        def _(c=c):
-            remote(late_part.at[c], late_in.at[me], 13, {"chan": c, "tm": 0}).start()
-
-    def to_group(send):
+        expand_pair[c] += expand_part[
+            :, pl.ds(pl.multiple_of(c * half + core * LANES, LANES), LANES)
+        ]
+    to_reducers(expand_piece, expand_in, 12)
+
+    def total_of(ref, count, rows, cols):
+        return lax.fori_loop(
+            0, count, lambda k, total: total + ref[k], jnp.zeros((rows, cols), F32)
+        )
+
+    def fold_lanes(v):
+        return v[:, 0:LANES] + v[:, LANES:half]
+
+    def to_group(src, dst, phase, targets):
         def one(k, carry):
-            send({"chan": chan, "tm": lax.rem(tm + k, tm_size)})
+            target = (
+                lax.rem(chip + k, chips) * 2 + core if targets == chips else lax.rem(tm + k, tm_size)
+            )
+            remote(src, dst, phase, {"chan": chan, "tm": target}).start()
             return carry
 
-        lax.fori_loop(1, tm_size, one, 0)
-
-    my_sum_rows = pl.ds(pl.multiple_of(piece * 16, 16), 16)
-
-    def sum_project():
-        rows, cols = project_piece(place)
-        wait_bytes(project_in.at[pl.ds(0, devices - 1)], recv_sem.at[10])
-        project_in[me] = project_part[rows, cols]
-
-        def add(k, total):
-            return total + project_in[k]
-
-        total = lax.fori_loop(0, devices, add, jnp.zeros((16, half), F32))
-        project_sum[my_sum_rows, :] = total
-        squares = jnp.sum(total * total, axis=0, keepdims=True)
-        square_part[...] = squares[:, 0:LANES] + squares[:, LANES:half]
-
-        def send(target):
-            remote(project_sum.at[my_sum_rows, :], project_sum.at[my_sum_rows, :], 14, target).start()
-
-        to_group(send)
-
-    when_reducer(sum_project)
-
-    @pl.when(tm == 0)
+        lax.fori_loop(1, targets, one, 0)
+
+    def group_sent(ref, phase, targets):
+        def one(k, carry):
+            wait_bytes(ref, send_sem.at[phase])
+            return carry
+
+        lax.fori_loop(1, targets, one, 0)
+
+    settle((10, "here"))
+    sum_rows = pl.ds(pl.multiple_of(core * LANES + spot * 16, 16), 16)
+
+    @when_reducer
     def _():
-        wait_bytes(small_in.at[pl.ds(0, devices - 1)], recv_sem.at[11])
+        project_in[mate] = project_piece(chan, spot)[...]
+        total = total_of(project_in, mates, 16, half)
+        project_sum[sum_rows, :] = total
+        square_part[...] = fold_lanes(jnp.sum(total * total, axis=0, keepdims=True))
+        to_group(project_sum.at[sum_rows, :], project_sum.at[sum_rows, :], 14, chips)
+
+    pending[14, "sent"] = lambda: when_reducer(
+        lambda: group_sent(project_sum.at[pl.ds(0, 16), :], 14, chips)
+    )
+    pending[14, "here"] = lambda: by_role(
+        lambda n: wait_bytes(project_sum.at[pl.ds(0, 16 * n), :], recv_sem.at[14]), PIECES // 2
+    )
+    settle((11, "here"))
+
+    @pl.when(first_of_group)
+    def _():
         small_in[me] = small_part[chan]
-
-        def add(k, total):
-            return total + small_in[k]
-
-        total = lax.fori_loop(0, devices, add, jnp.zeros((16, half), F32))
+        total = total_of(small_in, devices, 16, half)
         small_sum[...] = total
-        squares = jnp.sum((total * total)[0:BIAS_ROW], axis=0, keepdims=True)
-        square_part[...] += squares[:, 0:LANES] + squares[:, LANES:half]
-
-        def send(target):
-            remote(small_sum, small_sum, 15, target).start()
-
-        to_group(send)
+        square_part[...] += fold_lanes(
+            jnp.sum((total * total)[0:BIAS_ROW], axis=0, keepdims=True)
+        )
+        to_group(small_sum, small_sum, 15, tm_size)
+
+    pending[15, "sent"] = lambda: pl.when(first_of_group)(
+        lambda: group_sent(small_sum, 15, tm_size)
+    )
+    pending[15, "here"] = lambda: pl.when(jnp.logical_not(first_of_group))(
+        lambda: wait_bytes(small_sum, recv_sem.at[15])
+    )
 
     @own_loop()
     def _(r):
@@ -789,153 +906,73 @@
             above = cots[pl.ds(at(r, k), ROWS), 0:LANES].astype(F32)
             input_out[pl.ds(at(r, k, HALO), ROWS), :] = above + part(product, k, ROWS, 0)
 
-    stores.append(pltpu.make_async_copy(input_out, input_grad_ref, out_sem.at[2]))
-    stores[2].start()
-
-    def sum_piece(q):
-        j = lax.div(q, 2)
-        rows = pl.ds(pl.multiple_of(lax.div(j, 2) * 16, 16), 16)
-        return rows, pl.ds(pl.multiple_of(lax.rem(j, 2) * LANES, LANES), LANES)
-
-    @pl.when(tm == 0)
+    settle((13, "here"))
+    last_part[...] = jnp.zeros_like(last_part)
+
+    @pl.when(first_of_group)
     def _():
-        wait_bytes(late_in.at[pl.ds(0, devices - 1)], recv_sem.at[13])
         late_in[me] = late_part[chan]
-
-        def add(k, total):
-            return total + late_in[k]
-
-        total = lax.fori_loop(0, devices, add, jnp.zeros((8, half), F32))
-        late_sum[...] = total
+        total = total_of(late_in, devices, 2, half)
+        last_part[17:19, :] = total[:, 0:LANES]
+        last_part[19:21, :] = total[:, LANES:half]
         squares = (total * total)[0:1]
-        square_part[...] += squares[:, 0:LANES] + squares[:, LANES:half]
-
-        def send(target):
-            remote(late_sum, late_sum, 16, target).start()
-
-        to_group(send)
-
-    def sum_expand():
-        wait_bytes(expand_in.at[pl.ds(0, devices - 1)], recv_sem.at[12])
-        rows, cols = expand_piece(place)
-        expand_in[me] = expand_part[rows, cols]
-
-        def add(k, total):
-            return total + expand_in[k]
-
-        total = lax.fori_loop(0, devices, add, jnp.zeros((16, LANES), F32))
-        rows, cols = sum_piece(place)
-        expand_sum[rows, cols] = total
-        square_part[...] += jnp.sum(total * total, axis=0, keepdims=True)
-        square_in[place] = square_part[...]
-
-        def send(target):
-            remote(expand_sum.at[rows, cols], expand_sum.at[rows, cols], 17, target).start()
-
-        to_group(send)
-
-        def send_square(k, carry):
-            target = device(lax.rem(me + k, devices))
-            remote(square_part, square_in.at[place], 18, target).start()
+        square_part[...] += fold_lanes(squares)
+
+    settle((12, "here"))
+
+    @when_reducer
+    def _():
+        expand_in[mate] = expand_piece(chan, spot)[...]
+        total = total_of(expand_in, mates, 16, LANES)
+        last_part[0:16, :] = total
+        last_part[16:17, :] = square_part[...] + jnp.sum(total * total, axis=0, keepdims=True)
+        last_in[place] = last_part[...]
+        to_group(last_part, last_in.at[place], 17, tm_size)
+        tail = pl.ds(16, 8)
+
+        def send_tail(k, carry):
+            target = {"chan": other, "tm": lax.rem(tm + k, tm_size)}
+            remote(last_part.at[tail, :], last_in.at[place, tail, :], 18, target).start()
             return carry
 
-        lax.fori_loop(1, devices, send_square, 0)
-
-    when_reducer(sum_expand)
-
-    def wait_group(ref, phase, mine):
-        rows = ref.shape[0] // PIECES
-
-        def some(count):
-            wait_bytes(ref.at[pl.ds(0, count * rows)], recv_sem.at[phase])
-
-        if stride == 1:
-            some(PIECES - 1)
-        else:
-            is_reducer = lax.rem(tm, stride) == 0
-            pl.when(is_reducer)(lambda: some(PIECES - 1))
-            pl.when(jnp.logical_not(is_reducer))(lambda: some(PIECES))
-
-    wait_group(project_sum, 14, None)
+        lax.fori_loop(0, tm_size, send_tail, 0)
+
+    def tails(count, sem):
+        wait_bytes(last_in.at[pl.ds(0, count), pl.ds(16, 8), :], sem)
+
+    def tails_sent():
+        for _ in range(tm_size // PIECES):
+            tails(PIECES, send_sem.at[18])
+
+    pending[17, "sent"] = lambda: when_reducer(lambda: group_sent(last_part, 17, tm_size))
+    pending[17, "here"] = lambda: by_role(
+        lambda n: wait_bytes(last_in.at[pl.ds(0, n)], recv_sem.at[17]), PIECES
+    )
+    pending[18, "sent"] = lambda: when_reducer(tails_sent)
+    pending[18, "here"] = lambda: tails(PIECES, recv_sem.at[18])
+
+    settle((14, "here"))
+    started(remote(project_sum.at[mine, :], project_sum.at[mine, :], 16, sibling), 16)
+    settle((15, "here"), (16, "here"))
     for k in range(2):
         project_grad_ref[k] = project_sum[k * LANES : (k + 1) * LANES, :].T
-
-    @pl.when(tm != 0)
-    def _():
-        wait_bytes(small_sum, recv_sem.at[15])
-        wait_bytes(late_sum, recv_sem.at[16])
-
     small_grad_ref[...] = small_sum[...]
-    small_grad_ref[0:1, :] = late_sum[0:1, :]
-    small_grad_ref[SLOPE_ONE_ROW : SLOPE_ONE_ROW + 1, :] = late_sum[1:2, :]
-    wait_group(expand_sum, 17, None)
-    expand_grad_ref[...] = expand_sum[...]
-
-    def wait_squares(count):
-        wait_bytes(square_in.at[pl.ds(0, count)], recv_sem.at[18])
-
-    if stride == 1:
-        wait_squares(reducers - 1)
-    else:
-        is_reducer = lax.rem(tm, stride) == 0
-        pl.when(is_reducer)(lambda: wait_squares(reducers - 1))
-        pl.when(jnp.logical_not(is_reducer))(lambda: wait_squares(reducers))
-    total = square_in[0]
+    settle((17, "here"), (18, "here"))
+    for j in range(PIECES):
+        rows, lanes_here = slice(j // 2 * 16, j // 2 * 16 + 16), slice(j % 2 * LANES, (j % 2 + 1) * LANES)
+        expand_grad_ref[rows, lanes_here] = last_in[j * 2 + chan, 0:16, :]
+    for k in range(2):
+        where = slice(k * LANES, (k + 1) * LANES)
+        late = last_in[chan, 17 + 2 * k : 19 + 2 * k, :]
+        small_grad_ref[0:1, where] = late[0:1]
+        small_grad_ref[SLOPE_ONE_ROW : SLOPE_ONE_ROW + 1, where] = late[1:2]
+    total = last_in[0, 16:17, :]
     for q in range(1, reducers):
-        total = total + square_in[q]
+        total = total + last_in[q, 16:17, :]
     small_grad_ref[SQUARES_ROW : SQUARES_ROW + 1, 0:LANES] = total
     small_grad_ref[SQUARES_ROW : SQUARES_ROW + 1, LANES:half] = jnp.zeros((1, half - LANES), F32)
 
-    for send in sends + edges:
-        send.wait_send()
-    for phase, stats in ((7, stats_one), (8, stats_two), (9, stats_three)):
-        wait_bytes(stats, send_sem.at[phase])
-
-    def sent_to_reducers(ref, phase):
-        if stride == 1:
-            wait_bytes(ref.at[pl.ds(0, reducers - 1)], send_sem.at[phase])
-        else:
-            is_reducer = lax.rem(tm, stride) == 0
-            pl.when(is_reducer)(
-                lambda: wait_bytes(ref.at[pl.ds(0, reducers - 1)], send_sem.at[phase])
-            )
-            pl.when(jnp.logical_not(is_reducer))(
-                lambda: wait_bytes(ref.at[pl.ds(0, reducers)], send_sem.at[phase])
-            )
-
-    sent_to_reducers(project_in, 10)
-    sent_to_reducers(expand_in, 12)
-    for part, phase in ((small_in, 11), (late_in, 13)):
-        pl.when(tm == 0)(lambda: wait_bytes(part.at[0], send_sem.at[phase]))
-        pl.when(tm != 0)(lambda: wait_bytes(part.at[pl.ds(0, 2)], send_sem.at[phase]))
-
-    def group_bytes(ref, phase):
-        def one(k, carry):
-            wait_bytes(ref, send_sem.at[phase])
-            return carry
-
-        lax.fori_loop(1, tm_size, one, 0)
-
-    def sent_sums():
-        group_bytes(project_sum.at[pl.ds(0, 16), :], 14)
-        rows, cols = sum_piece(place)
-        group_bytes(expand_sum.at[rows, cols], 17)
-
-        def one(k, carry):
-            wait_bytes(square_part, send_sem.at[18])
-            return carry
-
-        lax.fori_loop(1, devices, one, 0)
-
-    when_reducer(sent_sums)
-
-    @pl.when(tm == 0)
-    def _():
-        group_bytes(small_sum, 15)
-        group_bytes(late_sum, 16)
-
-    for store in stores:
-        store.wait()
+    settle(*list(pending))
 
 
 def adam(weight, moment, square, gradient, scale, step_rate):
@@ -1040,13 +1077,18 @@
     devices = 2 * tm_size
     reducers = 2 * PIECES
     peers = 2 * (-(-LONGEST_ITEM // frames))
-    vmem, smem, anywhere = (
-        pl.BlockSpec(memory_space=pltpu.VMEM),
-        pl.BlockSpec(memory_space=pltpu.SMEM),
-        pl.BlockSpec(memory_space=pl.ANY),
+    tile_rows = spots_of(item_pad)[0]
+    vmem, smem, anywhere, hbm = (
+        pl.BlockSpec(memory_space=space)
+        for space in (pltpu.VMEM, pltpu.SMEM, pl.ANY, pltpu.HBM)
     )
     shape = jax.ShapeDtypeStruct
     scratch = [
+        ((inputs, half), F32),
+        ((2, half, inputs), F32),
+        ((3, half), F32),
+        ((6, half), F32),
+        ((2, inputs), F32),
         ((wide, inputs), BF16),
         ((wide, 2 * inputs), BF16),
         ((inputs, hidden), BF16),
@@ -1057,7 +1099,7 @@
         ((wide, LANES), F32),
         ((wide, LANES), F32),
         ((width, 4 * LANES), BF16),
-        ((peers, item_pad, LANES), F32),
+        ((peers + 1, 1, LANES), F32),
         ((wide, hidden), F32),
         ((wide, hidden), F32),
         ((wide, hidden), F32),
@@ -1067,29 +1109,27 @@
         ((frames, hidden), BF16),
         ((frames, 8 * LANES), BF16),
         ((COLUMN_SUMS, 8, hidden), F32),
-        ((frames, inputs), BF16),
-        ((frames, inputs), BF16),
-        ((frames, inputs), F32),
-        ((item_pad, LANES), F32),
-        ((item_pad, LANES), F32),
-        ((item_pad, LANES), F32),
-        ((peers, item_pad, LANES), F32),
-        ((peers, item_pad, LANES), F32),
-        ((peers, item_pad, LANES), F32),
+        ((tile_rows, LANES), F32),
+        ((tile_rows, LANES), F32),
+        ((tile_rows, LANES), F32),
+        ((peers, tile_rows, LANES), F32),
+        ((peers, tile_rows, LANES), F32),
+        ((peers, tile_rows, LANES), F32),
         ((2 * inputs, hidden), F32),
         ((inputs, hidden), F32),
-        ((devices, 16, half), F32),
-        ((devices, 16, LANES), F32),
+        ((inputs, hidden), F32),
+        ((2, inputs, LANES), F32),
+        ((tm_size, 16, half), F32),
+        ((tm_size, 16, LANES), F32),
         ((2, 16, half), F32),
         ((devices, 16, half), F32),
-        ((2, 8, half), F32),
-        ((devices, 8, half), F32),
+        ((2, 2, half), F32),
+        ((devices, 2, half), F32),
         ((2 * inputs, half), F32),
-        ((inputs, half), F32),
         ((16, half), F32),
-        ((8, half), F32),
         ((1, LANES), F32),
-        ((reducers, 1, LANES), F32),
+        ((24, LANES), F32),
+        ((reducers, 24, LANES), F32),
     ]
     block_raw, skip_raw, input_raw, expand_grad, project_grad, small_grad = pl.pallas_call(
         functools.partial(block_kernel, tm_size, items, item_pad),
@@ -1101,30 +1141,37 @@
             shape((2, half, inputs), F32),
             shape((16, half), F32),
         ],
-        in_specs=[smem, smem] + [anywhere] * 3 + [vmem] * 5,
-        out_specs=[anywhere] * 3 + [vmem] * 3,
-        scratch_shapes=[pltpu.VMEM(s, t) for s, t in scratch]
+        in_specs=[hbm] * 10,
+        out_specs=[vmem] * 6,
+        scratch_shapes=[pltpu.SMEM((items,), jnp.int32), pltpu.SMEM((2,), F32)]
+        + [pltpu.VMEM(s, t) for s, t in scratch]
         + [
-            pltpu.SemaphoreType.DMA((3,)),
-            pltpu.SemaphoreType.DMA((3,)),
+            pltpu.SemaphoreType.DMA((10,)),
             pltpu.SemaphoreType.DMA((19,)),
             pltpu.SemaphoreType.DMA((19,)),
+            pltpu.SemaphoreType.DMA((3, peers)),
+            pltpu.SemaphoreType.DMA((3, peers)),
         ],
         compiler_params=pltpu.CompilerParams(
-            collective_id=0, has_side_effects=True, vmem_limit_bytes=60 * 2**20
+            collective_id=0, has_side_effects=True, vmem_limit_bytes=52 * 2**20
         ),
         name="temporal_block",
     )(
-        item_lengths,
-        prelu_slopes,
-        frames_in,
-        out_cotangent,
-        skip_cotangent,
-        expand,
-        project,
-        depthwise,
-        channel_vectors,
-        output_biases,
+        *[
+            pltpu.with_memory_space_constraint(v, pltpu.HBM)
+            for v in (
+                item_lengths,
+                prelu_slopes,
+                frames_in,
+                out_cotangent,
+                skip_cotangent,
+                expand,
+                project,
+                depthwise,
+                channel_vectors,
+                output_biases,
+            )
+        ]
     )
     state = [
         expand,

time: 83.2 us -> 66.9 us (0.80)
  Pallas kernels: 75.3 us -> 63.9 us
  local copies, waits for them, and re-layouts: 6.47 us -> 1.82 us
    pallas_call x1, Pallas kernels: 71.9 us -> 60.5 us  [per_device(): pl.pallas_call(functools.partial(block_kernel, tm_size, items, item_pad),...]
    unnamed x48 -> x38, local copies, waits for them, and re-layouts: 6.47 us -> 1.82 us
where the time goes in v2:
time: 66.9 us; the launch traced here: 66.7 us
  Pallas kernels  63.9 us (96%)
  local copies, waits for them, and re-layouts  1.82 us (3%)
  between operations  0.94 us (1%)
    pallas_call x1, Pallas kernels, per_device(): pl.pallas_call(functools.partial(block_kernel, tm_size, items, item_pad),...  60.5 us
    pallas_call x1, Pallas kernels, per_device(): pl.pallas_call(adam_kernel, out_shape=[shape((frames, inputs), BF16), sha...  3.39 us
    unnamed x38, local copies, waits for them, and re-layouts  1.82 us

profile of v2, /device:TPU:0, one launch (start us, length us, event | category | flops | bytes accessed | tf_op | source)
XLA Modules:
  0.0 66.7 jit_solution(11387984312377981619)
XLA Ops:
  0.7 0.0 copy-start
  0.7 0.0 copy-start.2
  0.7 0.0 copy-start.4
  0.7 0.0 copy-start.3
  0.7 0.0 copy-start.6
  0.7 0.0 copy-start.5
  0.7 0.0 copy-start.8
  0.7 0.0 copy-start.9
  0.7 0.0 copy-start.10
  0.8 0.0 copy-start.11
  0.8 0.0 copy-start.12
  0.8 0.0 copy-start.15
  0.8 0.0 copy-start.16
  0.8 0.0 copy-start.17
  0.8 0.0 copy-start.18
  0.8 60.5 %temporal_block.1 = (bf16[2048,128]{1,0:T(8,128)(2,1)S(1)}, bf16[2048,128]{1,0:T(8,128)(2,1)S(1)}, f32[2048,128]{1,0:T(8,128)}, f32[128,256]{1,0:T(8,128)S(1)}, ...) custom-call(s32[16]{0:T(128)} %len_hbm.1, f32[2]{0:T(128)} %refs_15_.1, bf16[2048,128]{1,0:T(8,128)(2,1)} %frames_hbm.1, ...), custom_call_target="tpu_custom_call" | custom-call | tf_op jit(solution)/shard_map/temporal_block/pallas_call | solution.py:1134
  61.4 0.0 copy-start.7
  61.4 0.0 copy-start.13
  61.4 0.0 copy-start.14
  61.4 0.0 copy-done
  61.4 0.0 copy-done.2
  61.4 0.0 copy-done.4
  61.4 0.0 copy-done.3
  61.4 0.0 copy-done.6
  61.4 0.0 copy-done.5
  61.4 0.0 copy-done.8
  61.5 0.0 copy-done.9
  61.5 0.0 copy-done.10
  61.5 0.0 copy-done.11
  61.5 0.0 copy-done.12
  61.5 0.0 copy-done.15
  61.5 0.0 copy-done.16
  61.5 0.0 copy-done.17
  61.5 0.0 copy-done.18
  61.5 0.5 copy-done.7
  62.1 0.0 copy-done.13
  62.1 0.0 copy-done.14
  62.1 0.0 copy-start.1
  62.1 1.2 %copy-done.1 = f32[2048,128]{1,0:T(8,128)S(1)} copy-done((f32[2048,128]{1,0:T(8,128)S(1)}, f32[2048,128]{1,0:T(8,128)}, u32[]{:S(2)}) %copy-start.1) | copy-done | bytes 1048600
  63.3 3.4 %adam_step.1 = (bf16[2048,128]{1,0:T(8,128)(2,1)}, bf16[2048,128]{1,0:T(8,128)(2,1)}, f32[2048,128]{1,0:T(8,128)}, f32[1,1]{1,0:T(1,128)}, f32[128,256]{1,0:T(8,...) custom-call(bf16[2048,128]{1,0:T(8,128)(2,1)S(1)} %get-tuple-element, ...), custom_call_target="tpu_custom_call" | custom-call | tf_op jit(solution)/shard_map/adam_step/pallas_call | solution.py:1196
Async XLA Ops:
  0.7 60.7 %copy-start = (f32[2,256,128]{2,1,0:T(8,128)S(1)}, f32[2,256,128]{2,1,0:T(8,128)}, u32[]{:S(2)}) copy-start(f32[2,256,128]{2,1,0:T(8,128)} %refs_6_.1) | copy-start | bytes 786436
  0.7 60.7 %copy-start.2 = (f32[128,256]{1,0:T(8,128)S(1)}, f32[128,256]{1,0:T(8,128)}, u32[]{:S(2)}) copy-start(f32[128,256]{1,0:T(8,128)} %refs_0_.1) | copy-start | bytes 393220
  0.7 60.7 %copy-start.4 = (f32[2,256,128]{2,1,0:T(8,128)S(1)}, f32[2,256,128]{2,1,0:T(8,128)}, u32[]{:S(2)}) copy-start(f32[2,256,128]{2,1,0:T(8,128)} %refs_8_.1) | copy-start | bytes 786436
  0.7 60.7 %copy-start.3 = (f32[2,256,128]{2,1,0:T(8,128)S(1)}, f32[2,256,128]{2,1,0:T(8,128)}, u32[]{:S(2)}) copy-start(f32[2,256,128]{2,1,0:T(8,128)} %refs_7_.1) | copy-start | bytes 786436
  0.7 60.7 %copy-start.6 = (f32[128,256]{1,0:T(8,128)S(1)}, f32[128,256]{1,0:T(8,128)}, u32[]{:S(2)}) copy-start(f32[128,256]{1,0:T(8,128)} %refs_2_.1) | copy-start | bytes 393220
  0.7 60.7 %copy-start.5 = (f32[128,256]{1,0:T(8,128)S(1)}, f32[128,256]{1,0:T(8,128)}, u32[]{:S(2)}) copy-start(f32[128,256]{1,0:T(8,128)} %refs_1_.1) | copy-start | bytes 393220
  0.7 60.7 %copy-start.8 = (f32[3,256]{1,0:T(4,128)S(1)}, f32[3,256]{1,0:T(4,128)}, u32[]{:S(2)}) copy-start(f32[3,256]{1,0:T(4,128)} %refs_3_.1) | copy-start | bytes 9220
  0.7 60.7 %copy-start.9 = (f32[6,256]{1,0:T(8,128)S(1)}, f32[6,256]{1,0:T(8,128)}, u32[]{:S(2)}) copy-start(f32[6,256]{1,0:T(8,128)} %refs_10_.1) | copy-start | bytes 18436
  0.7 60.7 %copy-start.10 = (f32[6,256]{1,0:T(8,128)S(1)}, f32[6,256]{1,0:T(8,128)}, u32[]{:S(2)}) copy-start(f32[6,256]{1,0:T(8,128)} %refs_11_.1) | copy-start | bytes 18436
  0.8 60.7 %copy-start.11 = (f32[3,256]{1,0:T(4,128)S(1)}, f32[3,256]{1,0:T(4,128)}, u32[]{:S(2)}) copy-start(f32[3,256]{1,0:T(4,128)} %refs_4_.1) | copy-start | bytes 9220
  0.8 60.7 %copy-start.12 = (f32[3,256]{1,0:T(4,128)S(1)}, f32[3,256]{1,0:T(4,128)}, u32[]{:S(2)}) copy-start(f32[3,256]{1,0:T(4,128)} %refs_5_.1) | copy-start | bytes 9220
  0.8 60.7 %copy-start.15 = (f32[2,128]{1,0:T(2,128)S(1)}, f32[2,128]{1,0:T(2,128)}, u32[]{:S(2)}) copy-start(f32[2,128]{1,0:T(2,128)} %refs_13_.1) | copy-start | bytes 3076
  0.8 60.7 %copy-start.16 = (f32[2,128]{1,0:T(2,128)S(1)}, f32[2,128]{1,0:T(2,128)}, u32[]{:S(2)}) copy-start(f32[2,128]{1,0:T(2,128)} %refs_14_.1) | copy-start | bytes 3076
  0.8 60.7 %copy-start.17 = (f32[2]{0:T(128)S(1)}, f32[2]{0:T(128)}, u32[]{:S(2)}) copy-start(f32[2]{0:T(128)} %refs_16_.1) | copy-start | bytes 28
  0.8 60.7 %copy-start.18 = (f32[2]{0:T(128)S(1)}, f32[2]{0:T(128)}, u32[]{:S(2)}) copy-start(f32[2]{0:T(128)} %refs_17_.1) | copy-start | bytes 28
  61.4 0.7 %copy-start.7 = (f32[6,256]{1,0:T(8,128)S(1)}, f32[6,256]{1,0:T(8,128)}, u32[]{:S(2)}) copy-start(f32[6,256]{1,0:T(8,128)} %refs_9_.1) | copy-start | bytes 18436
  61.4 0.7 %copy-start.13 = (f32[2,128]{1,0:T(2,128)S(1)}, f32[2,128]{1,0:T(2,128)}, u32[]{:S(2)}) copy-start(f32[2,128]{1,0:T(2,128)} %refs_12_.1) | copy-start | bytes 3076
  61.4 0.7 %copy-start.14 = (f32[2]{0:T(128)S(1)}, f32[2]{0:T(128)}, u32[]{:S(2)}) copy-start(f32[2]{0:T(128)} %refs_15_.1) | copy-start | bytes 28
  62.1 1.2 %copy-start.1 = (f32[2048,128]{1,0:T(8,128)S(1)}, f32[2048,128]{1,0:T(8,128)}, u32[]{:S(2)}) copy-start(f32[2048,128]{1,0:T(8,128)} %get-tuple-element.52.input_in) | copy-start | bytes 3145732

commit v3 on v2

--- a/solution.py
+++ b/solution.py
@@ -58,6 +58,10 @@
     return jnp.broadcast_to(jnp.sum(v, axis=1, keepdims=True), (v.shape[0], LANES))
 
 
+def in_hbm(arrays):
+    return [pltpu.with_memory_space_constraint(v, pltpu.HBM) for v in arrays]
+
+
 def spots_of(item_pad):
     names = ("sum", "spread", "mean", "crossed")
     if 4 * item_pad <= LANES:
@@ -78,24 +82,15 @@
     frames_hbm,
     out_cot_hbm,
     skip_cot_hbm,
-    expand_hbm,
-    project_hbm,
-    taps_hbm,
-    vectors_hbm,
-    biases_hbm,
-    block_out,
-    skip_out,
-    input_out,
-    expand_grad_ref,
-    project_grad_ref,
-    small_grad_ref,
+    *refs,
+):
+    state_hbm, refs = refs[:15], refs[15:]
+    block_out, skip_out, input_out, expand_grad_ref, project_grad_ref, small_grad_ref = refs[:6]
+    state_refs, refs = refs[6:21], refs[21:]
+    expand_ref, taps_ref, project_ref, vectors_ref, biases_ref = state_refs[::3]
+    (
     len_ref,
     slope_ref,
-    expand_ref,
-    project_ref,
-    taps_ref,
-    vectors_ref,
-    biases_ref,
     x,
     cots,
     w_expand,
@@ -129,6 +124,7 @@
     project_in,
     expand_in,
     small_part,
+    small_pair,
     small_in,
     late_part,
     late_in,
@@ -137,12 +133,13 @@
     square_part,
     last_part,
     last_in,
+    tail_in,
     local_sem,
     send_sem,
     recv_sem,
     near_send,
     near_recv,
-):
+    ) = refs
     frames = block_out.shape[0]
     wide = x.shape[0]
     half = expand_ref.shape[1]
@@ -191,16 +188,16 @@
 
     own = pl.ds(HALO, frames)
     loads = {
-        "expand": (expand_hbm, expand_ref),
+        "expand": (state_hbm[0], expand_ref),
         "frames": (frames_hbm, x.at[own, :]),
-        "vectors": (vectors_hbm, vectors_ref),
-        "taps": (taps_hbm, taps_ref),
+        "vectors": (state_hbm[9], vectors_ref),
+        "taps": (state_hbm[3], taps_ref),
         "lengths": (len_hbm, len_ref),
         "slopes": (slope_hbm, slope_ref),
-        "project": (project_hbm, project_ref),
+        "project": (state_hbm[6], project_ref),
         "out": (out_cot_hbm, cots.at[own, pl.ds(0, LANES)]),
         "skip": (skip_cot_hbm, cots.at[own, pl.ds(LANES, LANES)]),
-        "biases": (biases_hbm, biases_ref),
+        "biases": (state_hbm[12], biases_ref),
     }
     for k, (name, (src, dst)) in enumerate(loads.items()):
         load = pltpu.make_async_copy(src, dst, local_sem.at[k])
@@ -232,7 +229,8 @@
     w_expand[:, my_half] = expand_ref[...].astype(BF16)
     params[0:6, my_half] = vectors_ref[...]
     params[6:9, my_half] = taps_ref[...]
-    params[9:16, my_half] = jnp.zeros((7, half), F32)
+    params[9:12, my_half] = vectors_ref[1:2, :] * taps_ref[...]
+    params[12:16, my_half] = jnp.zeros((4, half), F32)
     loaded("frames")
     pl.semaphore_wait(barrier, devices - 1)
 
@@ -266,6 +264,11 @@
     to_left(cots, DILATION, 5)
     to_right(cots, DILATION, 6)
     loaded("lengths", "slopes", "biases")
+    moments = [k for k in range(15) if k % 3]
+    for k in moments:
+        load = pltpu.make_async_copy(state_hbm[k], state_refs[k], local_sem.at[10 + k])
+        load.start()
+        pending["load", k] = load.wait
 
     width = table.shape[0]
     lane = lax.broadcasted_iota(jnp.int32, (8, width), 1)
@@ -511,11 +514,11 @@
         for k in range(0, n, size):
             total = jnp.zeros((size, LANES), F32)
             for b in range(blocks):
-                y = part(product, k, size, b)
-                mixed_grad[pl.ds(at(r, k), size), lanes(b)] = y
+                q = params[4:5, lanes(b)] * part(product, k, size, b)
+                mixed_grad[pl.ds(at(r, k), size), lanes(b)] = q
                 if add:
-                    total = total + params[4:5, lanes(b)] * y
-                    column[SHIFT_TWO, :, lanes(b)] += fold_rows(y)
+                    total = total + q
+                    column[SHIFT_TWO, :, lanes(b)] += fold_rows(q)
             if add:
                 put_seg(at(r, k, HALO), size, 4, total)
 
@@ -585,7 +588,7 @@
                 d = a - centre
                 total = total + d
                 squares = squares + d * d
-                crossed = crossed + params[4:5, lanes(b)] * mixed_grad[rows, lanes(b)] * d
+                crossed = crossed + mixed_grad[rows, lanes(b)] * d
             put_seg(at(r, k, HALO), ROWS, 0, total)
             put_seg(at(r, k, HALO), ROWS, 2, squares, exact=False)
             put_seg(at(r, k, HALO), ROWS, 3, crossed, exact=False)
@@ -619,15 +622,15 @@
             mean, scale, q_mean, cross_mean = [part(values, k, size, j) for j in range(4)]
             for b in range(blocks):
                 a = act_two[rows, lanes(b)]
-                y = mixed_grad[rows, lanes(b)]
+                q = mixed_grad[rows, lanes(b)]
                 xhat = (a - mean) * scale
-                g = (params[4:5, lanes(b)] * y) * scale - q_mean - xhat * cross_mean
+                g = q * scale - q_mean - xhat * cross_mean
                 act_two[rows, lanes(b)] = rounded(g * jnp.where(a > 0, 1.0, slope_two))
                 if add:
                     mixed[pl.ds(at(r, k, HALO), size), lanes(b)] = (
                         params[4:5, lanes(b)] * xhat + params[5:6, lanes(b)]
                     ).astype(BF16)
-                    column[GAIN_TWO, :, lanes(b)] += fold_rows(y * xhat)
+                    column[GAIN_TWO, :, lanes(b)] += fold_rows(q * xhat)
                     column[SLOPE_TWO, :, lanes(b)] += fold_rows(g * jnp.minimum(a, 0.0))
 
     @own_loop()
@@ -653,18 +656,17 @@
                 column[TAP_B, :, lanes(b)] += fold_rows(here * n)
                 column[TAP_C, :, lanes(b)] += fold_rows(earlier * n)
                 column[DEPTH_BIAS, :, lanes(b)] += fold_rows(here)
-                y = (
-                    params[6:7, lanes(b)] * later
-                    + params[7:8, lanes(b)] * here
-                    + params[8:9, lanes(b)] * earlier
+                q = (
+                    params[9:10, lanes(b)] * later
+                    + params[10:11, lanes(b)] * here
+                    + params[11:12, lanes(b)] * earlier
                 )
-                column[SHIFT_ONE, :, lanes(b)] += fold_rows(y)
-                xhat = xhat_one[rows, lanes(b)]
-                column[GAIN_ONE, :, lanes(b)] += fold_rows(y * xhat)
-                q = params[1:2, lanes(b)] * y
                 mixed_grad[rows, lanes(b)] = q
+                column[SHIFT_ONE, :, lanes(b)] += fold_rows(q)
+                q_xhat = q * xhat_one[rows, lanes(b)]
+                column[GAIN_ONE, :, lanes(b)] += fold_rows(q_xhat)
                 total = total + q
-                crossed = crossed + q * xhat
+                crossed = crossed + q_xhat
             put_seg(at(r, k, HALO), ROWS, 0, total)
             put_seg(at(r, k, HALO), ROWS, 2, crossed)
 
@@ -690,11 +692,11 @@
         return jnp.sum(column[which], axis=0, keepdims=True)
 
     early_rows = {
-        1: column_sum(GAIN_ONE),
-        2: column_sum(SHIFT_ONE),
+        1: column_sum(GAIN_ONE) / params[1:2, :],
+        2: column_sum(SHIFT_ONE) / params[1:2, :],
         3: column_sum(DEPTH_BIAS),
-        4: column_sum(GAIN_TWO),
-        5: column_sum(SHIFT_TWO),
+        4: column_sum(GAIN_TWO) / params[4:5, :],
+        5: column_sum(SHIFT_TWO) / params[4:5, :],
         TAP_ROW: column_sum(TAP_A),
         TAP_ROW + 1: column_sum(TAP_B),
         TAP_ROW + 2: column_sum(TAP_C),
@@ -713,8 +715,6 @@
     mates = 2 * chips
     mate = chip * 2 + chan
     spot = lax.div(chip, stride)
-    reducers = 2 * PIECES
-    place = (spot * 2 + core) * 2 + chan
     is_reducer = lax.rem(chip, stride) == 0
 
     def when_reducer(body):
@@ -762,30 +762,36 @@
     def expand_piece(c, at_spot):
         return expand_pair.at[c, piece_rows(at_spot), :]
 
-    first_of_group = tm == 0
-
-    def to_first(parts, ref, phase):
-        for c in range(2):
-
-            @pl.when((tm != 0) | (chan != c))
-            def _(c=c):
-                remote(parts.at[c], ref.at[me], phase, {"chan": c, "tm": 0}).start()
-
-        def sent():
-            pl.when(first_of_group)(lambda: wait_bytes(ref.at[0], send_sem.at[phase]))
-            pl.when(jnp.logical_not(first_of_group))(
-                lambda: wait_bytes(ref.at[pl.ds(0, 2)], send_sem.at[phase])
+    keeper = chips // 2 // stride * stride * 2
+    is_keeper = tm == keeper
+
+    def to_keepers(parts, ref, slot, count, phase, sends):
+        def each(act):
+            for c in range(2):
+                copy = remote(parts.at[c], ref.at[slot], phase + c, {"chan": c, "tm": keeper})
+                pl.when(sends & ((tm != keeper) | (chan != c)))(lambda: act(copy))
+
+        each(lambda copy: copy.start())
+        pending[phase, "sent"] = lambda: each(lambda copy: copy.wait_send())
+        pending[phase, "here"] = lambda: [
+            pl.when(is_keeper & (chan == c))(
+                lambda: wait_bytes(ref.at[pl.ds(0, count - 1)], recv_sem.at[phase + c])
             )
-
-        pending[phase, "sent"] = sent
-        pending[phase, "here"] = lambda: pl.when(first_of_group)(
-            lambda: wait_bytes(ref.at[pl.ds(0, devices - 1)], recv_sem.at[phase])
-        )
-
-    to_first(small_part, small_in, 11)
+            for c in range(2)
+        ]
+
+    pair = remote(small_part, small_pair, 10, sibling)
+    started(pair, 10, core == 1, core == 0)
     settle((7, "here"))
     project_pair[...] += project_part[mine, :]
-    to_reducers(project_piece, project_in, 10)
+    to_reducers(project_piece, project_in, 11)
+    settle((10, "here"))
+
+    @pl.when(core == 0)
+    def _():
+        small_part[...] += small_pair[...]
+
+    to_keepers(small_part, small_in, mate, mates, 12, core == 0)
 
     @own_loop()
     def _(r):
@@ -830,13 +836,13 @@
     for c in range(2):
         late_part[c, 0:1, :] = bias_one[:, c * half : (c + 1) * half]
         late_part[c, 1:2, :] = slope_row
-    to_first(late_part, late_in, 13)
+    to_keepers(late_part, late_in, me, devices, 14, tm >= 0)
     settle((8, "here"), (9, "here"))
     for c in range(2):
         expand_pair[c] += expand_part[
             :, pl.ds(pl.multiple_of(c * half + core * LANES, LANES), LANES)
         ]
-    to_reducers(expand_piece, expand_in, 12)
+    to_reducers(expand_piece, expand_in, 16)
 
     def total_of(ref, count, rows, cols):
         return lax.fori_loop(
@@ -863,7 +869,7 @@
 
         lax.fori_loop(1, targets, one, 0)
 
-    settle((10, "here"))
+    settle((11, "here"))
     sum_rows = pl.ds(pl.multiple_of(core * LANES + spot * 16, 16), 16)
 
     @when_reducer
@@ -872,31 +878,29 @@
         total = total_of(project_in, mates, 16, half)
         project_sum[sum_rows, :] = total
         square_part[...] = fold_lanes(jnp.sum(total * total, axis=0, keepdims=True))
-        to_group(project_sum.at[sum_rows, :], project_sum.at[sum_rows, :], 14, chips)
-
-    pending[14, "sent"] = lambda: when_reducer(
-        lambda: group_sent(project_sum.at[pl.ds(0, 16), :], 14, chips)
+        to_group(project_sum.at[sum_rows, :], project_sum.at[sum_rows, :], 17, chips)
+
+    pending[17, "sent"] = lambda: when_reducer(
+        lambda: group_sent(project_sum.at[pl.ds(0, 16), :], 17, chips)
     )
-    pending[14, "here"] = lambda: by_role(
-        lambda n: wait_bytes(project_sum.at[pl.ds(0, 16 * n), :], recv_sem.at[14]), PIECES // 2
+    pending[17, "here"] = lambda: by_role(
+        lambda n: wait_bytes(project_sum.at[pl.ds(0, 16 * n), :], recv_sem.at[17]), PIECES // 2
     )
-    settle((11, "here"))
-
-    @pl.when(first_of_group)
+    settle((12, "here"))
+
+    @pl.when(is_keeper)
     def _():
-        small_in[me] = small_part[chan]
-        total = total_of(small_in, devices, 16, half)
+        small_in[mate] = small_part[chan]
+        total = total_of(small_in, mates, 16, half)
         small_sum[...] = total
         square_part[...] += fold_lanes(
             jnp.sum((total * total)[0:BIAS_ROW], axis=0, keepdims=True)
         )
-        to_group(small_sum, small_sum, 15, tm_size)
-
-    pending[15, "sent"] = lambda: pl.when(first_of_group)(
-        lambda: group_sent(small_sum, 15, tm_size)
-    )
-    pending[15, "here"] = lambda: pl.when(jnp.logical_not(first_of_group))(
-        lambda: wait_bytes(small_sum, recv_sem.at[15])
+        to_group(small_sum, small_sum, 18, tm_size)
+
+    pending[18, "sent"] = lambda: pl.when(is_keeper)(lambda: group_sent(small_sum, 18, tm_size))
+    pending[18, "here"] = lambda: pl.when(jnp.logical_not(is_keeper))(
+        lambda: wait_bytes(small_sum, recv_sem.at[18])
     )
 
     @own_loop()
@@ -906,10 +910,10 @@
             above = cots[pl.ds(at(r, k), ROWS), 0:LANES].astype(F32)
             input_out[pl.ds(at(r, k, HALO), ROWS), :] = above + part(product, k, ROWS, 0)
 
-    settle((13, "here"))
     last_part[...] = jnp.zeros_like(last_part)
-
-    @pl.when(first_of_group)
+    settle((14, "here"))
+
+    @pl.when(is_keeper)
     def _():
         late_in[me] = late_part[chan]
         total = total_of(late_in, devices, 2, half)
@@ -918,58 +922,63 @@
         squares = (total * total)[0:1]
         square_part[...] += fold_lanes(squares)
 
-    settle((12, "here"))
+    settle((16, "here"))
 
     @when_reducer
     def _():
         expand_in[mate] = expand_piece(chan, spot)[...]
         total = total_of(expand_in, mates, 16, LANES)
+        squares = square_part[...] + jnp.sum(total * total, axis=0, keepdims=True)
+        square_part[...] = squares
         last_part[0:16, :] = total
-        last_part[16:17, :] = square_part[...] + jnp.sum(total * total, axis=0, keepdims=True)
-        last_in[place] = last_part[...]
-        to_group(last_part, last_in.at[place], 17, tm_size)
-        tail = pl.ds(16, 8)
+        last_part[16:17, :] = squares
+        last_in[core, spot] = last_part[...]
 
         def send_tail(k, carry):
-            target = {"chan": other, "tm": lax.rem(tm + k, tm_size)}
-            remote(last_part.at[tail, :], last_in.at[place, tail, :], 18, target).start()
+            target = {"chan": other, "tm": lax.rem(chip + k, chips) * 2 + core}
+            remote(square_part, tail_in.at[core, spot], 20, target).start()
             return carry
 
-        lax.fori_loop(0, tm_size, send_tail, 0)
-
-    def tails(count, sem):
-        wait_bytes(last_in.at[pl.ds(0, count), pl.ds(16, 8), :], sem)
+        to_group(last_part, last_in.at[core, spot], 19, chips)
+        lax.fori_loop(0, chips, send_tail, 0)
 
     def tails_sent():
-        for _ in range(tm_size // PIECES):
-            tails(PIECES, send_sem.at[18])
-
-    pending[17, "sent"] = lambda: when_reducer(lambda: group_sent(last_part, 17, tm_size))
-    pending[17, "here"] = lambda: by_role(
-        lambda n: wait_bytes(last_in.at[pl.ds(0, n)], recv_sem.at[17]), PIECES
+        for _ in range(stride):
+            wait_bytes(tail_in.at[0], send_sem.at[20])
+
+    pending[19, "sent"] = lambda: when_reducer(lambda: group_sent(last_part, 19, chips))
+    pending[19, "here"] = lambda: by_role(
+        lambda n: wait_bytes(last_in.at[0, pl.ds(0, n)], recv_sem.at[19]), PIECES // 2
     )
-    pending[18, "sent"] = lambda: when_reducer(tails_sent)
-    pending[18, "here"] = lambda: tails(PIECES, recv_sem.at[18])
-
-    settle((14, "here"))
-    started(remote(project_sum.at[mine, :], project_sum.at[mine, :], 16, sibling), 16)
-    settle((15, "here"), (16, "here"))
+    pending[20, "sent"] = lambda: when_reducer(tails_sent)
+    pending[20, "here"] = lambda: wait_bytes(tail_in.at[0], recv_sem.at[20])
+
+    settle((17, "here"))
+    started(remote(project_sum.at[mine, :], project_sum.at[mine, :], 21, sibling), 21)
+    settle((19, "here"))
+    started(remote(last_in.at[core], last_in.at[core], 22, sibling), 22)
+    settle((20, "here"))
+    started(remote(tail_in.at[core], tail_in.at[core], 23, sibling), 23)
+    settle((18, "here"), (21, "here"))
     for k in range(2):
         project_grad_ref[k] = project_sum[k * LANES : (k + 1) * LANES, :].T
     small_grad_ref[...] = small_sum[...]
-    settle((17, "here"), (18, "here"))
-    for j in range(PIECES):
-        rows, lanes_here = slice(j // 2 * 16, j // 2 * 16 + 16), slice(j % 2 * LANES, (j % 2 + 1) * LANES)
-        expand_grad_ref[rows, lanes_here] = last_in[j * 2 + chan, 0:16, :]
+    settle((22, "here"), (23, "here"))
+    for c in range(2):
+        for j in range(PIECES // 2):
+            expand_grad_ref[j * 16 : j * 16 + 16, c * LANES : (c + 1) * LANES] = last_in[c, j, 0:16]
+    keeper_spot = keeper // 2 // stride
     for k in range(2):
         where = slice(k * LANES, (k + 1) * LANES)
-        late = last_in[chan, 17 + 2 * k : 19 + 2 * k, :]
+        late = last_in[0, keeper_spot, 17 + 2 * k : 19 + 2 * k, :]
         small_grad_ref[0:1, where] = late[0:1]
         small_grad_ref[SLOPE_ONE_ROW : SLOPE_ONE_ROW + 1, where] = late[1:2]
-    total = last_in[0, 16:17, :]
-    for q in range(1, reducers):
-        total = total + last_in[q, 16:17, :]
-    small_grad_ref[SQUARES_ROW : SQUARES_ROW + 1, 0:LANES] = total
+    own_total, other_total = last_in[0, 0, 16:17, :], tail_in[0, 0]
+    for q in range(1, PIECES):
+        c, j = q // (PIECES // 2), q % (PIECES // 2)
+        own_total = own_total + last_in[c, j, 16:17, :]
+        other_total = other_total + tail_in[c, j]
+    small_grad_ref[SQUARES_ROW : SQUARES_ROW + 1, 0:LANES] = own_total + other_total
     small_grad_ref[SQUARES_ROW : SQUARES_ROW + 1, LANES:half] = jnp.zeros((1, half - LANES), F32)
 
     settle(*list(pending))
@@ -996,8 +1005,14 @@
     small_grad,
     *refs,
 ):
-    state, outs = refs[:18], refs[18:40]
-    sem = refs[40]
+    state, outs, slope_refs = list(refs[:15]), refs[18:40], refs[40:43]
+    sem = refs[43]
+    slope_loads = [
+        pltpu.make_async_copy(refs[15 + k], slope_refs[k], sem.at[3 + k]) for k in range(3)
+    ]
+    for load in slope_loads:
+        load.start()
+    state += slope_refs
     copies = [
         pltpu.make_async_copy(src, dst, sem.at[k])
         for k, (src, dst) in enumerate(
@@ -1032,6 +1047,8 @@
     lanes = biases.shape[1] // 2
     for k in range(2):
         update(4, biases[:, k * lanes : (k + 1) * lanes], small_rate, slice(k, k + 1))
+    for load in slope_loads:
+        load.wait()
     for k in range(2):
         results = adam(
             state[15][k], state[16][k], state[17][k], slopes[k], scale, small_rate
@@ -1075,7 +1092,6 @@
     width = -(-3 * item_pad // LANES) * LANES
     wide = frames + 2 * HALO
     devices = 2 * tm_size
-    reducers = 2 * PIECES
     peers = 2 * (-(-LONGEST_ITEM // frames))
     tile_rows = spots_of(item_pad)[0]
     vmem, smem, anywhere, hbm = (
@@ -1084,11 +1100,6 @@
     )
     shape = jax.ShapeDtypeStruct
     scratch = [
-        ((inputs, half), F32),
-        ((2, half, inputs), F32),
-        ((3, half), F32),
-        ((6, half), F32),
-        ((2, inputs), F32),
         ((wide, inputs), BF16),
         ((wide, 2 * inputs), BF16),
         ((inputs, hidden), BF16),
@@ -1122,57 +1133,17 @@
         ((tm_size, 16, half), F32),
         ((tm_size, 16, LANES), F32),
         ((2, 16, half), F32),
-        ((devices, 16, half), F32),
+        ((2, 16, half), F32),
+        ((tm_size, 16, half), F32),
         ((2, 2, half), F32),
         ((devices, 2, half), F32),
         ((2 * inputs, half), F32),
         ((16, half), F32),
         ((1, LANES), F32),
         ((24, LANES), F32),
-        ((reducers, 24, LANES), F32),
+        ((2, PIECES // 2, 24, LANES), F32),
+        ((2, PIECES // 2, 1, LANES), F32),
     ]
-    block_raw, skip_raw, input_raw, expand_grad, project_grad, small_grad = pl.pallas_call(
-        functools.partial(block_kernel, tm_size, items, item_pad),
-        out_shape=[
-            shape((frames, inputs), BF16),
-            shape((frames, inputs), BF16),
-            shape((frames, inputs), F32),
-            shape((inputs, half), F32),
-            shape((2, half, inputs), F32),
-            shape((16, half), F32),
-        ],
-        in_specs=[hbm] * 10,
-        out_specs=[vmem] * 6,
-        scratch_shapes=[pltpu.SMEM((items,), jnp.int32), pltpu.SMEM((2,), F32)]
-        + [pltpu.VMEM(s, t) for s, t in scratch]
-        + [
-            pltpu.SemaphoreType.DMA((10,)),
-            pltpu.SemaphoreType.DMA((19,)),
-            pltpu.SemaphoreType.DMA((19,)),
-            pltpu.SemaphoreType.DMA((3, peers)),
-            pltpu.SemaphoreType.DMA((3, peers)),
-        ],
-        compiler_params=pltpu.CompilerParams(
-            collective_id=0, has_side_effects=True, vmem_limit_bytes=52 * 2**20
-        ),
-        name="temporal_block",
-    )(
-        *[
-            pltpu.with_memory_space_constraint(v, pltpu.HBM)
-            for v in (
-                item_lengths,
-                prelu_slopes,
-                frames_in,
-                out_cotangent,
-                skip_cotangent,
-                expand,
-                project,
-                depthwise,
-                channel_vectors,
-                output_biases,
-            )
-        ]
-    )
     state = [
         expand,
         expand_moment,
@@ -1189,10 +1160,37 @@
         output_biases,
         bias_moment,
         bias_square,
-        prelu_slopes,
-        slope_moment,
-        slope_square,
     ]
+    state = in_hbm(state)
+    slopes = in_hbm([prelu_slopes, slope_moment, slope_square])
+    arrays = in_hbm([item_lengths, frames_in, out_cotangent, skip_cotangent])
+    kept = pl.pallas_call(
+        functools.partial(block_kernel, tm_size, items, item_pad),
+        out_shape=[
+            shape((frames, inputs), BF16),
+            shape((frames, inputs), BF16),
+            shape((frames, inputs), F32),
+            shape((inputs, half), F32),
+            shape((2, half, inputs), F32),
+            shape((16, half), F32),
+        ]
+        + [shape(v.shape, F32) for v in state],
+        in_specs=[hbm] * 20,
+        out_specs=[vmem] * 21,
+        scratch_shapes=[pltpu.SMEM((items,), jnp.int32), pltpu.SMEM((2,), F32)]
+        + [pltpu.VMEM(s, t) for s, t in scratch]
+        + [
+            pltpu.SemaphoreType.DMA((25,)),
+            pltpu.SemaphoreType.DMA((24,)),
+            pltpu.SemaphoreType.DMA((24,)),
+            pltpu.SemaphoreType.DMA((3, peers)),
+            pltpu.SemaphoreType.DMA((3, peers)),
+        ],
+        compiler_params=pltpu.CompilerParams(
+            collective_id=0, has_side_effects=True, vmem_limit_bytes=48 * 2**20
+        ),
+        name="temporal_block",
+    )(arrays[0], slopes[0], *arrays[1:], *state)
     results = pl.pallas_call(
         adam_kernel,
         out_shape=[
@@ -1201,13 +1199,13 @@
             shape((frames, inputs), F32),
             shape((1, 1), F32),
         ]
-        + [shape(v.shape, F32) for v in state],
-        in_specs=[anywhere] * 3 + [vmem] * 18 + [smem] * 3,
+        + [shape(v.shape, F32) for v in state + slopes],
+        in_specs=[anywhere] * 3 + [vmem] * 18 + [hbm] * 3,
         out_specs=[anywhere] * 3 + [smem] + [vmem] * 15 + [smem] * 3,
-        scratch_shapes=[pltpu.SemaphoreType.DMA((3,))],
-        compiler_params=pltpu.CompilerParams(vmem_limit_bytes=32 * 2**20),
+        scratch_shapes=[pltpu.SMEM((2,), F32)] * 3 + [pltpu.SemaphoreType.DMA((6,))],
+        compiler_params=pltpu.CompilerParams(vmem_limit_bytes=8 * 2**20),
         name="adam_step",
-    )(block_raw, skip_raw, input_raw, expand_grad, project_grad, small_grad, *state)
+    )(*kept, *slopes)
     results = list(results)
     results[3] = results[3].reshape(())
     return tuple(results)

time: 66.9 us -> 62.9 us (0.940)
  Pallas kernels: 63.9 us -> 61.9 us
  local copies, waits for them, and re-layouts: 1.82 us -> 0 us
    unnamed x38 -> x0, local copies, waits for them, and re-layouts: 1.82 us -> none
    pallas_call x1, Pallas kernels: 60.5 us -> 59.4 us  [per_device(): pl.pallas_call(functools.partial(block_kernel, tm_size, items, item_pad),...]
    pallas_call x1, Pallas kernels: 3.39 us -> 2.5 us  [per_device(): pl.pallas_call(adam_kernel, out_shape=[shape((frames, inputs), BF16), sha...]
where the time goes in v3:
time: 62.9 us; the launch traced here: 62.6 us
  Pallas kernels  61.9 us (98%)
  between operations  0.67 us (1%)
    pallas_call x1, Pallas kernels, per_device(): pl.pallas_call(functools.partial(block_kernel, tm_size, items, item_pad),...  59.4 us
    pallas_call x1, Pallas kernels, per_device(): pl.pallas_call(adam_kernel, out_shape=[shape((frames, inputs), BF16), sha...  2.5 us

profile of v3, /device:TPU:0, one launch (start us, length us, event | category | flops | bytes accessed | tf_op | source)
XLA Modules:
  0.0 62.6 jit_solution(7898167760536864309)
XLA Ops:
  0.7 59.4 %temporal_block.1 = (bf16[2048,128]{1,0:T(8,128)(2,1)S(1)}, bf16[2048,128]{1,0:T(8,128)(2,1)S(1)}, f32[2048,128]{1,0:T(8,128)S(1)}, f32[128,256]{1,0:T(8,128)S(1...) custom-call(s32[16]{0:T(128)} %len_hbm.1, ...), custom_call_target="tpu_custom_call" | custom-call | tf_op jit(solution)/shard_map/temporal_block/pallas_call | solution.py:1167
  60.1 2.5 %adam_step.1 = (bf16[2048,128]{1,0:T(8,128)(2,1)}, bf16[2048,128]{1,0:T(8,128)(2,1)}, f32[2048,128]{1,0:T(8,128)}, f32[1,1]{1,0:T(1,128)}, f32[128,256]{1,0:T(8,...) custom-call(bf16[2048,128]{1,0:T(8,128)(2,1)S(1)} %get-tuple-element, ...), custom_call_target="tpu_custom_call" | custom-call | tf_op jit(solution)/shard_map/adam_step/pallas_call | solution.py:1194

commit v4 on v3

--- a/solution.py
+++ b/solution.py
@@ -131,6 +131,7 @@
     project_sum,
     small_sum,
     square_part,
+    extra,
     last_part,
     last_in,
     tail_in,
@@ -199,10 +200,13 @@
         "skip": (skip_cot_hbm, cots.at[own, pl.ds(LANES, LANES)]),
         "biases": (state_hbm[12], biases_ref),
     }
-    for k, (name, (src, dst)) in enumerate(loads.items()):
-        load = pltpu.make_async_copy(src, dst, local_sem.at[k])
-        load.start()
-        pending["load", name] = load.wait
+    def load_some(first, last):
+        for k, (name, (src, dst)) in list(enumerate(loads.items()))[first:last]:
+            load = pltpu.make_async_copy(src, dst, local_sem.at[k])
+            load.start()
+            pending["load", name] = load.wait
+
+    load_some(0, 2)
 
     def loaded(*names):
         settle(*[("load", name) for name in names])
@@ -216,22 +220,29 @@
 
     barrier = pltpu.get_barrier_semaphore()
 
+    def wrapped(v, size):
+        return jnp.where(v >= size, v - size, v)
+
     def greet(k, carry):
-        pl.semaphore_signal(
-            barrier, inc=1, device_id=device(lax.rem(me + k, devices)), device_id_type=MESH
-        )
+        t = wrapped(tm + k, tm_size)
+        for c in range(2):
+            pl.semaphore_signal(
+                barrier, inc=1, device_id={"chan": c, "tm": t}, device_id_type=MESH
+            )
         return carry
 
-    lax.fori_loop(1, devices, greet, 0)
+    pl.semaphore_signal(barrier, inc=1, device_id={"chan": other, "tm": tm}, device_id_type=MESH)
+    if tm_size <= 16:
+        for k in range(1, tm_size):
+            greet(k, 0)
+    else:
+        lax.fori_loop(1, tm_size, greet, 0)
+
+    load_some(2, len(loads))
 
     my_half = pl.ds(pl.multiple_of(chan * half, half), half)
-    loaded("expand", "vectors", "taps")
+    loaded("expand")
     w_expand[:, my_half] = expand_ref[...].astype(BF16)
-    params[0:6, my_half] = vectors_ref[...]
-    params[6:9, my_half] = taps_ref[...]
-    params[9:12, my_half] = vectors_ref[1:2, :] * taps_ref[...]
-    params[12:16, my_half] = jnp.zeros((4, half), F32)
-    loaded("frames")
     pl.semaphore_wait(barrier, devices - 1)
 
     partner = device(tm * 2 + other)
@@ -254,7 +265,13 @@
         started(copy, name, has_right, has_left)
 
     started(remote(w_expand.at[:, my_half], w_expand.at[:, my_half], 0, partner), 0)
+    loaded("vectors", "taps")
+    params[0:6, my_half] = vectors_ref[...]
+    params[6:9, my_half] = taps_ref[...]
+    params[9:12, my_half] = vectors_ref[1:2, :] * taps_ref[...]
+    params[12:16, my_half] = jnp.zeros((4, half), F32)
     started(remote(params.at[:, my_half], params.at[:, my_half], 1, partner), 1)
+    loaded("frames")
     to_left(x, HALO, 2)
     to_right(x, HALO, 3)
     loaded("project", "out", "skip")
@@ -637,8 +654,112 @@
     def _(r):
         second_back(r, BLOCK, ROWS, True)
 
+    chips = tm_size // 2
+    chip = lax.div(tm, 2)
+    mates = 2 * chips
+    mate = chip * 2 + chan
+    spot = lax.div(chip, stride)
+    is_reducer = lax.rem(chip, stride) == 0
+
+    def when_reducer(body):
+        if stride == 1:
+            body()
+        else:
+            pl.when(is_reducer)(body)
+
+    def by_role(body, count):
+        if stride == 1:
+            body(count - 1)
+        else:
+            pl.when(is_reducer)(lambda: body(count - 1))
+            pl.when(jnp.logical_not(is_reducer))(lambda: body(count))
+
+    spots_here = PIECES // 2
+
+    def send_pieces(source, ref, phase, c):
+        for k in range(spots_here):
+            at_spot = wrapped(spot + k, spots_here)
+            target = {"chan": c, "tm": at_spot * (2 * stride) + core}
+            copy = remote(source(c, at_spot), ref.at[mate], phase, target)
+            if k == 0:
+                pl.when(jnp.logical_not(is_reducer & (chan == c)))(copy.start)
+            else:
+                copy.start()
+
+    def pieces_pending(ref, phase):
+        pending[phase, "sent"] = lambda: by_role(
+            lambda n: wait_bytes(ref.at[pl.ds(0, n)], send_sem.at[phase]), PIECES
+        )
+        pending[phase, "here"] = lambda: when_reducer(
+            lambda: wait_bytes(ref.at[pl.ds(0, mates - 1)], recv_sem.at[phase])
+        )
+
+    def piece_rows(at_spot):
+        return pl.ds(pl.multiple_of(at_spot * 16, 16), 16)
+
+    def project_piece(c, at_spot):
+        return project_pair.at[piece_rows(at_spot), pl.ds(pl.multiple_of(c * half, half), half)]
+
+    def expand_piece(c, at_spot):
+        return expand_pair.at[c, piece_rows(at_spot), :]
+
+    def total_of(ref, count, rows, cols):
+        if count <= 32:
+            total = ref[0]
+            for k in range(1, count):
+                total = total + ref[k]
+            return total
+        return lax.fori_loop(
+            0, count, lambda k, total: total + ref[k], jnp.zeros((rows, cols), F32)
+        )
+
+    def fold_lanes(v):
+        return v[:, 0:LANES] + v[:, LANES:half]
+
+    def to_group(src, dst, phase, targets):
+        def one(k, carry):
+            if targets == chips:
+                t = wrapped(chip + k, chips) * 2 + core
+            else:
+                t = wrapped(tm + k, tm_size)
+            remote(src, dst, phase, {"chan": chan, "tm": t}).start()
+            return carry
+
+        if targets <= 16:
+            for k in range(1, targets):
+                one(k, 0)
+        else:
+            lax.fori_loop(1, targets, one, 0)
+
+    def group_sent(ref, phase, targets):
+        def one(k, carry):
+            wait_bytes(ref, send_sem.at[phase])
+            return carry
+
+        lax.fori_loop(1, targets, one, 0)
+
+    step = 512
+    total = jnp.zeros((2 * LANES, hidden), F32)
+    for k in range(frames // step):
+        total = total + dot_frames(
+            cots[pl.ds(HALO + k * step, step), :], mixed[pl.ds(k * step, step), :]
+        )
+    project_part[...] = total
+
+    core = lax.rem(tm, 2)
+    sibling = {"chan": chan, "tm": tm + 1 - 2 * core}
+    mine = pl.ds(pl.multiple_of(core * LANES, LANES), LANES)
+    yours = pl.ds(pl.multiple_of((1 - core) * LANES, LANES), LANES)
+    started(remote(project_part.at[yours, :], project_pair, 7, sibling), 7)
+
     for r in (HALO - DILATION, HALO + frames):
         second_back(r, DILATION, DILATION, False)
+
+    settle((7, "here"))
+    project_pair[...] += project_part[mine, :]
+    for c in range(2):
+        send_pieces(project_piece, project_in, 11, c)
+    pieces_pending(project_in, 11)
 
     @functools.partial(loop, HALO, 2 * ROWS, frames // (2 * ROWS))
     def _(r):
@@ -674,20 +795,6 @@
     pack_tile(tile_three, {"sum": total, "crossed": crossed})
     exchange(tile_three, stats_three, 2)
 
-    step = 512
-    total = jnp.zeros((2 * LANES, hidden), F32)
-    for k in range(frames // step):
-        total = total + dot_frames(
-            cots[pl.ds(HALO + k * step, step), :], mixed[pl.ds(k * step, step), :]
-        )
-    project_part[...] = total
-
-    core = lax.rem(tm, 2)
-    sibling = {"chan": chan, "tm": tm + 1 - 2 * core}
-    mine = pl.ds(pl.multiple_of(core * LANES, LANES), LANES)
-    yours = pl.ds(pl.multiple_of((1 - core) * LANES, LANES), LANES)
-    started(remote(project_part.at[yours, :], project_pair, 7, sibling), 7)
-
     def column_sum(which):
         return jnp.sum(column[which], axis=0, keepdims=True)
 
@@ -710,58 +817,6 @@
         small_part[c, BIAS_ROW : BIAS_ROW + 1, :] = bias_sum
         small_part[c, SLOPE_TWO_ROW : SLOPE_TWO_ROW + 1, :] = slope_two_row
 
-    chips = tm_size // 2
-    chip = lax.div(tm, 2)
-    mates = 2 * chips
-    mate = chip * 2 + chan
-    spot = lax.div(chip, stride)
-    is_reducer = lax.rem(chip, stride) == 0
-
-    def when_reducer(body):
-        if stride == 1:
-            body()
-        else:
-            pl.when(is_reducer)(body)
-
-    def by_role(body, count):
-        if stride == 1:
-            body(count - 1)
-        else:
-            pl.when(is_reducer)(lambda: body(count - 1))
-            pl.when(jnp.logical_not(is_reducer))(lambda: body(count))
-
-    def to_reducers(source, ref, phase):
-        def one(k, carry):
-            q = lax.rem(spot * 2 + chan + k, PIECES)
-            c, at_spot = lax.rem(q, 2), lax.div(q, 2)
-            target = {"chan": c, "tm": at_spot * stride * 2 + core}
-
-            def send():
-                remote(source(c, at_spot), ref.at[mate], phase, target).start()
-
-            if stride == 1:
-                send()
-            else:
-                pl.when(at_spot * stride * 2 + c != mate)(send)
-            return carry
-
-        lax.fori_loop(1 if stride == 1 else 0, PIECES, one, 0)
-        pending[phase, "sent"] = lambda: by_role(
-            lambda n: wait_bytes(ref.at[pl.ds(0, n)], send_sem.at[phase]), PIECES
-        )
-        pending[phase, "here"] = lambda: when_reducer(
-            lambda: wait_bytes(ref.at[pl.ds(0, mates - 1)], recv_sem.at[phase])
-        )
-
-    def piece_rows(at_spot):
-        return pl.ds(pl.multiple_of(at_spot * 16, 16), 16)
-
-    def project_piece(c, at_spot):
-        return project_pair.at[piece_rows(at_spot), pl.ds(pl.multiple_of(c * half, half), half)]
-
-    def expand_piece(c, at_spot):
-        return expand_pair.at[c, piece_rows(at_spot), :]
-
     keeper = chips // 2 // stride * stride * 2
     is_keeper = tm == keeper
 
@@ -782,17 +837,6 @@
 
     pair = remote(small_part, small_pair, 10, sibling)
     started(pair, 10, core == 1, core == 0)
-    settle((7, "here"))
-    project_pair[...] += project_part[mine, :]
-    to_reducers(project_piece, project_in, 11)
-    settle((10, "here"))
-
-    @pl.when(core == 0)
-    def _():
-        small_part[...] += small_pair[...]
-
-    to_keepers(small_part, small_in, mate, mates, 12, core == 0)
-
     @own_loop()
     def _(r):
         product = dot(mixed[pl.ds(at(r, 0, HALO), BLOCK), :], w_project[...])
@@ -804,32 +848,77 @@
             ).astype(BF16)
             skip_out[rows, :] = (part(product, k, ROWS, 1) + biases_ref[1:2, :]).astype(BF16)
 
+    settle((10, "here"))
+
+    @pl.when(core == 0)
+    def _():
+        small_part[...] += small_pair[...]
+
+    to_keepers(small_part, small_in, mate, mates, 12, core == 0)
+    settle((11, "here"))
+    sum_rows = pl.ds(pl.multiple_of(core * LANES + spot * 16, 16), 16)
+
+    @when_reducer
+    def _():
+        project_in[mate] = project_piece(chan, spot)[...]
+        total = total_of(project_in, mates, 16, half)
+        project_sum[sum_rows, :] = total
+        square_part[...] = fold_lanes(jnp.sum(total * total, axis=0, keepdims=True))
+        to_group(project_sum.at[sum_rows, :], project_sum.at[sum_rows, :], 17, chips)
+
+    pending[17, "sent"] = lambda: when_reducer(
+        lambda: group_sent(project_sum.at[pl.ds(0, 16), :], 17, chips)
+    )
+    pending[17, "here"] = lambda: by_role(
+        lambda n: wait_bytes(project_sum.at[pl.ds(0, 16 * n), :], recv_sem.at[17]), PIECES // 2
+    )
+
     settle(("near", 2, "here"))
     put_table(0, sum_of("sum", tile_three, stats_three) / elements)
     put_table(1, sum_of("crossed", tile_three, stats_three) / elements)
     put_table(2, scale_one)
 
-    @own_loop()
-    def _(r):
-        values = rows_of(r, BLOCK, 3)
-        for k in range(0, BLOCK, ROWS):
-            rows, local = pl.ds(at(r, k), ROWS), pl.ds(at(r, k, HALO), ROWS)
-            q_mean, cross_mean, scale = [part(values, k, ROWS, j) for j in range(3)]
-            for b in range(blocks):
-                a = act_one[rows, lanes(b)]
-                g = (mixed_grad[rows, lanes(b)] - q_mean - xhat_one[rows, lanes(b)] * cross_mean) * scale
-                column[SLOPE_ONE, :, lanes(b)] += fold_rows(g * jnp.minimum(a, 0.0))
-                hidden_grad[local, lanes(b)] = (g * jnp.where(a > 0, 1.0, slope_one)).astype(BF16)
-
-    total = jnp.zeros((LANES, hidden), F32)
-    for k in range(frames // step):
-        total = total + dot_frames(
-            x[pl.ds(HALO + k * step, step), :], hidden_grad[pl.ds(k * step, step), :]
-        )
-    expand_part[...] = total
+
     for c in range(2):
+
+        @own_loop()
+        def _(r, c=c):
+            if c == 0:
+                values = rows_of(r, BLOCK, 3)
+                act_two[pl.ds(r, BLOCK), 0 : 3 * LANES] = values
+            for k in range(0, BLOCK, ROWS):
+                rows, local = pl.ds(at(r, k), ROWS), pl.ds(at(r, k, HALO), ROWS)
+                if c == 0:
+                    q_mean, cross_mean, scale = [part(values, k, ROWS, j) for j in range(3)]
+                else:
+                    q_mean, cross_mean, scale = [act_two[rows, lanes(j)] for j in range(3)]
+                for b in range(c * blocks // 2, (c + 1) * blocks // 2):
+                    a = act_one[rows, lanes(b)]
+                    g = mixed_grad[rows, lanes(b)] - q_mean
+                    g = (g - xhat_one[rows, lanes(b)] * cross_mean) * scale
+                    column[SLOPE_ONE, :, lanes(b)] += fold_rows(g * jnp.minimum(a, 0.0))
+                    hidden_grad[local, lanes(b)] = (g * jnp.where(a > 0, 1.0, slope_one)).astype(
+                        BF16
+                    )
+
+        total = jnp.zeros((LANES, half), F32)
+        for k in range(frames // step):
+            total = total + dot_frames(
+                x[pl.ds(HALO + k * step, step), :],
+                hidden_grad[pl.ds(k * step, step), c * half : (c + 1) * half],
+            )
+        expand_part[:, c * half : (c + 1) * half] = total
         source = pl.ds(pl.multiple_of(c * half + (1 - core) * LANES, LANES), LANES)
         started(remote(expand_part.at[:, source], expand_pair.at[c], 8 + c, sibling), 8 + c)
+
+    def send_expand(c):
+        settle((8 + c, "here"))
+        expand_pair[c] += expand_part[
+            :, pl.ds(pl.multiple_of(c * half + core * LANES, LANES), LANES)
+        ]
+        send_pieces(expand_piece, expand_in, 16, c)
+
+    send_expand(0)
     bias_one = dot(jnp.ones((16, frames), BF16), hidden_grad[...])[0:1]
     slope_row = column_sum(SLOPE_ONE)
     slope_row = (slope_row[:, 0:half] + slope_row[:, half:hidden]) / slope_one
@@ -837,55 +926,9 @@
         late_part[c, 0:1, :] = bias_one[:, c * half : (c + 1) * half]
         late_part[c, 1:2, :] = slope_row
     to_keepers(late_part, late_in, me, devices, 14, tm >= 0)
-    settle((8, "here"), (9, "here"))
-    for c in range(2):
-        expand_pair[c] += expand_part[
-            :, pl.ds(pl.multiple_of(c * half + core * LANES, LANES), LANES)
-        ]
-    to_reducers(expand_piece, expand_in, 16)
-
-    def total_of(ref, count, rows, cols):
-        return lax.fori_loop(
-            0, count, lambda k, total: total + ref[k], jnp.zeros((rows, cols), F32)
-        )
-
-    def fold_lanes(v):
-        return v[:, 0:LANES] + v[:, LANES:half]
-
-    def to_group(src, dst, phase, targets):
-        def one(k, carry):
-            target = (
-                lax.rem(chip + k, chips) * 2 + core if targets == chips else lax.rem(tm + k, tm_size)
-            )
-            remote(src, dst, phase, {"chan": chan, "tm": target}).start()
-            return carry
-
-        lax.fori_loop(1, targets, one, 0)
-
-    def group_sent(ref, phase, targets):
-        def one(k, carry):
-            wait_bytes(ref, send_sem.at[phase])
-            return carry
-
-        lax.fori_loop(1, targets, one, 0)
-
-    settle((11, "here"))
-    sum_rows = pl.ds(pl.multiple_of(core * LANES + spot * 16, 16), 16)
-
-    @when_reducer
-    def _():
-        project_in[mate] = project_piece(chan, spot)[...]
-        total = total_of(project_in, mates, 16, half)
-        project_sum[sum_rows, :] = total
-        square_part[...] = fold_lanes(jnp.sum(total * total, axis=0, keepdims=True))
-        to_group(project_sum.at[sum_rows, :], project_sum.at[sum_rows, :], 17, chips)
-
-    pending[17, "sent"] = lambda: when_reducer(
-        lambda: group_sent(project_sum.at[pl.ds(0, 16), :], 17, chips)
-    )
-    pending[17, "here"] = lambda: by_role(
-        lambda n: wait_bytes(project_sum.at[pl.ds(0, 16 * n), :], recv_sem.at[17]), PIECES // 2
-    )
+    send_expand(1)
+    pieces_pending(expand_in, 16)
+
     settle((12, "here"))
 
     @pl.when(is_keeper)
@@ -910,15 +953,23 @@
             above = cots[pl.ds(at(r, k), ROWS), 0:LANES].astype(F32)
             input_out[pl.ds(at(r, k, HALO), ROWS), :] = above + part(product, k, ROWS, 0)
 
-    last_part[...] = jnp.zeros_like(last_part)
+    extra[...] = jnp.zeros_like(extra)
+
+    def put_extra(k, v):
+        high = rounded(v)
+        middle = rounded(v - high)
+        for j, p in enumerate((high, middle, v - high - middle)):
+            extra[3 * k + j : 3 * k + j + 1, :] = p
+
     settle((14, "here"))
 
     @pl.when(is_keeper)
     def _():
         late_in[me] = late_part[chan]
         total = total_of(late_in, devices, 2, half)
-        last_part[17:19, :] = total[:, 0:LANES]
-        last_part[19:21, :] = total[:, LANES:half]
+        for k in range(2):
+            for j in range(2):
+                put_extra(1 + 2 * k + j, total[j : j + 1, k * LANES : (k + 1) * LANES])
         squares = (total * total)[0:1]
         square_part[...] += fold_lanes(squares)
 
@@ -930,54 +981,66 @@
         total = total_of(expand_in, mates, 16, LANES)
         squares = square_part[...] + jnp.sum(total * total, axis=0, keepdims=True)
         square_part[...] = squares
-        last_part[0:16, :] = total
-        last_part[16:17, :] = squares
-        last_in[core, spot] = last_part[...]
+        put_extra(0, squares)
+        last_part[0:16, :] = total.astype(BF16)
+        last_part[16:32, :] = extra[...].astype(BF16)
+        slot = core * spots_here + spot
+        last_in[slot] = last_part[...]
+        to_group(last_part, last_in.at[slot], 19, tm_size)
 
         def send_tail(k, carry):
-            target = {"chan": other, "tm": lax.rem(chip + k, chips) * 2 + core}
-            remote(square_part, tail_in.at[core, spot], 20, target).start()
+            target = {"chan": other, "tm": wrapped(tm + k, tm_size)}
+            remote(square_part, tail_in.at[slot], 20, target).start()
             return carry
 
-        to_group(last_part, last_in.at[core, spot], 19, chips)
-        lax.fori_loop(0, chips, send_tail, 0)
+        if tm_size <= 16:
+            for k in range(tm_size):
+                send_tail(k, 0)
+        else:
+            lax.fori_loop(0, tm_size, send_tail, 0)
 
     def tails_sent():
         for _ in range(stride):
-            wait_bytes(tail_in.at[0], send_sem.at[20])
-
-    pending[19, "sent"] = lambda: when_reducer(lambda: group_sent(last_part, 19, chips))
-    pending[19, "here"] = lambda: by_role(
-        lambda n: wait_bytes(last_in.at[0, pl.ds(0, n)], recv_sem.at[19]), PIECES // 2
-    )
+            wait_bytes(tail_in, send_sem.at[20])
+
+    def from_reducers(n):
+        wait_bytes(last_in.at[pl.ds(0, n)], recv_sem.at[19])
+
+    pending[19, "sent"] = lambda: when_reducer(lambda: group_sent(last_part, 19, tm_size))
+    pending[19, "here"] = lambda: by_role(from_reducers, PIECES)
     pending[20, "sent"] = lambda: when_reducer(tails_sent)
-    pending[20, "here"] = lambda: wait_bytes(tail_in.at[0], recv_sem.at[20])
+    pending[20, "here"] = lambda: wait_bytes(tail_in, recv_sem.at[20])
 
     settle((17, "here"))
     started(remote(project_sum.at[mine, :], project_sum.at[mine, :], 21, sibling), 21)
-    settle((19, "here"))
-    started(remote(last_in.at[core], last_in.at[core], 22, sibling), 22)
-    settle((20, "here"))
-    started(remote(tail_in.at[core], tail_in.at[core], 23, sibling), 23)
     settle((18, "here"), (21, "here"))
     for k in range(2):
         project_grad_ref[k] = project_sum[k * LANES : (k + 1) * LANES, :].T
     small_grad_ref[...] = small_sum[...]
-    settle((22, "here"), (23, "here"))
+    settle((19, "here"), (20, "here"))
     for c in range(2):
-        for j in range(PIECES // 2):
-            expand_grad_ref[j * 16 : j * 16 + 16, c * LANES : (c + 1) * LANES] = last_in[c, j, 0:16]
+        for j in range(spots_here):
+            where = slice(c * LANES, (c + 1) * LANES)
+            expand_grad_ref[j * 16 : j * 16 + 16, where] = last_in[c * spots_here + j, 0:16, :].astype(F32)
     keeper_spot = keeper // 2 // stride
+
+    def extras(c, j):
+        return last_in[c * spots_here + j, 16:32, :].astype(F32)
+
+    def get_extra(rows, k):
+        return rows[3 * k : 3 * k + 1] + rows[3 * k + 1 : 3 * k + 2] + rows[3 * k + 2 : 3 * k + 3]
+
+    late = extras(0, keeper_spot)
     for k in range(2):
         where = slice(k * LANES, (k + 1) * LANES)
-        late = last_in[0, keeper_spot, 17 + 2 * k : 19 + 2 * k, :]
-        small_grad_ref[0:1, where] = late[0:1]
-        small_grad_ref[SLOPE_ONE_ROW : SLOPE_ONE_ROW + 1, where] = late[1:2]
-    own_total, other_total = last_in[0, 0, 16:17, :], tail_in[0, 0]
-    for q in range(1, PIECES):
-        c, j = q // (PIECES // 2), q % (PIECES // 2)
-        own_total = own_total + last_in[c, j, 16:17, :]
-        other_total = other_total + tail_in[c, j]
+        small_grad_ref[0:1, where] = get_extra(late, 1 + 2 * k)
+        small_grad_ref[SLOPE_ONE_ROW : SLOPE_ONE_ROW + 1, where] = get_extra(late, 2 + 2 * k)
+    own_total, other_total = None, None
+    for q in range(PIECES):
+        c, j = q // spots_here, q % spots_here
+        mine_here, theirs = get_extra(extras(c, j), 0), tail_in[q]
+        own_total = mine_here if own_total is None else own_total + mine_here
+        other_total = theirs if other_total is None else other_total + theirs
     small_grad_ref[SQUARES_ROW : SQUARES_ROW + 1, 0:LANES] = own_total + other_total
     small_grad_ref[SQUARES_ROW : SQUARES_ROW + 1, LANES:half] = jnp.zeros((1, half - LANES), F32)
 
@@ -1140,9 +1203,10 @@
         ((2 * inputs, half), F32),
         ((16, half), F32),
         ((1, LANES), F32),
-        ((24, LANES), F32),
-        ((2, PIECES // 2, 24, LANES), F32),
-        ((2, PIECES // 2, 1, LANES), F32),
+        ((16, LANES), F32),
+        ((32, LANES), BF16),
+        ((PIECES, 32, LANES), BF16),
+        ((PIECES, 1, LANES), F32),
     ]
     state = [
         expand,

time: 62.9 us -> 61.1 us (0.971)
  Pallas kernels: 61.9 us -> 60.2 us
    pallas_call x1, Pallas kernels: 59.4 us -> 57.7 us  [per_device(): pl.pallas_call(functools.partial(block_kernel, tm_size, items, item_pad),...]
where the time goes in v4:
time: 61.1 us; the launch traced here: 60.9 us
  Pallas kernels  60.2 us (99%)
  between operations  0.67 us (1%)
    pallas_call x1, Pallas kernels, per_device(): pl.pallas_call(functools.partial(block_kernel, tm_size, items, item_pad),...  57.7 us
    pallas_call x1, Pallas kernels, per_device(): pl.pallas_call(adam_kernel, out_shape=[shape((frames, inputs), BF16), sha...  2.5 us

profile of v4, /device:TPU:0, one launch (start us, length us, event | category | flops | bytes accessed | tf_op | source)
XLA Modules:
  0.0 60.9 jit_solution(14702649073037735777)
XLA Ops:
  0.7 57.7 %temporal_block.1 = (bf16[2048,128]{1,0:T(8,128)(2,1)S(1)}, bf16[2048,128]{1,0:T(8,128)(2,1)S(1)}, f32[2048,128]{1,0:T(8,128)S(1)}, f32[128,256]{1,0:T(8,128)S(1...) custom-call(s32[16]{0:T(128)} %len_hbm.1, ...), custom_call_target="tpu_custom_call" | custom-call | tf_op jit(solution)/shard_map/temporal_block/pallas_call | solution.py:1231
  58.4 2.5 %adam_step.1 = (bf16[2048,128]{1,0:T(8,128)(2,1)}, bf16[2048,128]{1,0:T(8,128)(2,1)}, f32[2048,128]{1,0:T(8,128)}, f32[1,1]{1,0:T(1,128)}, f32[128,256]{1,0:T(8,...) custom-call(bf16[2048,128]{1,0:T(8,128)(2,1)S(1)} %get-tuple-element, ...), custom_call_target="tpu_custom_call" | custom-call | tf_op jit(solution)/shard_map/adam_step/pallas_call | solution.py:1258

commit v5 on v4

--- a/solution.py
+++ b/solution.py
@@ -15,8 +15,8 @@
 HALO = 2 * DILATION
 LONGEST_ITEM = 8192
 LANES = 128
-ROWS = 64
-BLOCK = 512
+ROWS = 32
+BLOCK = 2048
 PIECES = 16
 
 norm_eps = 1e-06

time: 61.1 us -> 57 us (0.933)
  Pallas kernels: 60.2 us -> 56 us
    pallas_call x1, Pallas kernels: 57.7 us -> 53.5 us  [per_device(): pl.pallas_call(functools.partial(block_kernel, tm_size, items, item_pad),...]
where the time goes in v5:
time: 57 us; the launch traced here: 56.9 us
  Pallas kernels  56 us (98%)
  between operations  0.83 us (1%)
    pallas_call x1, Pallas kernels, per_device(): pl.pallas_call(functools.partial(block_kernel, tm_size, items, item_pad),...  53.5 us
    pallas_call x1, Pallas kernels, per_device(): pl.pallas_call(adam_kernel, out_shape=[shape((frames, inputs), BF16), sha...  2.5 us

profile of v5, /device:TPU:0, one launch (start us, length us, event | category | flops | bytes accessed | tf_op | source)
XLA Modules:
  0.0 56.9 jit_solution(13619657524540102038)
XLA Ops:
  0.7 53.5 %temporal_block.1 = (bf16[2048,128]{1,0:T(8,128)(2,1)S(1)}, bf16[2048,128]{1,0:T(8,128)(2,1)S(1)}, f32[2048,128]{1,0:T(8,128)S(1)}, f32[128,256]{1,0:T(8,128)S(1...) custom-call(s32[16]{0:T(128)} %len_hbm.1, ...), custom_call_target="tpu_custom_call" | custom-call | tf_op jit(solution)/shard_map/temporal_block/pallas_call | solution.py:1231
  54.2 2.5 %adam_step.1 = (bf16[2048,128]{1,0:T(8,128)(2,1)}, bf16[2048,128]{1,0:T(8,128)(2,1)}, f32[2048,128]{1,0:T(8,128)}, f32[1,1]{1,0:T(1,128)}, f32[128,256]{1,0:T(8,...) custom-call(bf16[2048,128]{1,0:T(8,128)(2,1)S(1)} %get-tuple-element, ...), custom_call_target="tpu_custom_call" | custom-call | tf_op jit(solution)/shard_map/adam_step/pallas_call | solution.py:1258

commit v6 on v5

--- a/solution.py
+++ b/solution.py
@@ -384,10 +384,10 @@
     put_table(0, row_start.astype(F32))
     put_table(1, row_end.astype(F32))
 
-    wide_block = wide // 4
-    wide_rows = wide_block // 11
-
-    @functools.partial(loop, 0, wide_block, 4)
+    wide_block = wide
+    wide_rows = wide_block // 44
+
+    @functools.partial(loop, 0, wide_block, 1)
     def _(r):
         for k in range(0, wide_block, wide_rows):
             position = first - HALO + r + k + lax.broadcasted_iota(jnp.int32, (wide_rows, width), 0)
@@ -553,7 +553,7 @@
     put_table(0, mean_one)
     put_table(1, scale_one)
 
-    @functools.partial(loop, 0, wide_block, 4)
+    @functools.partial(loop, 0, wide_block, 1)
     def _(r):
         values = rows_of(r, wide_block, 2)
         for k in range(0, wide_block, wide_rows):
@@ -761,9 +761,9 @@
         send_pieces(project_piece, project_in, 11, c)
     pieces_pending(project_in, 11)
 
-    @functools.partial(loop, HALO, 2 * ROWS, frames // (2 * ROWS))
+    @functools.partial(loop, HALO, 512, frames // 512)
     def _(r):
-        for k in range(0, 2 * ROWS, ROWS):
+        for k in range(0, 512, ROWS):
             rows = pl.ds(at(r, k), ROWS)
             low, high = mask_low[rows, :], mask_high[rows, :]
             total = jnp.zeros((ROWS, LANES), F32)

time: 57 us -> 56.5 us (level)
  no operation moved by 1% of the time
where the time goes in v6:
time: 56.5 us; the launch traced here: 56.3 us
  Pallas kernels  55.5 us (98%)
  between operations  0.83 us (1%)
    pallas_call x1, Pallas kernels, per_device(): pl.pallas_call(functools.partial(block_kernel, tm_size, items, item_pad),...  53 us
    pallas_call x1, Pallas kernels, per_device(): pl.pallas_call(adam_kernel, out_shape=[shape((frames, inputs), BF16), sha...  2.5 us

profile of v6, /device:TPU:0, one launch (start us, length us, event | category | flops | bytes accessed | tf_op | source)
XLA Modules:
  0.0 56.3 jit_solution(15641924052115965627)
XLA Ops:
  0.7 53.0 %temporal_block.1 = (bf16[2048,128]{1,0:T(8,128)(2,1)S(1)}, bf16[2048,128]{1,0:T(8,128)(2,1)S(1)}, f32[2048,128]{1,0:T(8,128)S(1)}, f32[128,256]{1,0:T(8,128)S(1...) custom-call(s32[16]{0:T(128)} %len_hbm.1, ...), custom_call_target="tpu_custom_call" | custom-call | tf_op jit(solution)/shard_map/temporal_block/pallas_call | solution.py:1231
  53.7 2.5 %adam_step.1 = (bf16[2048,128]{1,0:T(8,128)(2,1)}, bf16[2048,128]{1,0:T(8,128)(2,1)}, f32[2048,128]{1,0:T(8,128)}, f32[1,1]{1,0:T(1,128)}, f32[128,256]{1,0:T(8,...) custom-call(bf16[2048,128]{1,0:T(8,128)(2,1)S(1)} %get-tuple-element, ...), custom_call_target="tpu_custom_call" | custom-call | tf_op jit(solution)/shard_map/adam_step/pallas_call | solution.py:1258
